TPU v7x, 32 devices: a whole 2x2x4 slice. The times are simulated.
32 devices in a mesh: wide: 8 (over y, x, core), narrow: 4 (over z).
Axes of the slice: x: 2, y: 2, z: 4, core: 2. Of those that a mesh axis runs over, the one named last changes fastest.
Arguments:
- layer_input: bfloat16 [16384, 1024], P(('wide', 'narrow')), may hold values from -6 to 6
- out_grad: bfloat16 [16384, 1024], P(('wide', 'narrow')), may hold values from -6 to 6
- norm_attn_gain: bfloat16 [1024], replicated, may hold values from 0.5 to 1.5
- w_query: bfloat16 [1024, 1024], P(None, 'narrow'), may hold values from -0.0234375 to 0.0234375
- w_key: bfloat16 [1024, 1024], P(None, 'narrow'), may hold values from -0.1875 to 0.1875
- w_value: bfloat16 [1024, 1024], P(None, 'narrow'), may hold values from -0.1875 to 0.1875
- w_out: bfloat16 [1024, 1024], P('narrow'), may hold values from -1 to 1
- rel_table: bfloat16 [32, 16], P(None, 'narrow'), may hold values from -4 to 4
- layout_table: bfloat16 [64, 16], P(None, 'narrow'), may hold values from -4 to 4
- norm_ffn_gain: bfloat16 [1024], replicated, may hold values from 0.5 to 1.5
- w_gate: bfloat16 [1024, 2816], P(None, 'narrow'), may hold values from -0.1875 to 0.1875
- w_up: bfloat16 [1024, 2816], P(None, 'narrow'), may hold values from -0.1875 to 0.1875
- down_projection_weight: bfloat16 [2816, 1024], P('narrow'), may hold values from -0.109375 to 0.109375
- page_lengths: int32 [8, 4], P('wide'), may hold values from 1 to 1024, 2048 in all within a row
- key_mask: int32 [16384], P('wide'), may hold values 0 or 1
- rel_bucket: int32 [16384, 2048], P('wide'), may hold values from 0 to 31
- layout_bucket: int32 [16384, 2048], P('wide'), may hold values from 0 to 63
Outputs:
- layer_out: bfloat16 [16384, 1024], P(('wide', 'narrow'))
- in_grad: float32 [16384, 1024], P(('wide', 'narrow'))
- grad_norm_attn: float32 [1024], P(('wide', 'narrow'))
- grad_query: float32 [1024, 1024], P('wide', 'narrow')
- grad_key: float32 [1024, 1024], P('wide', 'narrow')
- grad_value: float32 [1024, 1024], P('wide', 'narrow')
- grad_out_proj: float32 [1024, 1024], P('narrow', 'wide')
- grad_rel_table: float32 [32, 16], P('wide', 'narrow')
- grad_layout_table: float32 [64, 16], P('wide', 'narrow')
- grad_norm_ffn: float32 [1024], P(('wide', 'narrow'))
- grad_gate: float32 [1024, 2816], P('wide', 'narrow')
- grad_up: float32 [1024, 2816], P('wide', 'narrow')
- grad_down: float32 [2816, 1024], P('narrow', 'wide')
Inputs may be any that keep to these rules, and one draw needn't show every extreme that they name: `page_lengths`: each row sums to 2048; the pages fill the block of tokens of that index of wide in order, and one of them has exactly 1024 tokens.
All inputs are finite; a program needn't handle non-finite values. No bound on the sum of `key_mask` on one device may be relied on, other than what follows from the above.
Results may differ from a plain program's by a relative error of at most 0.015.
Values may be sent and summed in bfloat16 or wider, within the bound.
No kernel may reach another device: no remote copies, remote signals or barrier semaphores. Data moves between devices by JAX's collectives and lax.ppermute only.
A program may use at most 320 MiB of HBM per device.

v0:
```python
import jax
import jax.numpy as jnp
from jax import lax
from jax.sharding import PartitionSpec as P

DH = 64


epsilon = 1e-06
masked_score = -1e30
highest = lax.Precision.HIGHEST


def contract_rows(left, right):
    return lax.dot_general(
        left, right, (((0,), (0,)), ((), ())), preferred_element_type=jnp.float32
    )


def contract_cols(left, right):
    return lax.dot_general(
        left, right, (((1,), (1,)), ((), ())), preferred_element_type=jnp.float32
    )


def row_blocks(array, block):
    return array.reshape((array.shape[0] // block, block) + array.shape[1:])


def gated(gate, upward):
    return jax.nn.gelu(gate, approximate=True) * upward


def norm_rows(rows, gain):
    scale = lax.rsqrt(jnp.mean(rows * rows, axis=-1, keepdims=True) + epsilon)
    return (scale, (rows * scale * gain).astype(jnp.bfloat16))


def norm_back(d_normed, rows, scale, gain):
    shaped = d_normed * gain
    gain_term = jnp.sum(d_normed * rows * scale, axis=0)
    cubed = scale * scale * scale
    d_rows = scale * shaped - rows * cubed * jnp.mean(shaped * rows, axis=-1, keepdims=True)
    return (d_rows, gain_term)


def bucket_bias(bucket_rows, table):
    piece_rows = min(128, bucket_rows.shape[0])
    labels = lax.iota(jnp.int32, table.shape[0])
    table_reduced = table.astype(jnp.bfloat16)

    def one_piece(bucket_ids):
        indicator_matrix = (bucket_ids[None] == labels[:, None, None]).astype(jnp.bfloat16)
        return jnp.einsum(
            "car,cg->gar", indicator_matrix, table_reduced, preferred_element_type=jnp.float32
        )

    pieces = lax.map(one_piece, row_blocks(bucket_rows, piece_rows))
    return jnp.transpose(pieces, (1, 0, 2, 3)).reshape(
        table.shape[1], bucket_rows.shape[0], bucket_rows.shape[1]
    )


def bucket_grad(bucket_rows, d_scores, buckets):
    piece_rows = min(128, bucket_rows.shape[0])
    labels = lax.iota(jnp.int32, buckets)

    def one_piece(summed, step_index):
        first_row = step_index * piece_rows
        bucket_ids = lax.dynamic_slice_in_dim(bucket_rows, first_row, piece_rows, 0)
        score_piece = lax.dynamic_slice_in_dim(d_scores, first_row, piece_rows, 1)
        indicator_matrix = (bucket_ids[None] == labels[:, None, None]).astype(jnp.float32)
        return (
            summed
            + jnp.einsum(
                "nas,las->nl",
                indicator_matrix,
                score_piece,
                precision=highest,
                preferred_element_type=jnp.float32,
            ),
            None,
        )

    initial = jnp.zeros((buckets, d_scores.shape[0]), jnp.float32)
    steps_count = bucket_rows.shape[0] // piece_rows
    summed, unused_out = lax.scan(one_piece, initial, lax.iota(jnp.int32, steps_count))
    return summed


def block_scores(query_rows, keys, relative_rows, layout_rows, page_rows, place_rows, context):
    page_of, position, key_mask, relative_float, layout_float = context
    raw = jnp.einsum("qhd,khd->hqk", query_rows, keys, preferred_element_type=jnp.float32)
    biased = (
        raw + bucket_bias(relative_rows, relative_float) + bucket_bias(layout_rows, layout_float)
    )
    same_page = page_rows[:, None] == page_of[None, :]
    visible = (key_mask[None, :] == 1) | (place_rows[:, None] == position[None, :])
    return jnp.where((same_page & visible)[None], biased, masked_score)


def split_heads(projected, head_cols):
    count = projected.shape[0]
    shape = (count, head_cols // DH, DH)
    return (
        projected[:, :head_cols].reshape(shape),
        projected[:, head_cols : 2 * head_cols].reshape(shape),
        projected[:, 2 * head_cols :].reshape(shape),
    )


def attention_forward(query, keys, values, inputs, context, block):

    def one_block(pieces):
        query_rows, relative_rows, layout_rows, page_rows, place_rows = pieces
        scores = block_scores(
            query_rows, keys, relative_rows, layout_rows, page_rows, place_rows, context
        )
        top = jnp.max(scores, axis=-1, keepdims=True)
        exponent = jnp.exp(scores - top)
        total = jnp.sum(exponent, axis=-1, keepdims=True)
        probs_low = (exponent / total).astype(jnp.bfloat16)
        mixed = jnp.einsum("hqk,khd->qhd", probs_low, values, preferred_element_type=jnp.float32)
        return (mixed.astype(jnp.bfloat16), (top + jnp.log(total))[:, :, 0])

    mixed, log_total = lax.map(one_block, (row_blocks(query, block),) + inputs)
    return (mixed.reshape(query.shape[0], -1), log_total)


def attention_backward(query, keys, values, d_attended, log_total, inputs, context, block):
    relative_float = context[3]
    layout_float = context[4]

    def one_block(carry, pieces):
        d_keys, d_values, grad_relative, grad_layout = carry
        query_rows, grad_rows, total_rows, relative_rows, layout_rows, page_rows, place_rows = (
            pieces
        )
        scores = block_scores(
            query_rows, keys, relative_rows, layout_rows, page_rows, place_rows, context
        )
        probs = jnp.exp(scores - total_rows[:, :, None])
        d_probs = jnp.einsum("qhd,khd->hqk", grad_rows, values, preferred_element_type=jnp.float32)
        d_scores = probs * (d_probs - jnp.sum(probs * d_probs, axis=-1, keepdims=True))
        grad_relative = grad_relative + bucket_grad(
            relative_rows, d_scores, relative_float.shape[0]
        )
        grad_layout = grad_layout + bucket_grad(layout_rows, d_scores, layout_float.shape[0])
        scores_low = d_scores.astype(jnp.bfloat16)
        d_query = jnp.einsum("hqk,khd->qhd", scores_low, keys, preferred_element_type=jnp.float32)
        d_keys = d_keys + jnp.einsum(
            "hqk,qhd->khd", scores_low, query_rows, preferred_element_type=jnp.float32
        )
        d_values = d_values + jnp.einsum(
            "hqk,qhd->khd",
            probs.astype(jnp.bfloat16),
            grad_rows,
            preferred_element_type=jnp.float32,
        )
        return ((d_keys, d_values, grad_relative, grad_layout), d_query.astype(jnp.bfloat16))

    count = query.shape[0]
    initial = (
        jnp.zeros(keys.shape, jnp.float32),
        jnp.zeros(keys.shape, jnp.float32),
        jnp.zeros(relative_float.shape, jnp.float32),
        jnp.zeros(layout_float.shape, jnp.float32),
    )
    pieces = (
        row_blocks(query, block),
        row_blocks(d_attended.reshape(keys.shape), block),
        log_total,
    ) + inputs
    carry, d_query = lax.scan(one_block, initial, pieces)
    d_keys, d_values, grad_relative, grad_layout = carry
    d_project = jnp.concatenate(
        [
            d_query.reshape(count, -1),
            d_keys.reshape(count, -1).astype(jnp.bfloat16),
            d_values.reshape(count, -1).astype(jnp.bfloat16),
        ],
        axis=1,
    )
    return (d_project, grad_relative, grad_layout)


def run_forward(resid, weights, context, inputs, block):
    gain_attn, w_project, w_out_used, gain_ffn, w_gate_up, down_projection_weight = weights
    head_cols = w_project.shape[1] // 3
    hidden_cols = down_projection_weight.shape[0]
    scale_attn, normed_attn = norm_rows(resid, gain_attn)
    normed_attn_all = lax.all_gather(normed_attn, "narrow", axis=0, tiled=True)
    projected = jnp.dot(normed_attn_all, w_project, preferred_element_type=jnp.float32).astype(
        jnp.bfloat16
    )
    query, keys, values = split_heads(projected, head_cols)
    attended, log_total = attention_forward(query, keys, values, inputs, context, block)
    middle = resid + lax.psum_scatter(
        jnp.dot(attended, w_out_used, preferred_element_type=jnp.float32),
        "narrow",
        scatter_dimension=0,
        tiled=True,
    )
    scale_ffn, normed_ffn = norm_rows(middle, gain_ffn)
    normed_ffn_all = lax.all_gather(normed_ffn, "narrow", axis=0, tiled=True)
    gate_up = jnp.dot(normed_ffn_all, w_gate_up, preferred_element_type=jnp.float32)
    hidden = gated(gate_up[:, :hidden_cols], gate_up[:, hidden_cols:]).astype(jnp.bfloat16)
    block_out = middle + lax.psum_scatter(
        jnp.dot(hidden, down_projection_weight, preferred_element_type=jnp.float32).astype(
            jnp.bfloat16
        ),
        "narrow",
        scatter_dimension=0,
        tiled=True,
    ).astype(jnp.float32)
    return (
        scale_attn,
        normed_attn_all,
        projected,
        attended,
        log_total,
        middle,
        scale_ffn,
        normed_ffn_all,
        gate_up,
        hidden,
        block_out,
    )


def on_device(
    layer_input,
    out_grad,
    norm_attn_gain,
    w_query,
    w_key,
    w_value,
    w_out,
    rel_table,
    layout_table,
    norm_ffn_gain,
    w_gate,
    w_up,
    down_projection_weight,
    page_lengths,
    key_mask,
    rel_bucket,
    layout_bucket,
):
    count = key_mask.shape[0]
    block = min(512, count)
    head_cols = w_query.shape[1]
    hidden_cols = w_gate.shape[1]
    ends = jnp.cumsum(page_lengths[0], dtype=jnp.int32)
    position = lax.iota(jnp.int32, count)
    page_of = jnp.sum(
        (position[:, None] >= ends[None, :]).astype(jnp.int32), axis=1, dtype=jnp.int32
    )
    context = (
        page_of,
        position,
        key_mask,
        rel_table.astype(jnp.float32),
        layout_table.astype(jnp.float32),
    )
    inputs = (
        row_blocks(rel_bucket, block),
        row_blocks(layout_bucket, block),
        row_blocks(page_of, block),
        row_blocks(position, block),
    )
    gain_attn = norm_attn_gain.astype(jnp.float32)
    gain_ffn = norm_ffn_gain.astype(jnp.float32)
    w_project = jnp.concatenate([w_query, w_key, w_value], axis=1)
    w_gate_up = jnp.concatenate([w_gate, w_up], axis=1)
    weights = (gain_attn, w_project, w_out, gain_ffn, w_gate_up, down_projection_weight)
    resid = layer_input.astype(jnp.float32)
    state = run_forward(resid, weights, context, inputs, block)
    layer_out = state[10].astype(jnp.bfloat16)
    (
        scale_attn,
        normed_attn_all,
        projected,
        attended,
        log_total,
        middle,
        scale_ffn,
        normed_ffn_all,
        gate_up,
        hidden,
        unused_out,
    ) = state
    piece = lax.all_gather(out_grad, "narrow", axis=0, tiled=True)
    grad_down = contract_rows(hidden, piece)
    d_hidden = contract_cols(piece, down_projection_weight)
    grad_down, d_hidden = (grad_down, d_hidden)
    unused_value, pullback = jax.vjp(gated, gate_up[:, :hidden_cols], gate_up[:, hidden_cols:])
    d_gate, d_up = pullback(d_hidden)
    d_gate_up = jnp.concatenate([d_gate, d_up], axis=1).astype(jnp.bfloat16)
    grad_gate_up = contract_rows(normed_ffn_all, d_gate_up)
    d_normed_ffn = lax.psum_scatter(
        contract_cols(d_gate_up, w_gate_up), "narrow", scatter_dimension=0, tiled=True
    )
    d_middle_norm, gain_ffn_term = norm_back(d_normed_ffn, middle, scale_ffn, gain_ffn)
    d_middle = out_grad.astype(jnp.float32) + d_middle_norm
    piece = lax.all_gather(d_middle.astype(jnp.bfloat16), "narrow", axis=0, tiled=True)
    grad_wout = contract_rows(attended, piece)
    d_attended = contract_cols(piece, w_out)
    grad_wout, d_attended = (grad_wout, d_attended)
    query, keys, values = split_heads(projected, head_cols)
    d_project, grad_relative, grad_layout = attention_backward(
        query, keys, values, d_attended.astype(jnp.bfloat16), log_total, inputs, context, block
    )
    grad_project = contract_rows(normed_attn_all, d_project)
    d_normed_attn = lax.psum_scatter(
        contract_cols(d_project, w_project), "narrow", scatter_dimension=0, tiled=True
    )
    d_resid, gain_attn_term = norm_back(d_normed_attn, resid, scale_attn, gain_attn)
    in_grad = d_middle + d_resid
    sum_project, sum_wout, sum_gate_up, sum_down, sum_relative, sum_layout = (
        lax.psum_scatter(grad_project, "wide", scatter_dimension=0, tiled=True),
        lax.psum_scatter(grad_wout, "wide", scatter_dimension=1, tiled=True),
        lax.psum_scatter(grad_gate_up, "wide", scatter_dimension=0, tiled=True),
        lax.psum_scatter(grad_down, "wide", scatter_dimension=1, tiled=True),
        lax.psum_scatter(grad_relative, "wide", scatter_dimension=0, tiled=True),
        lax.psum_scatter(grad_layout, "wide", scatter_dimension=0, tiled=True),
    )
    sum_gain_attn, sum_gain_ffn = (
        lax.psum_scatter(gain_attn_term, ("wide", "narrow"), scatter_dimension=0, tiled=True),
        lax.psum_scatter(gain_ffn_term, ("wide", "narrow"), scatter_dimension=0, tiled=True),
    )
    return (
        layer_out,
        in_grad,
        sum_gain_attn,
        sum_project[:, :head_cols],
        sum_project[:, head_cols : 2 * head_cols],
        sum_project[:, 2 * head_cols :],
        sum_wout,
        sum_relative,
        sum_layout,
        sum_gain_ffn,
        sum_gate_up[:, :hidden_cols],
        sum_gate_up[:, hidden_cols:],
        sum_down,
    )


def solution(mesh):
    placed = (
        P(("wide", "narrow"), None),
        P(("wide", "narrow"), None),
        P(),
        P(None, "narrow"),
        P(None, "narrow"),
        P(None, "narrow"),
        P("narrow", None),
        P(None, "narrow"),
        P(None, "narrow"),
        P(),
        P(None, "narrow"),
        P(None, "narrow"),
        P("narrow", None),
        P("wide", None),
        P("wide"),
        P("wide", None),
        P("wide", None),
    )
    return jax.shard_map(
        on_device,
        mesh=mesh,
        in_specs=placed,
        out_specs=(
            P(("wide", "narrow"), None),
            P(("wide", "narrow"), None),
            P(("wide", "narrow")),
            P("wide", "narrow"),
            P("wide", "narrow"),
            P("wide", "narrow"),
            P("narrow", "wide"),
            P("wide", "narrow"),
            P("wide", "narrow"),
            P(("wide", "narrow")),
            P("wide", "narrow"),
            P("wide", "narrow"),
            P("narrow", "wide"),
        ),
        check_vma=False,
    )
```

profile of v0, /device:TPU:0, one launch (start us, length us, event | category | flops | bytes accessed | tf_op | source)
XLA Modules:
  0.0 3646.5 jit_solution(6577897113658551657)
XLA Ops:
  17.5 79.4 %all-gather.5.cloned.1.call-done = bf16[2048,1024]{1,0:T(8,128)(2,1)} async-done(((bf16[512,1024]{1,0:T(8,128)(2,1)}), bf16[2048,1024]{1,0:T(8,128)(2,1)}) %all-gather.5.cloned.1.call-update) | async-done | bytes 4194320 | tf_op jit(solution)/shard_map/all_gather | solution.py:192
  108.9 726.0 %while.146 = (s32[]{:T(128)}, bf16[4,512,4,64]{1,3,2,0:T(8,128)(2,1)}, f32[4,4,512]{2,1,0:T(4,128)}, s32[4,512]{1,0:T(4,128)}, s32[2048]{0:T(1024)S(1)}, /*index...) while((s32[]{:T(128)}, ...), condition=%wide.region_10.11_spmd.clone, body=%wide.region_3.10_spmd.clone.sunk | while | flops 1342308352 | bytes 220827888 | solution.py:126
  142.1 50.7 %while.152 = (s32[]{:T(128)}, f32[4,4,128,2048]{3,1,2,0:T(4,128)}, s32[4,128,2048]{2,1,0:T(8,128)}, bf16[64,4]{0,1:T(4,128)(2,1)S(1)}, s32[]{:T(128)}) while((s32[]{:T(128)}, f32[4,4,128,2048]{3,1,2,0:T(4,128)}, s32[4,128,2048]{2,1,0:T(8,128)}, bf16[64,4]{0,1:T(4,128)(2,1)S(1)}, s32[]{:T(128)}) %tuple.309), condition=%wide.region_7.7_spmd.clone, body=%wide.region_6.6_spmd.clone.sunk | while | flops 150994944 | bytes 7340621 | solution.py:58
  319.5 50.7 %while.152 = (s32[]{:T(128)}, f32[4,4,128,2048]{3,1,2,0:T(4,128)}, s32[4,128,2048]{2,1,0:T(8,128)}, bf16[64,4]{0,1:T(4,128)(2,1)S(1)}, s32[]{:T(128)}) while((s32[]{:T(128)}, f32[4,4,128,2048]{3,1,2,0:T(4,128)}, s32[4,128,2048]{2,1,0:T(8,128)}, bf16[64,4]{0,1:T(4,128)(2,1)S(1)}, s32[]{:T(128)}) %tuple.309), condition=%wide.region_7.7_spmd.clone, body=%wide.region_6.6_spmd.clone.sunk | while | flops 150994944 | bytes 7340621 | solution.py:58
  496.9 50.7 %while.152 = (s32[]{:T(128)}, f32[4,4,128,2048]{3,1,2,0:T(4,128)}, s32[4,128,2048]{2,1,0:T(8,128)}, bf16[64,4]{0,1:T(4,128)(2,1)S(1)}, s32[]{:T(128)}) while((s32[]{:T(128)}, f32[4,4,128,2048]{3,1,2,0:T(4,128)}, s32[4,128,2048]{2,1,0:T(8,128)}, bf16[64,4]{0,1:T(4,128)(2,1)S(1)}, s32[]{:T(128)}) %tuple.309), condition=%wide.region_7.7_spmd.clone, body=%wide.region_6.6_spmd.clone.sunk | while | flops 150994944 | bytes 7340621 | solution.py:58
  674.4 50.7 %while.152 = (s32[]{:T(128)}, f32[4,4,128,2048]{3,1,2,0:T(4,128)}, s32[4,128,2048]{2,1,0:T(8,128)}, bf16[64,4]{0,1:T(4,128)(2,1)S(1)}, s32[]{:T(128)}) while((s32[]{:T(128)}, f32[4,4,128,2048]{3,1,2,0:T(4,128)}, s32[4,128,2048]{2,1,0:T(8,128)}, bf16[64,4]{0,1:T(4,128)(2,1)S(1)}, s32[]{:T(128)}) %tuple.309), condition=%wide.region_7.7_spmd.clone, body=%wide.region_6.6_spmd.clone.sunk | while | flops 150994944 | bytes 7340621 | solution.py:58
  843.5 142.5 %reduce-scatter.10.cloned.1.call-done = f32[512,1024]{1,0:T(8,128)} async-done(((f32[2048,1024]{1,0:T(8,128)}), f32[512,1024]{1,0:T(8,128)}) %reduce-scatter.10.cloned.1.call-update) | async-done | bytes 2097168 | tf_op jit(solution)/shard_map/reduce_scatter | solution.py:198
  996.3 75.8 %all-gather.7.cloned.1.call-done = bf16[2048,1024]{1,0:T(8,128)(2,1)} async-done(((bf16[512,1024]{1,0:T(8,128)(2,1)}), bf16[2048,1024]{1,0:T(8,128)(2,1)}) %all-gather.7.cloned.1.call-update) | async-done | bytes 4194320 | tf_op jit(solution)/shard_map/all_gather | solution.py:205
  1083.8 69.1 %all-gather.9.cloned.1.call-done = bf16[2048,1024]{1,0:T(8,128)(2,1)} async-done(((bf16[512,1024]{1,0:T(8,128)(2,1)}), bf16[2048,1024]{1,0:T(8,128)(2,1)}) %all-gather.9.cloned.1.call-update) | async-done | bytes 4194320 | tf_op jit(solution)/shard_map/all_gather | solution.py:293
  1185.6 135.9 %reduce-scatter.14.cloned.1.call-done = f32[512,1024]{1,0:T(8,128)} async-done(((f32[2048,1024]{1,0:T(8,128)}), f32[512,1024]{1,0:T(8,128)}) %reduce-scatter.14.cloned.1.call-update) | async-done | bytes 2097168 | tf_op jit(solution)/shard_map/reduce_scatter | solution.py:301
  1324.9 76.3 %reduce-scatter.12.cloned.1.call-done = bf16[512,1024]{1,0:T(8,128)(2,1)} async-done(((bf16[2048,1024]{1,0:T(8,128)(2,1)}), bf16[512,1024]{1,0:T(8,128)(2,1)}) %reduce-scatter.12.cloned.1.call-update) | async-done | bytes 1048592 | tf_op jit(solution)/shard_map/reduce_scatter | solution.py:208
  1418.5 69.4 %all-gather.11.cloned.1.call-done = bf16[2048,1024]{1,0:T(8,128)(2,1)} async-done(((bf16[512,1024]{1,0:T(8,128)(2,1)}), bf16[2048,1024]{1,0:T(8,128)(2,1)}) %all-gather.11.cloned.1.call-update) | async-done | bytes 4194320 | tf_op jit(solution)/shard_map/all_gather | solution.py:306
  1498.4 1848.2 %while.151 = (s32[]{:T(128)}, f32[2048,4,64]{0,2,1:T(8,128)}, f32[2048,4,64]{0,2,1:T(8,128)}, f32[32,4]{0,1:T(4,128)}, f32[64,4]{0,1:T(4,128)}, /*index=5*/bf16[...) while((s32[]{:T(128)}, f32[2048,4,64]{0,2,1:T(8,128)}, ...), condition=%wide.region_26.27_spmd.clone, body=%wide.region_16.26_spmd.clone.sunk | while | flops 4196533760 | bytes 442931200 | solution.py:174
  1528.0 50.8 %while.154 = (s32[]{:T(128)}, f32[4,4,128,2048]{3,1,2,0:T(4,128)}, s32[4,128,2048]{2,1,0:T(8,128)}, bf16[64,4]{0,1:T(4,128)(2,1)S(1)}, s32[]{:T(128)}) while((s32[]{:T(128)}, f32[4,4,128,2048]{3,1,2,0:T(4,128)}, s32[4,128,2048]{2,1,0:T(8,128)}, bf16[64,4]{0,1:T(4,128)(2,1)S(1)}, s32[]{:T(128)}) %tuple.288), condition=%wide.region_20.20_spmd.clone, body=%wide.region_19.19_spmd.clone.sunk | while | flops 150994944 | bytes 7340621 | solution.py:58
  1736.7 138.7 %while.157 = (s32[]{:T(128)}, f32[64,4]{0,1:T(4,128)S(1)}, s32[4]{0:T(128)S(1)}, s32[512,2048]{1,0:T(8,128)}, f32[4,512,2048]{2,0,1:T(4,128)}, /*index=5*/s32[]{:T(128)}, s32[1]{0:T(128)}, s32[]{:T(128)}, s32[]{:T(128)}) while((s32[]{:T(128)}, f32[64,4]{0,1:T(4,128)S(1)}, s32[4]{0:T(128)S(1)}, s32[512,2048]{1,0:T(8,128)}, ...), condition=%wide.region_25.25_spmd.clone, body=%wide.region_24.24_spmd.clone.sunk | while | flops 822084096 | bytes 7342257 | solution.py:87
  1739.5 32.0 fusion.215
  1774.0 32.0 fusion.215
  1808.6 32.0 fusion.215
  1843.2 32.0 fusion.215
  1876.0 80.7 %while.156 = (s32[]{:T(128)}, f32[32,4]{0,1:T(4,128)S(1)}, s32[4]{0:T(128)S(1)}, s32[512,2048]{1,0:T(8,128)}, f32[4,512,2048]{2,0,1:T(4,128)}, /*index=5*/s32[]{:T(128)}, s32[1]{0:T(128)}, s32[]{:T(128)}, s32[]{:T(128)}) while((s32[]{:T(128)}, f32[32,4]{0,1:T(4,128)S(1)}, s32[4]{0:T(128)S(1)}, s32[512,2048]{1,0:T(8,128)}, ...), condition=%wide.region_23.23_spmd.clone, body=%wide.region_22.22_spmd.clone.sunk | while | flops 411042048 | bytes 7341233 | solution.py:87
  1986.6 50.8 %while.154 = (s32[]{:T(128)}, f32[4,4,128,2048]{3,1,2,0:T(4,128)}, s32[4,128,2048]{2,1,0:T(8,128)}, bf16[64,4]{0,1:T(4,128)(2,1)S(1)}, s32[]{:T(128)}) while((s32[]{:T(128)}, f32[4,4,128,2048]{3,1,2,0:T(4,128)}, s32[4,128,2048]{2,1,0:T(8,128)}, bf16[64,4]{0,1:T(4,128)(2,1)S(1)}, s32[]{:T(128)}) %tuple.288), condition=%wide.region_20.20_spmd.clone, body=%wide.region_19.19_spmd.clone.sunk | while | flops 150994944 | bytes 7340621 | solution.py:58
  2196.7 138.7 %while.157 = (s32[]{:T(128)}, f32[64,4]{0,1:T(4,128)S(1)}, s32[4]{0:T(128)S(1)}, s32[512,2048]{1,0:T(8,128)}, f32[4,512,2048]{2,0,1:T(4,128)}, /*index=5*/s32[]{:T(128)}, s32[1]{0:T(128)}, s32[]{:T(128)}, s32[]{:T(128)}) while((s32[]{:T(128)}, f32[64,4]{0,1:T(4,128)S(1)}, s32[4]{0:T(128)S(1)}, s32[512,2048]{1,0:T(8,128)}, ...), condition=%wide.region_25.25_spmd.clone, body=%wide.region_24.24_spmd.clone.sunk | while | flops 822084096 | bytes 7342257 | solution.py:87
  2336.0 80.7 %while.156 = (s32[]{:T(128)}, f32[32,4]{0,1:T(4,128)S(1)}, s32[4]{0:T(128)S(1)}, s32[512,2048]{1,0:T(8,128)}, f32[4,512,2048]{2,0,1:T(4,128)}, /*index=5*/s32[]{:T(128)}, s32[1]{0:T(128)}, s32[]{:T(128)}, s32[]{:T(128)}) while((s32[]{:T(128)}, f32[32,4]{0,1:T(4,128)S(1)}, s32[4]{0:T(128)S(1)}, s32[512,2048]{1,0:T(8,128)}, ...), condition=%wide.region_23.23_spmd.clone, body=%wide.region_22.22_spmd.clone.sunk | while | flops 411042048 | bytes 7341233 | solution.py:87
  2446.7 50.8 %while.154 = (s32[]{:T(128)}, f32[4,4,128,2048]{3,1,2,0:T(4,128)}, s32[4,128,2048]{2,1,0:T(8,128)}, bf16[64,4]{0,1:T(4,128)(2,1)S(1)}, s32[]{:T(128)}) while((s32[]{:T(128)}, f32[4,4,128,2048]{3,1,2,0:T(4,128)}, s32[4,128,2048]{2,1,0:T(8,128)}, bf16[64,4]{0,1:T(4,128)(2,1)S(1)}, s32[]{:T(128)}) %tuple.288), condition=%wide.region_20.20_spmd.clone, body=%wide.region_19.19_spmd.clone.sunk | while | flops 150994944 | bytes 7340621 | solution.py:58
  2656.5 138.7 %while.157 = (s32[]{:T(128)}, f32[64,4]{0,1:T(4,128)S(1)}, s32[4]{0:T(128)S(1)}, s32[512,2048]{1,0:T(8,128)}, f32[4,512,2048]{2,0,1:T(4,128)}, /*index=5*/s32[]{:T(128)}, s32[1]{0:T(128)}, s32[]{:T(128)}, s32[]{:T(128)}) while((s32[]{:T(128)}, f32[64,4]{0,1:T(4,128)S(1)}, s32[4]{0:T(128)S(1)}, s32[512,2048]{1,0:T(8,128)}, ...), condition=%wide.region_25.25_spmd.clone, body=%wide.region_24.24_spmd.clone.sunk | while | flops 822084096 | bytes 7342257 | solution.py:87
  2795.9 80.7 %while.156 = (s32[]{:T(128)}, f32[32,4]{0,1:T(4,128)S(1)}, s32[4]{0:T(128)S(1)}, s32[512,2048]{1,0:T(8,128)}, f32[4,512,2048]{2,0,1:T(4,128)}, /*index=5*/s32[]{:T(128)}, s32[1]{0:T(128)}, s32[]{:T(128)}, s32[]{:T(128)}) while((s32[]{:T(128)}, f32[32,4]{0,1:T(4,128)S(1)}, s32[4]{0:T(128)S(1)}, s32[512,2048]{1,0:T(8,128)}, ...), condition=%wide.region_23.23_spmd.clone, body=%wide.region_22.22_spmd.clone.sunk | while | flops 411042048 | bytes 7341233 | solution.py:87
  2906.5 50.8 %while.154 = (s32[]{:T(128)}, f32[4,4,128,2048]{3,1,2,0:T(4,128)}, s32[4,128,2048]{2,1,0:T(8,128)}, bf16[64,4]{0,1:T(4,128)(2,1)S(1)}, s32[]{:T(128)}) while((s32[]{:T(128)}, f32[4,4,128,2048]{3,1,2,0:T(4,128)}, s32[4,128,2048]{2,1,0:T(8,128)}, bf16[64,4]{0,1:T(4,128)(2,1)S(1)}, s32[]{:T(128)}) %tuple.288), condition=%wide.region_20.20_spmd.clone, body=%wide.region_19.19_spmd.clone.sunk | while | flops 150994944 | bytes 7340621 | solution.py:58
  3116.5 138.7 %while.157 = (s32[]{:T(128)}, f32[64,4]{0,1:T(4,128)S(1)}, s32[4]{0:T(128)S(1)}, s32[512,2048]{1,0:T(8,128)}, f32[4,512,2048]{2,0,1:T(4,128)}, /*index=5*/s32[]{:T(128)}, s32[1]{0:T(128)}, s32[]{:T(128)}, s32[]{:T(128)}) while((s32[]{:T(128)}, f32[64,4]{0,1:T(4,128)S(1)}, s32[4]{0:T(128)S(1)}, s32[512,2048]{1,0:T(8,128)}, ...), condition=%wide.region_25.25_spmd.clone, body=%wide.region_24.24_spmd.clone.sunk | while | flops 822084096 | bytes 7342257 | solution.py:87
  3255.8 80.7 %while.156 = (s32[]{:T(128)}, f32[32,4]{0,1:T(4,128)S(1)}, s32[4]{0:T(128)S(1)}, s32[512,2048]{1,0:T(8,128)}, f32[4,512,2048]{2,0,1:T(4,128)}, /*index=5*/s32[]{:T(128)}, s32[1]{0:T(128)}, s32[]{:T(128)}, s32[]{:T(128)}) while((s32[]{:T(128)}, f32[32,4]{0,1:T(4,128)S(1)}, s32[4]{0:T(128)S(1)}, s32[512,2048]{1,0:T(8,128)}, ...), condition=%wide.region_23.23_spmd.clone, body=%wide.region_22.22_spmd.clone.sunk | while | flops 411042048 | bytes 7341233 | solution.py:87
  3409.9 139.8 %reduce-scatter.16.cloned.1.call-done = f32[512,1024]{1,0:T(8,128)} async-done(((f32[2048,1024]{1,0:T(8,128)}), f32[512,1024]{1,0:T(8,128)}) %reduce-scatter.16.cloned.1.call-update) | async-done | bytes 2097168 | tf_op jit(solution)/shard_map/reduce_scatter | solution.py:315
  3552.1 41.1 %all-reduce.4 = (f32[1024]{0:T(1024)S(1)}, f32[1024]{0:T(1024)S(1)}) all-reduce(f32[1024]{0:T(1024)S(1)} %get-tuple-element.1026, f32[1024]{0:T(1024)S(1)} %copy-done.31), channel_id=6, replica_groups=mesh['wide'=8,'narrow'=4] {'wide','narrow'}, use_global_device_ids=true, to_apply=%region_30.31.clone | all-reduce | flops 2048 | bytes 16384
  3599.8 39.6 %reduce-scatter.20.cloned.1.call-done = f32[256,128]{1,0:T(8,128)} async-done(((f32[256,1024]{1,0:T(8,128)}), f32[256,128]{1,0:T(8,128)}) %reduce-scatter.20.cloned.1.call-update) | async-done | bytes 131088 | tf_op jit(solution)/shard_map/reduce_scatter | solution.py:322
  (679 shorter events, 2832.8 us)
Async XLA Ops:
  7.2 1145.7 %copy-start = (bf16[704,1024]{1,0:T(8,128)(2,1)S(1)}, bf16[704,1024]{1,0:T(8,128)(2,1)}, u32[]{:S(2)}) copy-start(bf16[704,1024]{1,0:T(8,128)(2,1)} %param.45) | copy-start | bytes 4325380
  7.2 89.7 %all-gather.5.cloned.1.call-start = ((), (), s32[]{:S(2)}) async-start(), calls=%async_computation.8 | async-start | bytes 5242880 | tf_op jit(solution)/shard_map/all_gather | solution.py:192
  13.3 972.7 %reduce-scatter.10.cloned.1.call-start = ((), (), s32[]{:S(2)}) async-start(), calls=%async_computation.9 | async-start | bytes 10485760 | tf_op jit(solution)/shard_map/reduce_scatter | solution.py:198
  842.8 143.2 %copy-start.6 = (bf16[512,1024]{1,0:T(8,128)(2,1)S(1)}, bf16[512,1024]{1,0:T(8,128)(2,1)}, u32[]{:S(2)}) copy-start(bf16[512,1024]{1,0:T(8,128)(2,1)} %param.33) | copy-start | bytes 3145732
  842.9 229.3 %all-gather.7.cloned.1.call-start = ((), (), s32[]{:S(2)}) async-start(), calls=%async_computation.10 | async-start | bytes 5242880 | tf_op jit(solution)/shard_map/all_gather | solution.py:205
  990.5 162.4 %all-gather.9.cloned.1.call-start = ((), (), s32[]{:S(2)}) async-start(), calls=%async_computation.12 | async-start | bytes 5242880 | tf_op jit(solution)/shard_map/all_gather | solution.py:293
  991.1 330.5 %reduce-scatter.14.cloned.1.call-start = ((), (), s32[]{:S(2)}) async-start(), calls=%async_computation.13 | async-start | bytes 10485760 | tf_op jit(solution)/shard_map/reduce_scatter | solution.py:301
  1178.4 222.8 %reduce-scatter.12.cloned.1.call-start = ((), (), s32[]{:S(2)}) async-start(), calls=%async_computation.11 | async-start | bytes 5242880 | tf_op jit(solution)/shard_map/reduce_scatter | solution.py:208
  1185.4 215.8 %copy-start.11 = (bf16[512,1024]{1,0:T(8,128)(2,1)S(1)}, bf16[512,1024]{1,0:T(8,128)(2,1)}, u32[]{:S(2)}) copy-start(bf16[512,1024]{1,0:T(8,128)(2,1)} %param.34) | copy-start | bytes 3145732
  1185.4 302.5 %all-gather.11.cloned.1.call-start = ((), (), s32[]{:S(2)}) async-start(), calls=%async_computation.14 | async-start | bytes 5242880 | tf_op jit(solution)/shard_map/all_gather | solution.py:306
  1406.4 1972.7 %reduce-scatter.22.cloned.1.call-start = ((), (), s32[]{:S(2)}) async-start(), calls=%async_computation.18 | async-start | bytes 6488064 | tf_op jit(solution)/shard_map/reduce_scatter | solution.py:323
  1418.4 1989.7 %reduce-scatter.18.cloned.1.call-start = ((), (), s32[]{:S(2)}) async-start(), calls=%async_computation.16 | async-start | bytes 3538944 | tf_op jit(solution)/shard_map/reduce_scatter | solution.py:321
  1736.6 138.8 %copy-start.19 = (f32[64,4]{0,1:T(4,128)S(1)}, f32[64,4]{0,1:T(4,128)}, u32[]{:S(2)}) copy-start(f32[64,4]{0,1:T(4,128)} %get-tuple-element.1841) | copy-start | bytes 3076 | tf_op jit(solution)/shard_map/while
  1736.7 138.8 %copy-start.27 = (f32[32,4]{0,1:T(4,128)S(1)}, f32[32,4]{0,1:T(4,128)}, u32[]{:S(2)}) copy-start(f32[32,4]{0,1:T(4,128)} %custom-call.15) | copy-start | bytes 1540 | tf_op jit(solution)/shard_map/while
  1736.7 138.8 %copy-start.42 = (s32[4]{0:T(128)S(1)}, s32[4]{0:T(128)}, u32[]{:S(2)}) copy-start(s32[4]{0:T(128)} %iota.160) | copy-start | bytes 52 | tf_op jit(solution)/shard_map/while
  2196.7 138.7 %copy-start.19 = (f32[64,4]{0,1:T(4,128)S(1)}, f32[64,4]{0,1:T(4,128)}, u32[]{:S(2)}) copy-start(f32[64,4]{0,1:T(4,128)} %get-tuple-element.1841) | copy-start | bytes 3076 | tf_op jit(solution)/shard_map/while
  2196.7 138.7 %copy-start.27 = (f32[32,4]{0,1:T(4,128)S(1)}, f32[32,4]{0,1:T(4,128)}, u32[]{:S(2)}) copy-start(f32[32,4]{0,1:T(4,128)} %custom-call.15) | copy-start | bytes 1540 | tf_op jit(solution)/shard_map/while
  2196.7 138.7 %copy-start.42 = (s32[4]{0:T(128)S(1)}, s32[4]{0:T(128)}, u32[]{:S(2)}) copy-start(s32[4]{0:T(128)} %iota.160) | copy-start | bytes 52 | tf_op jit(solution)/shard_map/while
  2656.5 138.8 %copy-start.19 = (f32[64,4]{0,1:T(4,128)S(1)}, f32[64,4]{0,1:T(4,128)}, u32[]{:S(2)}) copy-start(f32[64,4]{0,1:T(4,128)} %get-tuple-element.1841) | copy-start | bytes 3076 | tf_op jit(solution)/shard_map/while
  2656.5 138.8 %copy-start.27 = (f32[32,4]{0,1:T(4,128)S(1)}, f32[32,4]{0,1:T(4,128)}, u32[]{:S(2)}) copy-start(f32[32,4]{0,1:T(4,128)} %custom-call.15) | copy-start | bytes 1540 | tf_op jit(solution)/shard_map/while
  2656.5 138.8 %copy-start.42 = (s32[4]{0:T(128)S(1)}, s32[4]{0:T(128)}, u32[]{:S(2)}) copy-start(s32[4]{0:T(128)} %iota.160) | copy-start | bytes 52 | tf_op jit(solution)/shard_map/while
  3116.5 138.7 %copy-start.19 = (f32[64,4]{0,1:T(4,128)S(1)}, f32[64,4]{0,1:T(4,128)}, u32[]{:S(2)}) copy-start(f32[64,4]{0,1:T(4,128)} %get-tuple-element.1841) | copy-start | bytes 3076 | tf_op jit(solution)/shard_map/while
  3116.5 138.7 %copy-start.27 = (f32[32,4]{0,1:T(4,128)S(1)}, f32[32,4]{0,1:T(4,128)}, u32[]{:S(2)}) copy-start(f32[32,4]{0,1:T(4,128)} %custom-call.15) | copy-start | bytes 1540 | tf_op jit(solution)/shard_map/while
  3116.5 138.7 %copy-start.42 = (s32[4]{0:T(128)S(1)}, s32[4]{0:T(128)}, u32[]{:S(2)}) copy-start(s32[4]{0:T(128)} %iota.160) | copy-start | bytes 52 | tf_op jit(solution)/shard_map/while
  3356.9 192.8 %reduce-scatter.16.cloned.1.call-start = ((), (), s32[]{:S(2)}) async-start(), calls=%async_computation.15 | async-start | bytes 10485760 | tf_op jit(solution)/shard_map/reduce_scatter | solution.py:315
  3364.1 235.7 %reduce-scatter.24.cloned.1.call-start = ((), (), s32[]{:S(2)}) async-start(), calls=%async_computation.19 | async-start | bytes 3244032 | tf_op jit(solution)/shard_map/reduce_scatter | solution.py:324
  3372.6 266.8 %reduce-scatter.20.cloned.1.call-start = ((), (), s32[]{:S(2)}) async-start(), calls=%async_computation.17 | async-start | bytes 1179648 | tf_op jit(solution)/shard_map/reduce_scatter | solution.py:322
  3379.0 170.6 %copy-start.7 = (bf16[512,1024]{1,0:T(8,128)(2,1)S(1)}, bf16[512,1024]{1,0:T(8,128)(2,1)}, u32[]{:S(2)}) copy-start(bf16[512,1024]{1,0:T(8,128)(2,1)} %param.33) | copy-start | bytes 3145732
  3379.0 170.6 %copy-start.26 = (f32[1024]{0:T(1024)S(1)}, f32[1024]{0:T(1024)}, u32[]{:S(2)}) copy-start(f32[1024]{0:T(1024)} %copy-done.25) | copy-start | bytes 12292
  3379.0 170.6 %copy-start.30 = (f32[512]{0:T(512)S(1)}, f32[512]{0:T(512)}, u32[]{:S(2)}) copy-start(f32[512]{0:T(512)} %copy-done.29) | copy-start | bytes 6148
  3379.0 173.0 %copy-start.31 = (f32[1024]{0:T(1024)S(1)}, f32[1024]{0:T(1024)}, u32[]{:S(2)}) copy-start(f32[1024]{0:T(1024)} %get-tuple-element.1024) | copy-start | bytes 12292
  3379.1 215.3 %copy-start.32 = (f32[512]{0:T(512)S(1)}, f32[512]{0:T(512)}, u32[]{:S(2)}) copy-start(f32[512]{0:T(512)} %get-tuple-element.1178) | copy-start | bytes 6148
  (90 other events, 2138.9 us)
Sparse Core Ops, SparseCore 0:
  13.5 83.4 all-gather.4
  843.0 142.9 reduce-scatter.9
  990.6 81.4 all-gather.6
  1073.6 79.2 all-gather.8
  1178.5 143.0 reduce-scatter.13
  1323.7 77.4 reduce-scatter.11
  1406.6 81.2 all-gather.10
  1491.7 57.5 reduce-scatter.21
  3357.0 45.7 reduce-scatter.17
  3405.1 144.5 reduce-scatter.15
  3554.0 45.7 reduce-scatter.23
  3603.4 35.9 reduce-scatter.19
where the time goes:
time: 3660 us; the launch traced here: 3650 us
  matrix products  1820 us (50%)
  waiting for transfers between devices  830 us (23%)
  local copies, waits for them, and re-layouts  739 us (20%)
  other arithmetic  127 us (3%)
  blocking collectives  65.6 us (2%)
  loops' own time  52.7 us (1%)
    dot_general x32, matrix products, one_piece(): jnp.einsum('nas,las->nl', indicator_matrix, score_piece, precision=highes...  793 us
    dot_general x64, matrix products, one_piece(): jnp.einsum('car,cg->gar', indicator_matrix, table_reduced, preferred_elem...  573 us
    transpose x16, local copies, waits for them, and re-layouts, bucket_bias(): jnp.transpose(pieces, (1, 0, 2, 3))  285 us
    dot_general x8, matrix products, block_scores(): jnp.einsum('qhd,khd->hqk', query_rows, keys, preferred_element_type=jnp.f...  175 us
    reduce_scatter x1, waiting for transfers between devices, run_forward(): lax.psum_scatter(jnp.dot(attended, w_out_used, preferred_element_type=jnp...  142 us
    reduce_scatter x1, waiting for transfers between devices, on_device(): lax.psum_scatter(contract_cols(d_project, w_project), 'narrow', scatter_d...  140 us
    reduce_scatter x1, waiting for transfers between devices, on_device(): lax.psum_scatter(contract_cols(d_gate_up, w_gate_up), 'narrow', scatter_d...  136 us
    another operation x18, local copies, waits for them, and re-layouts  105 us
  transfers between devices with their start and end apart: 12, of which 10 were waited for; matrix products, arithmetic and copies ran while one was open for 52% of the time, Pallas kernels for 0%

commit v1 on v0

v1 whole, which is shorter than its diff:
```python
import functools
import jax
import jax.numpy as jnp
from jax import lax
from jax.experimental import pallas as pl
from jax.experimental.pallas import tpu as pltpu
from jax.sharding import PartitionSpec as P

DH = 64
BIAS_SCALE = 4096.0
LOG2E = 1.4426950408889634
f32 = jnp.float32
bf16 = jnp.bfloat16
NT = (((1,), (1,)), ((), ()))
NN = (((1,), (0,)), ((), ()))


def dot(a, b, dims=NN):
    return lax.dot_general(a, b, dims, preferred_element_type=f32)


def key_window(len_ref, first, last, count, width):
    ends = []
    total = 0
    for p in range(len_ref.shape[1]):
        total = total + len_ref[0, p]
        ends.append(total)
    start = 0
    stop = count
    for e in ends:
        start = jnp.where(e <= first, e, start)
    for e in reversed(ends):
        stop = jnp.where(e > last, e, stop)
    base = (start // 128) * 128
    steps = (stop - base + width - 1) // width
    base = jnp.minimum(base, count - steps * width)
    return ends, base, steps


def own_half(shape, head):
    lane = lax.broadcasted_iota(jnp.int32, shape, len(shape) - 1)
    return (lane < DH) if head % 2 == 0 else (lane >= DH)


def fill_values(vext, v_ref, heads):
    for h in range(heads):
        vp = v_ref[:, (h // 2) * 128:(h // 2 + 1) * 128]
        vext[h] = jnp.where(own_half(vp.shape, h), vp, jnp.ones_like(vp))


def forward_kernel(len_ref, q_ref, k_ref, v_ref, rel_ref, lay_ref, tab_ref, kmask_ref,
                   att_ref, rinv_ref, e_ref, code_ref,
                   s_scr, m_scr, vext, colcode, *, width, heads):
    tq, count = rel_ref.shape
    pairs = heads // 2
    i = pl.program_id(0)
    t0 = i * tq
    ends, base, steps = key_window(len_ref, t0, t0 + tq - 1, count, width)

    @pl.when(i == 0)
    def _():
        fill_values(vext, v_ref, heads)
        pos = lax.broadcasted_iota(jnp.int32, (8, count), 1)
        page = jnp.zeros((8, count), jnp.int32)
        for e in ends:
            page = page + (pos >= e).astype(jnp.int32)
        colcode[...] = jnp.where(kmask_ref[...] == 1, page, -1)

    rowpos = lax.broadcasted_iota(jnp.int32, (tq, 128), 0) + t0
    rowpage = jnp.zeros((tq, 128), jnp.int32)
    for e in ends:
        rowpage = rowpage + (rowpos >= e).astype(jnp.int32)
    lanes = lax.broadcasted_iota(jnp.int32, (tq, 128), 1)
    scaled = []
    for h in range(heads):
        qp = q_ref[:, (h // 2) * 128:(h // 2 + 1) * 128]
        scaled.append(jnp.where(own_half(qp.shape, h), qp * bf16(BIAS_SCALE), jnp.zeros_like(qp)))
        m_scr[h] = jnp.full((tq, 128), -3e38, f32)
    tabs = [[jnp.broadcast_to(tab_ref[2 * p + r:2 * p + r + 1, :], (tq, 128)) for r in range(2)]
            for p in range(pairs)]

    def scores(j, carry):
        c0 = pl.multiple_of(base + j * width, 128)
        raw = [dot(scaled[h], k_ref[pl.ds(c0, width), (h // 2) * 128:(h // 2 + 1) * 128], NT)
               for h in range(heads)]
        for half in range(width // 128):
            cc = pl.multiple_of(c0 + half * 128, 128)
            rel = rel_ref[:, pl.ds(cc, 128)]
            lay = lay_ref[:, pl.ds(cc, 128)]
            code_ref[:, pl.ds(cc, 128)] = (rel + lay * 32).astype(jnp.int16)
            col = jnp.broadcast_to(colcode[0:1, pl.ds(cc, 128)], (tq, 128))
            seen = (rowpage == col) | (rowpos == lanes + cc)
            hide = jnp.where(seen, f32(0.0), f32(-1e30))
            for p in range(pairs):
                word = (jnp.take_along_axis(tabs[p][0], rel, axis=1, mode="promise_in_bounds")
                        + jnp.take_along_axis(tabs[p][1], lay, axis=1, mode="promise_in_bounds"))
                parts = ((word & 0xFFFF).astype(f32), (word >> 16).astype(f32))
                for r in range(2):
                    h = 2 * p + r
                    s = raw[h][:, half * 128:(half + 1) * 128] + parts[r] + hide
                    s_scr[h, :, pl.ds(cc, 128)] = s
                    m_scr[h] = jnp.maximum(m_scr[h], s)
        return carry

    lax.fori_loop(0, steps, scores, 0)

    for p in range(pairs):
        accs = []
        for h in (2 * p, 2 * p + 1):
            top = jnp.max(m_scr[h], axis=1, keepdims=True)

            def values(j, acc):
                c0 = pl.multiple_of(base + j * width, 128)
                e = jnp.exp2((s_scr[h, :, pl.ds(c0, width)] - top) * f32(LOG2E / BIAS_SCALE)).astype(bf16)
                e_ref[h, :, pl.ds(c0, width)] = e
                return acc + dot(e, vext[h, pl.ds(c0, width), :])

            accs.append(lax.fori_loop(0, steps, values, jnp.zeros((tq, 128), f32)))
        low = own_half((tq, 128), 0)
        mixed = jnp.where(low, accs[0], accs[1])
        total = pltpu.roll(jnp.where(low, accs[1], accs[0]), DH, 1)
        rinv = 1.0 / total
        att_ref[:, p * 128:(p + 1) * 128] = (mixed * rinv).astype(bf16)
        rinv_ref[:, p * 128:(p + 1) * 128] = rinv


def attention_forward(page_lengths, proj, rel, lay, tab, kmask, tq=256, width=256):
    count = proj.shape[0]
    hc = proj.shape[1] // 3
    heads = hc // DH
    grid = (count // tq,)
    return pl.pallas_call(
        functools.partial(forward_kernel, width=width, heads=heads),
        grid=grid,
        in_specs=[
            pl.BlockSpec(memory_space=pltpu.SMEM),
            pl.BlockSpec((tq, hc), lambda i: (i, 0)),
            pl.BlockSpec((count, hc), lambda i: (0, 1)),
            pl.BlockSpec((count, hc), lambda i: (0, 2)),
            pl.BlockSpec((tq, count), lambda i: (i, 0)),
            pl.BlockSpec((tq, count), lambda i: (i, 0)),
            pl.BlockSpec(tab.shape, lambda i: (0, 0)),
            pl.BlockSpec((1, count), lambda i: (0, 0)),
        ],
        out_specs=[
            pl.BlockSpec((tq, hc), lambda i: (i, 0)),
            pl.BlockSpec((tq, hc), lambda i: (i, 0)),
            pl.BlockSpec((heads, tq, count), lambda i: (0, i, 0)),
            pl.BlockSpec((tq, count), lambda i: (i, 0)),
        ],
        out_shape=[
            jax.ShapeDtypeStruct((count, hc), bf16),
            jax.ShapeDtypeStruct((count, hc), f32),
            jax.ShapeDtypeStruct((heads, count, count), bf16),
            jax.ShapeDtypeStruct((count, count), jnp.int16),
        ],
        scratch_shapes=[
            pltpu.VMEM((heads, tq, count), f32),
            pltpu.VMEM((heads, tq, 128), f32),
            pltpu.VMEM((heads, count, 128), bf16),
            pltpu.VMEM((8, count), jnp.int32),
        ],
        compiler_params=pltpu.CompilerParams(vmem_limit_bytes=56 << 20),
        name="attention_forward",
    )(page_lengths, proj, proj, proj, rel, lay, tab, kmask.reshape(1, count))


def bias_words(rel_table, layout_table):
    def pack(table):
        whole = jnp.round(table.astype(f32) * BIAS_SCALE).astype(jnp.int32)
        low = jnp.clip(whole[:, 0::2] + 16384, 0, 32767)
        high = jnp.clip(whole[:, 1::2], -16384, 16383)
        words = (high * 65536 + low).T
        return jnp.pad(words, ((0, 0), (0, 128 - words.shape[1])))
    both = jnp.stack([pack(rel_table), pack(layout_table)], axis=1)
    return both.reshape(-1, 128)


def signs(code, shift, bits):
    return [jnp.where((code & jnp.int16(1 << (shift + b))) == 0, bf16(1.0), bf16(-1.0))
            for b in range(bits)]


def walsh(sign_list):
    out = [None]
    for s in sign_list:
        out = out + [s if o is None else o * s for o in out]
    return out


def backward_kernel(len_ref, q_ref, k_ref, v_ref, e_ref, code_ref, da_ref, att_ref, rinv_ref,
                    dq_ref, dk_ref, dv_ref, hl_ref, hr_ref,
                    vext, lhs_scr, dat_scr, qt_scr, ds_scr, dq_scr, dkt, dvt, left, blay, brel,
                    *, width, heads):
    tq, count = code_ref.shape
    pairs = heads // 2
    i = pl.program_id(0)
    t0 = i * tq
    ends, base, steps = key_window(len_ref, t0, t0 + tq - 1, count, width)

    @pl.when(i == 0)
    def _():
        fill_values(vext, v_ref, heads)
        dkt[...] = jnp.zeros_like(dkt)
        dvt[...] = jnp.zeros_like(dvt)
        hl_ref[...] = jnp.zeros_like(hl_ref)
        hr_ref[...] = jnp.zeros_like(hr_ref)

    low = own_half((tq, 128), 0)
    lane = lax.broadcasted_iota(jnp.int32, (tq, 128), 1)
    first_part = (lane & 32) == 0
    for p in range(pairs):
        cols = slice(p * 128, (p + 1) * 128)
        da = (da_ref[:, cols].astype(f32) * rinv_ref[:, cols]).astype(bf16)
        daf = da.astype(f32)
        prod = daf * att_ref[:, cols].astype(f32)
        for r in range(2):
            own = low if r == 0 else jnp.logical_not(low)
            delta = jnp.sum(jnp.where(own, prod, 0.0), axis=1, keepdims=True) * f32(-1.0 / 32)
            high = delta.astype(bf16).astype(f32)
            rest = delta - high
            lhs_scr[2 * p + r] = jnp.where(own, daf, jnp.where(first_part, high, rest)).astype(bf16)
        dat_scr[p] = daf.T.astype(bf16)
        qt_scr[p] = q_ref[:, cols].astype(f32).T.astype(bf16)
        dq_scr[p] = jnp.zeros((tq, 128), f32)

    def chunk(j, carry):
        c0 = pl.multiple_of(base + j * width, 128)
        here = pl.ds(c0, width)
        for p in range(pairs):
            cols = slice(p * 128, (p + 1) * 128)
            kp = k_ref[here, cols]
            dqs = []
            for r in range(2):
                h = 2 * p + r
                rows = slice(r * DH, (r + 1) * DH)
                e = e_ref[h, :, here]
                d = dot(lhs_scr[h], vext[h, here, :], NT)
                ds = (e.astype(f32) * d).astype(bf16)
                ds_scr[h] = ds
                dqs.append(dot(ds, kp))
                dkt[p, rows, here] += dot(qt_scr[p, rows, :], ds)
                dvt[p, rows, here] += dot(dat_scr[p, rows, :], e)
            dq_scr[p] += jnp.where(low, dqs[0], dqs[1])
        for b in range(tq // 16):
            rows = slice(16 * b, 16 * (b + 1))
            span = slice(b * width, (b + 1) * width)
            code = code_ref[rows, here]
            rel_signs = signs(code, 0, 5)
            lay_signs = signs(code, 5, 6)
            left_lay = walsh(lay_signs[:2])[1:]
            left_rel = walsh(rel_signs[:2])[1:]
            for h in range(heads):
                ds = ds_scr[h, rows, :]
                place = 16 * (3 * heads + h)
                left[place:place + 16, span] = ds
                for a in range(3):
                    place = 16 * (a * heads + h)
                    left[place:place + 16, span] = ds * left_lay[a]
                    place = 16 * ((4 + a) * heads + h)
                    left[place:place + 16, span] = ds * left_rel[a]
            for n, func in enumerate(walsh(lay_signs[2:])):
                blay[16 * n:16 * (n + 1), span] = jnp.ones((16, width), bf16) if func is None else func
            for n, func in enumerate(walsh(rel_signs[2:])):
                brel[16 * n:16 * (n + 1), span] = jnp.ones((16, width), bf16) if func is None else func
        group = 64 * heads
        hl_ref[...] += dot(left[:group, :], blay[...], NT)
        hr_ref[...] += dot(left[48 * heads:48 * heads + group, :], brel[...], NT)
        return carry

    lax.fori_loop(0, steps, chunk, 0)
    for p in range(pairs):
        dq_ref[:, p * 128:(p + 1) * 128] = dq_scr[p].astype(bf16)

    @pl.when(i == pl.num_programs(0) - 1)
    def _():
        for p in range(pairs):
            for c in range(0, count, 256):
                dk_ref[c:c + 256, p * 128:(p + 1) * 128] = dkt[p, :, c:c + 256].T.astype(bf16)
                dv_ref[c:c + 256, p * 128:(p + 1) * 128] = dvt[p, :, c:c + 256].T.astype(bf16)


def attention_backward(page_lengths, proj, e, code, d_att, att, rinv, tq=256, width=256):
    count = proj.shape[0]
    hc = proj.shape[1] // 3
    heads = hc // DH
    pairs = heads // 2
    grid = (count // tq,)
    deep = tq // 16 * width
    tile = lambda i: (i, 0)
    fixed = lambda i: (0, 0)
    return pl.pallas_call(
        functools.partial(backward_kernel, width=width, heads=heads),
        grid=grid,
        in_specs=[
            pl.BlockSpec(memory_space=pltpu.SMEM),
            pl.BlockSpec((tq, hc), tile),
            pl.BlockSpec((count, hc), lambda i: (0, 1)),
            pl.BlockSpec((count, hc), lambda i: (0, 2)),
            pl.BlockSpec((heads, tq, count), lambda i: (0, i, 0)),
            pl.BlockSpec((tq, count), tile),
            pl.BlockSpec((tq, hc), tile),
            pl.BlockSpec((tq, hc), tile),
            pl.BlockSpec((tq, hc), tile),
        ],
        out_specs=[
            pl.BlockSpec((tq, hc), tile),
            pl.BlockSpec((count, hc), fixed),
            pl.BlockSpec((count, hc), fixed),
            pl.BlockSpec((64 * heads, 256), fixed),
            pl.BlockSpec((64 * heads, 128), fixed),
        ],
        out_shape=[
            jax.ShapeDtypeStruct((count, hc), bf16),
            jax.ShapeDtypeStruct((count, hc), bf16),
            jax.ShapeDtypeStruct((count, hc), bf16),
            jax.ShapeDtypeStruct((64 * heads, 256), f32),
            jax.ShapeDtypeStruct((64 * heads, 128), f32),
        ],
        scratch_shapes=[
            pltpu.VMEM((heads, count, 128), bf16),
            pltpu.VMEM((heads, tq, 128), bf16),
            pltpu.VMEM((pairs, 128, tq), bf16),
            pltpu.VMEM((pairs, 128, tq), bf16),
            pltpu.VMEM((heads, tq, width), bf16),
            pltpu.VMEM((pairs, tq, 128), f32),
            pltpu.VMEM((pairs, 128, count), f32),
            pltpu.VMEM((pairs, 128, count), f32),
            pltpu.VMEM((112 * heads, deep), bf16),
            pltpu.VMEM((256, deep), bf16),
            pltpu.VMEM((128, deep), bf16),
        ],
        compiler_params=pltpu.CompilerParams(vmem_limit_bytes=56 << 20),
        name="attention_backward",
    )(page_lengths, proj, proj, proj, e, code, d_att, att, rinv)


def bucket_sums(raw, heads, left_first, right_bits):
    right = raw.shape[1] // 16
    cube = raw.reshape(4, heads, 16, right, 16)
    traced = jnp.sum(cube * jnp.eye(16, dtype=f32)[None, None, :, None, :], axis=(2, 4))
    if not left_first:
        traced = jnp.concatenate([traced[3:], traced[:3]], axis=0)

    def table(n):
        v = lax.iota(jnp.int32, n)
        both = v[:, None] & v[None, :]
        return (1 - 2 * (lax.population_count(both) & 1)).astype(f32)

    hi = table(right)
    lo = table(4)
    out = jnp.einsum("ahn,ax,ny->yxh", traced, lo, hi, precision=lax.Precision.HIGHEST)
    return out.reshape(4 * right, heads) / (4 * right)


epsilon = 1e-06


def contract_rows(left, right):
    return lax.dot_general(
        left, right, (((0,), (0,)), ((), ())), preferred_element_type=jnp.float32
    )


def contract_cols(left, right):
    return lax.dot_general(
        left, right, (((1,), (1,)), ((), ())), preferred_element_type=jnp.float32
    )


def gated(gate, upward):
    return jax.nn.gelu(gate, approximate=True) * upward


def norm_rows(rows, gain):
    scale = lax.rsqrt(jnp.mean(rows * rows, axis=-1, keepdims=True) + epsilon)
    return (scale, (rows * scale * gain).astype(jnp.bfloat16))


def norm_back(d_normed, rows, scale, gain):
    shaped = d_normed * gain
    gain_term = jnp.sum(d_normed * rows * scale, axis=0)
    cubed = scale * scale * scale
    d_rows = scale * shaped - rows * cubed * jnp.mean(shaped * rows, axis=-1, keepdims=True)
    return (d_rows, gain_term)


def scatter_narrow(array):
    return lax.psum_scatter(array.astype(bf16), "narrow", scatter_dimension=0, tiled=True).astype(f32)


def on_device(
    layer_input,
    out_grad,
    norm_attn_gain,
    w_query,
    w_key,
    w_value,
    w_out,
    rel_table,
    layout_table,
    norm_ffn_gain,
    w_gate,
    w_up,
    down_projection_weight,
    page_lengths,
    key_mask,
    rel_bucket,
    layout_bucket,
):
    head_cols = w_query.shape[1]
    heads = head_cols // DH
    hidden_cols = w_gate.shape[1]
    gain_attn = norm_attn_gain.astype(f32)
    gain_ffn = norm_ffn_gain.astype(f32)
    w_project = jnp.concatenate([w_query, w_key, w_value], axis=1)
    w_gate_up = jnp.concatenate([w_gate, w_up], axis=1)
    resid = layer_input.astype(f32)
    grad_all = lax.all_gather(out_grad, "narrow", axis=0, tiled=True)

    scale_attn, normed_attn = norm_rows(resid, gain_attn)
    normed_attn_all = lax.all_gather(normed_attn, "narrow", axis=0, tiled=True)
    projected = dot(normed_attn_all, w_project).astype(bf16)
    attended, rinv, exps, codes = attention_forward(
        page_lengths, projected, rel_bucket, layout_bucket, bias_words(rel_table, layout_table), key_mask)
    middle = resid + scatter_narrow(dot(attended, w_out))
    scale_ffn, normed_ffn = norm_rows(middle, gain_ffn)
    normed_ffn_all = lax.all_gather(normed_ffn, "narrow", axis=0, tiled=True)
    gate_up = dot(normed_ffn_all, w_gate_up)
    hidden, pullback = jax.vjp(gated, gate_up[:, :hidden_cols], gate_up[:, hidden_cols:])
    hidden = hidden.astype(bf16)
    layer_out = (middle + scatter_narrow(dot(hidden, down_projection_weight))).astype(bf16)

    grad_down = contract_rows(hidden, grad_all)
    d_hidden = contract_cols(grad_all, down_projection_weight)
    d_gate, d_up = pullback(d_hidden)
    d_gate_up = jnp.concatenate([d_gate, d_up], axis=1).astype(bf16)
    grad_gate_up = contract_rows(normed_ffn_all, d_gate_up)
    d_normed_ffn = scatter_narrow(contract_cols(d_gate_up, w_gate_up))
    d_middle_norm, gain_ffn_term = norm_back(d_normed_ffn, middle, scale_ffn, gain_ffn)
    d_middle = out_grad.astype(f32) + d_middle_norm
    d_middle_all = lax.all_gather(d_middle.astype(bf16), "narrow", axis=0, tiled=True)
    grad_wout = contract_rows(attended, d_middle_all)
    d_attended = contract_cols(d_middle_all, w_out).astype(bf16)
    d_query, d_keys, d_values, raw_lay, raw_rel = attention_backward(
        page_lengths, projected, exps, codes, d_attended, attended, rinv)
    grad_relative = bucket_sums(raw_rel, heads, True, 3)
    grad_layout = bucket_sums(raw_lay, heads, False, 4)
    d_project = jnp.concatenate([d_query, d_keys, d_values], axis=1)
    grad_project = contract_rows(normed_attn_all, d_project)
    d_normed_attn = scatter_narrow(contract_cols(d_project, w_project))
    d_resid, gain_attn_term = norm_back(d_normed_attn, resid, scale_attn, gain_attn)
    in_grad = d_middle + d_resid

    def over_wide(array, dim):
        return lax.psum_scatter(array, "wide", scatter_dimension=dim, tiled=True)

    sum_project = over_wide(grad_project, 0)
    sum_wout = over_wide(grad_wout, 1)
    sum_gate_up = over_wide(grad_gate_up, 0)
    sum_down = over_wide(grad_down, 1)
    sum_relative = over_wide(grad_relative, 0)
    sum_layout = over_wide(grad_layout, 0)
    sum_gain_attn = lax.psum_scatter(gain_attn_term, ("wide", "narrow"), scatter_dimension=0, tiled=True)
    sum_gain_ffn = lax.psum_scatter(gain_ffn_term, ("wide", "narrow"), scatter_dimension=0, tiled=True)
    return (
        layer_out,
        in_grad,
        sum_gain_attn,
        sum_project[:, :head_cols],
        sum_project[:, head_cols : 2 * head_cols],
        sum_project[:, 2 * head_cols :],
        sum_wout,
        sum_relative,
        sum_layout,
        sum_gain_ffn,
        sum_gate_up[:, :hidden_cols],
        sum_gate_up[:, hidden_cols:],
        sum_down,
    )


def solution(mesh):
    placed = (
        P(("wide", "narrow"), None),
        P(("wide", "narrow"), None),
        P(),
        P(None, "narrow"),
        P(None, "narrow"),
        P(None, "narrow"),
        P("narrow", None),
        P(None, "narrow"),
        P(None, "narrow"),
        P(),
        P(None, "narrow"),
        P(None, "narrow"),
        P("narrow", None),
        P("wide", None),
        P("wide"),
        P("wide", None),
        P("wide", None),
    )
    return jax.shard_map(
        on_device,
        mesh=mesh,
        in_specs=placed,
        out_specs=(
            P(("wide", "narrow"), None),
            P(("wide", "narrow"), None),
            P(("wide", "narrow")),
            P("wide", "narrow"),
            P("wide", "narrow"),
            P("wide", "narrow"),
            P("narrow", "wide"),
            P("wide", "narrow"),
            P("wide", "narrow"),
            P(("wide", "narrow")),
            P("wide", "narrow"),
            P("wide", "narrow"),
            P("narrow", "wide"),
        ),
        check_vma=False,
    )
```

time: 3660 us -> 1020 us (0.28)
  matrix products: 1820 us -> 99.2 us
  local copies, waits for them, and re-layouts: 739 us -> 43.3 us
  waiting for transfers between devices: 830 us -> 624 us
  Pallas kernels: 0 us -> 126 us
  other arithmetic: 127 us -> 26.2 us
  loops' own time: 52.7 us -> 0 us
    dot_general x128 -> x8, matrix products: 1750 us -> 34.5 us  [the longest x4 30.7 us: dot(): return lax.dot_general(a, b, dims, preferred_element_type=f32)]
    transpose x16 -> x0, local copies, waits for them, and re-layouts: 285 us -> none  [bucket_bias(): jnp.transpose(pieces, (1, 0, 2, 3))]
    reduce_scatter x8, waiting for transfers between devices: 535 us -> 328 us  [the longest x4 243 us: scatter_narrow(): lax.psum_scatter(array.astype(bf16), 'narrow', scatter_dimension=0, tiled...]
    dynamic_slice x80 -> x0, local copies, waits for them, and re-layouts: 132 us -> none  [the longest x16 70.3 us: attention_forward(): mixed, log_total = lax.map(one_block, (row_blocks(query, block),) + inputs)]
    pallas_call x0 -> x2, Pallas kernels: none -> 126 us  [the longest x1 69.7 us: attention_backward(): pl.pallas_call(functools.partial(backward_kernel, width=width, heads=head...]
    another operation x20 -> x2, local copies, waits for them, and re-layouts: 109 us -> 0.59 us  [bias_words(): both = jnp.stack([pack(rel_table), pack(layout_table)], axis=1)]
    while x167 -> x0, local copies, waits for them, and re-layouts: 92.7 us -> none
    eq x64 -> x0, local copies, waits for them, and re-layouts: 83.6 us -> none  [one_piece(): bucket_ids[None] == labels[:, None, None]]
  transfers between devices with their start and end apart: 12 -> 12, of which waited for: 10 -> 10; matrix products, arithmetic and copies ran while one was open for 52% -> 11% of each run, Pallas kernels for 0% -> 7%
where the time goes in v1:
time: 1020 us; the launch traced here: 1010 us
  waiting for transfers between devices  624 us (61%)
  Pallas kernels  126 us (12%)
  matrix products  99.2 us (10%)
  blocking collectives  79.3 us (8%)
  local copies, waits for them, and re-layouts  43.3 us (4%)
  other arithmetic  26.2 us (3%)
  between operations  16 us (2%)
    reduce_scatter x4, waiting for transfers between devices, scatter_narrow(): lax.psum_scatter(array.astype(bf16), 'narrow', scatter_dimension=0, tiled...  243 us
    reduce_scatter x4, waiting for transfers between devices, over_wide(): return lax.psum_scatter(array, 'wide', scatter_dimension=dim, tiled=True)  85 us
    all_gather x1, waiting for transfers between devices, on_device(): normed_attn_all = lax.all_gather(normed_attn, 'narrow', axis=0, tiled=True)  80.1 us
    unnamed x2, blocking collectives  79.3 us
    all_gather x1, waiting for transfers between devices, on_device(): normed_ffn_all = lax.all_gather(normed_ffn, 'narrow', axis=0, tiled=True)  76.6 us
    pallas_call x1, Pallas kernels, attention_backward(): pl.pallas_call(functools.partial(backward_kernel, width=width, heads=head...  69.7 us
    all_gather x1, waiting for transfers between devices, on_device(): grad_all = lax.all_gather(out_grad, 'narrow', axis=0, tiled=True)  69.4 us
    all_gather x1, waiting for transfers between devices, on_device(): lax.all_gather(d_middle.astype(bf16), 'narrow', axis=0, tiled=True)  69.1 us
  transfers between devices with their start and end apart: 12, of which 10 were waited for; matrix products, arithmetic and copies ran while one was open for 11% of the time, Pallas kernels for 7%

profile of v1, /device:TPU:0, one launch (start us, length us, event | category | flops | bytes accessed | tf_op | source)
XLA Modules:
  0.0 1015.0 jit_solution(6375769103610516322)
XLA Ops:
  16.3 80.1 %all-gather.5.cloned.1.call-done = bf16[2048,1024]{1,0:T(8,128)(2,1)} async-done(((bf16[512,1024]{1,0:T(8,128)(2,1)}), bf16[2048,1024]{1,0:T(8,128)(2,1)}) %all-gather.5.cloned.1.call-update) | async-done | bytes 4194320 | tf_op jit(solution)/shard_map/all_gather | solution.py:422
  96.4 7.8 convolution_convert_fusion.4.q_ref.k_ref.v_ref
  104.2 56.2 %attention_forward.1 = (bf16[2048,256]{1,0:T(8,128)(2,1)}, f32[2048,256]{1,0:T(8,128)}, bf16[4,2048,2048]{2,1,0:T(8,128)(2,1)}, s16[2048,2048]{1,0:T(8,128)(2,1)}) custom-call(s32[1,4]{1,0:T(1,128)} %len_ref.3, bf16[2048,768]{1,0:T(8,128)(2,1)} %convolution_convert_fusion.4.q_ref.k_ref.v_ref, bf16[2048,768]{1,0:T(8,128)(2,1)} %convolution_convert_fusion.4.q_ref.k_ref.v_ref, ...), custom_call_target="tpu_custom_call" | custom-call | tf_op jit(solution)/shard_map/attention_forward/pallas_call | solution.py:132
  160.4 4.6 convolution_convert_fusion.2
  165.6 89.2 %reduce-scatter.11.cloned.1.call-done = bf16[512,1024]{1,0:T(8,128)(2,1)} async-done(((bf16[2048,1024]{1,0:T(8,128)(2,1)}), bf16[512,1024]{1,0:T(8,128)(2,1)}) %reduce-scatter.11.cloned.1.call-update) | async-done | bytes 1048592 | tf_op jit(solution)/shard_map/reduce_scatter | solution.py:389
  256.4 2.6 multiply_convert_fusion.2
  259.9 2.7 constant_dynamic-update-slice_fusion.4
  263.9 76.6 %all-gather.7.cloned.1.call-done = bf16[2048,1024]{1,0:T(8,128)(2,1)} async-done(((bf16[512,1024]{1,0:T(8,128)(2,1)}), bf16[2048,1024]{1,0:T(8,128)(2,1)}) %all-gather.7.cloned.1.call-update) | async-done | bytes 4194320 | tf_op jit(solution)/shard_map/all_gather | solution.py:428
  340.5 11.5 %fusion.78 = f32[2048,1408]{0,1:T(8,128)} fusion(bf16[2048,1024]{1,0:T(8,128)(2,1)} %all-gather.7.cloned.1.call-done, bf16[1024,1408]{0,1:T(8,128)(2,1)} %constant_dynamic-update-slice_fusion.3), kind=kOutput, calls=%fused_computation.131 | convolution fusion | flops 5905580032 | bytes 18612224 | tf_op jit(solution)/shard_map/dot_general | solution.py:19
  351.9 69.4 %all-gather.9.cloned.1.call-done = bf16[2048,1024]{1,0:T(8,128)(2,1)} async-done(((bf16[512,1024]{1,0:T(8,128)(2,1)}), bf16[2048,1024]{1,0:T(8,128)(2,1)}) %all-gather.9.cloned.1.call-update) | async-done | bytes 4194320 | tf_op jit(solution)/shard_map/all_gather | solution.py:419
  421.3 12.4 %fusion.6 = (bf16[2048,704]{0,1:T(8,128)(2,1)S(1)}, bf16[2048,704]{0,1:T(8,128)(2,1)S(1)}, bf16[2048,704]{0,1:T(8,128)(2,1)}) fusion(f32[2048,1408]{0,1:T(8,128)} %fusion.78, bf16[2048,1024]{1,0:T(8,128)(2,1)} %all-gather.9.cloned.1.call-done, bf16[704,1024]{1,0:T(8,128)(2,1)S(1)} %copy-done), kind=kOutput, calls=%fused_computation.8 | convolution fusion | flops 2990276608 | bytes 25821184 | tf_op jit(solution)/shard_map/dot_general | solution.py:366
  436.2 10.2 %convolution_convert_fusion = bf16[2048,1024]{1,0:T(8,128)(2,1)} fusion(bf16[1024,1408]{0,1:T(8,128)(2,1)} %constant_dynamic-update-slice_fusion.3, bf16[2048,704]{0,1:T(8,128)(2,1)S(1)} %get-tuple-element.92, bf16[2048,704]{0,1:T(8,128)(2,1)S(1)} %get-tuple-element.91), kind=kOutput, calls=%fused_computation.19 | convolution fusion | flops 5919211520 | bytes 12845056 | tf_op jit(solution)/shard_map/dot_general | solution.py:366
  446.4 75.4 %reduce-scatter.15.cloned.1.call-done = bf16[512,1024]{1,0:T(8,128)(2,1)} async-done(((bf16[2048,1024]{1,0:T(8,128)(2,1)}), bf16[512,1024]{1,0:T(8,128)(2,1)}) %reduce-scatter.15.cloned.1.call-update) | async-done | bytes 1048592 | tf_op jit(solution)/shard_map/reduce_scatter | solution.py:389
  521.8 2.8 fusion.17
  527.1 11.8 %fusion.7 = f32[1024,1408]{1,0:T(8,128)} fusion(bf16[2048,1024]{1,0:T(8,128)(2,1)} %all-gather.7.cloned.1.call-done, bf16[2048,704]{0,1:T(8,128)(2,1)} %copy-done.24, bf16[2048,704]{0,1:T(8,128)(2,1)} %copy-done.23), kind=kOutput, calls=%fused_computation.23 | convolution fusion | flops 5917114368 | bytes 15728640 | tf_op jit(solution)/shard_map/dot_general | solution.py:360
  539.4 69.1 %all-gather.11.cloned.1.call-done = bf16[2048,1024]{1,0:T(8,128)(2,1)} async-done(((bf16[512,1024]{1,0:T(8,128)(2,1)}), bf16[2048,1024]{1,0:T(8,128)(2,1)}) %all-gather.11.cloned.1.call-update) | async-done | bytes 4194320 | tf_op jit(solution)/shard_map/all_gather | solution.py:442
  608.5 4.6 convolution_convert_fusion.5.da_ref
  613.1 69.7 %attention_backward.1 = (bf16[2048,256]{1,0:T(8,128)(2,1)}, bf16[2048,256]{1,0:T(8,128)(2,1)}, bf16[2048,256]{1,0:T(8,128)(2,1)}, f32[256,256]{1,0:T(8,128)}, f32[256,128]{1,0:T(8,128)}) custom-call(s32[1,4]{1,0:T(1,128)} %len_ref.3, bf16[2048,768]{1,0:T(8,128)(2,1)} %convolution_convert_fusion.4.q_ref.k_ref.v_ref, ...), custom_call_target="tpu_custom_call" | custom-call | tf_op jit(solution)/shard_map/attention_backward/pallas_call | solution.py:292
  687.7 5.4 fusion.79
  693.2 7.8 convolution_convert_fusion.3
  701.2 6.9 convolution_convert_fusion.1
  708.2 7.8 fusion.81
  724.6 2.8 reshape.93
  736.8 4.8 fusion.80
  748.6 33.5 %all-reduce.7 = (f32[32,4]{0,1:T(4,128)}, f32[64,4]{0,1:T(4,128)}) all-reduce(f32[32,4]{0,1:T(4,128)} %div.34, f32[64,4]{0,1:T(4,128)} %div.37), channel_id=9, replica_groups=mesh['wide'=8,'narrow'=4] {'wide'}, use_global_device_ids=true, to_apply=%region_13.14.clone | all-reduce | flops 384 | bytes 3072
  787.8 50.1 %reduce-scatter.17.cloned.1.call-done = bf16[512,1024]{1,0:T(8,128)(2,1)} async-done(((bf16[2048,1024]{1,0:T(8,128)(2,1)}), bf16[512,1024]{1,0:T(8,128)(2,1)}) %reduce-scatter.17.cloned.1.call-update) | async-done | bytes 1048592 | tf_op jit(solution)/shard_map/reduce_scatter | solution.py:389
  838.0 2.7 fusion.24
  840.7 45.8 %all-reduce.6 = (f32[1024]{0:T(1024)}, f32[1024]{0:T(1024)}) all-reduce(f32[1024]{0:T(1024)} %get-tuple-element.85, f32[1024]{0:T(1024)} %get-tuple-element.83), channel_id=6, replica_groups=mesh['wide'=8,'narrow'=4] {'wide','narrow'}, use_global_device_ids=true, to_apply=%region_9.10.clone | all-reduce | flops 2048 | bytes 16384
  890.2 28.4 %reduce-scatter.13.cloned.1.call-done = bf16[512,1024]{1,0:T(8,128)(2,1)} async-done(((bf16[2048,1024]{1,0:T(8,128)(2,1)}), bf16[512,1024]{1,0:T(8,128)(2,1)}) %reduce-scatter.13.cloned.1.call-update) | async-done | bytes 1048592 | tf_op jit(solution)/shard_map/reduce_scatter | solution.py:389
  918.6 4.4 fusion.12
  923.0 45.0 %reduce-scatter.25.cloned.1.call-done = f32[704,128]{1,0:T(8,128)} async-done(((f32[704,1024]{1,0:T(8,128)}), f32[704,128]{1,0:T(8,128)}) %reduce-scatter.25.cloned.1.call-update) | async-done | bytes 360464 | tf_op jit(solution)/shard_map/reduce_scatter | solution.py:456
  967.9 40.0 %reduce-scatter.21.cloned.1.call-done = f32[256,128]{1,0:T(8,128)} async-done(((f32[256,1024]{1,0:T(8,128)}), f32[256,128]{1,0:T(8,128)}) %reduce-scatter.21.cloned.1.call-update) | async-done | bytes 131088 | tf_op jit(solution)/shard_map/reduce_scatter | solution.py:456
  (129 shorter events, 57.2 us)
Async XLA Ops:
  7.2 414.1 %copy-start = (bf16[704,1024]{1,0:T(8,128)(2,1)S(1)}, bf16[704,1024]{1,0:T(8,128)(2,1)}, u32[]{:S(2)}) copy-start(bf16[704,1024]{1,0:T(8,128)(2,1)} %param.29) | copy-start | bytes 4325380
  7.2 5.6 copy-start.19
  7.2 5.7 copy-start.20
  7.2 6.4 copy-start.8
  7.2 7.3 copy-start.9
  7.2 89.1 %all-gather.5.cloned.1.call-start = ((), (), s32[]{:S(2)}) async-start(), calls=%async_computation.8 | async-start | bytes 5242880 | tf_op jit(solution)/shard_map/all_gather | solution.py:422
  8.9 6.4 copy-start.10
  9.5 6.7 copy-start.14
  12.8 242.0 %reduce-scatter.11.cloned.1.call-start = ((), (), s32[]{:S(2)}) async-start(), calls=%async_computation.9 | async-start | bytes 5242880 | tf_op jit(solution)/shard_map/reduce_scatter | solution.py:389
  104.2 56.2 %copy-start.7 = (bf16[256,1024]{1,0:T(8,128)(2,1)S(1)}, bf16[256,1024]{1,0:T(8,128)(2,1)}, u32[]{:S(2)}) copy-start(bf16[256,1024]{1,0:T(8,128)(2,1)} %param.23) | copy-start | bytes 1572868
  164.9 89.9 %copy-start.1 = (bf16[512,1024]{1,0:T(8,128)(2,1)S(1)}, bf16[512,1024]{1,0:T(8,128)(2,1)}, u32[]{:S(2)}) copy-start(bf16[512,1024]{1,0:T(8,128)(2,1)} %param.17) | copy-start | bytes 3145732
  164.9 175.6 %all-gather.7.cloned.1.call-start = ((), (), s32[]{:S(2)}) async-start(), calls=%async_computation.10 | async-start | bytes 5242880 | tf_op jit(solution)/shard_map/all_gather | solution.py:428
  256.4 268.2 %copy-start.12 = (f32[512]{0:T(512)}, f32[512]{0:T(512)S(1)}, u32[]{:S(2)}) copy-start(f32[512]{0:T(512)S(1)} %get-tuple-element.104) | copy-start | bytes 6148
  256.4 268.2 %copy-start.16 = (f32[512]{0:T(512)}, f32[512]{0:T(512)S(1)}, u32[]{:S(2)}) copy-start(f32[512]{0:T(512)S(1)} %get-tuple-element.103) | copy-start | bytes 6148
  259.1 162.3 %all-gather.9.cloned.1.call-start = ((), (), s32[]{:S(2)}) async-start(), calls=%async_computation.12 | async-start | bytes 5242880 | tf_op jit(solution)/shard_map/all_gather | solution.py:419
  259.6 262.2 %reduce-scatter.15.cloned.1.call-start = ((), (), s32[]{:S(2)}) async-start(), calls=%async_computation.13 | async-start | bytes 5242880 | tf_op jit(solution)/shard_map/reduce_scatter | solution.py:389
  259.9 2.7 copy-start.5
  433.7 2.4 copy-start.24
  446.3 75.5 %copy-start.2 = (bf16[512,1024]{1,0:T(8,128)(2,1)S(1)}, bf16[512,1024]{1,0:T(8,128)(2,1)}, u32[]{:S(2)}) copy-start(bf16[512,1024]{1,0:T(8,128)(2,1)} %reduce-scatter.11.cloned.1.call-done) | copy-start | bytes 3145732
  446.4 162.1 %all-gather.11.cloned.1.call-start = ((), (), s32[]{:S(2)}) async-start(), calls=%async_computation.14 | async-start | bytes 5242880 | tf_op jit(solution)/shard_map/all_gather | solution.py:442
  521.8 3.4 copy-start.3
  521.8 3.4 copy-start.4
  527.1 191.5 %reduce-scatter.23.cloned.1.call-start = ((), (), s32[]{:S(2)}) async-start(), calls=%async_computation.18 | async-start | bytes 6488064 | tf_op jit(solution)/shard_map/reduce_scatter | solution.py:456
  539.0 247.1 %reduce-scatter.19.cloned.1.call-start = ((), (), s32[]{:S(2)}) async-start(), calls=%async_computation.16 | async-start | bytes 3538944 | tf_op jit(solution)/shard_map/reduce_scatter | solution.py:456
  682.8 3.2 copy-start.6
  682.8 4.9 copy-start.21
  693.1 144.9 %reduce-scatter.17.cloned.1.call-start = ((), (), s32[]{:S(2)}) async-start(), calls=%async_computation.15 | async-start | bytes 5242880 | tf_op jit(solution)/shard_map/reduce_scatter | solution.py:389
  701.0 217.7 %reduce-scatter.13.cloned.1.call-start = ((), (), s32[]{:S(2)}) async-start(), calls=%async_computation.11 | async-start | bytes 5242880 | tf_op jit(solution)/shard_map/reduce_scatter | solution.py:389
  708.1 259.8 %reduce-scatter.25.cloned.1.call-start = ((), (), s32[]{:S(2)}) async-start(), calls=%async_computation.19 | async-start | bytes 3244032 | tf_op jit(solution)/shard_map/reduce_scatter | solution.py:456
  716.0 291.9 %reduce-scatter.21.cloned.1.call-start = ((), (), s32[]{:S(2)}) async-start(), calls=%async_computation.17 | async-start | bytes 1179648 | tf_op jit(solution)/shard_map/reduce_scatter | solution.py:456
  736.7 101.3 %copy-start.15 = (f32[512]{0:T(512)S(1)}, f32[512]{0:T(512)}, u32[]{:S(2)}) copy-start(f32[512]{0:T(512)} %copy-done.14) | copy-start | bytes 6148
  741.5 177.1 %copy-start.13 = (f32[512]{0:T(512)S(1)}, f32[512]{0:T(512)}, u32[]{:S(2)}) copy-start(f32[512]{0:T(512)} %copy-done.12) | copy-start | bytes 6148
  (5 other events, 5.2 us)
Sparse Core Ops, SparseCore 0:
  12.9 83.4 all-gather.4
  165.1 89.6 reduce-scatter.10
  259.2 81.2 all-gather.6
  342.0 79.2 all-gather.8
  446.5 75.2 reduce-scatter.14
  527.2 81.2 all-gather.10
  611.9 57.5 reduce-scatter.22
  693.2 65.6 reduce-scatter.18
  761.2 76.7 reduce-scatter.16
  840.2 78.3 reduce-scatter.12
  922.6 45.3 reduce-scatter.24
  971.9 36.0 reduce-scatter.20

commit v2 on v1

--- a/solution.py
+++ b/solution.py
@@ -161,6 +161,8 @@
             pltpu.VMEM((8, count), jnp.int32),
         ],
         compiler_params=pltpu.CompilerParams(vmem_limit_bytes=56 << 20),
+        cost_estimate=pl.CostEstimate(
+            flops=heads * count * count * 256, bytes_accessed=180 << 20, transcendentals=heads * count * count // 2),
         name="attention_forward",
     )(page_lengths, proj, proj, proj, rel, lay, tab, kmask.reshape(1, count))
 
@@ -331,6 +333,8 @@
             pltpu.VMEM((128, deep), bf16),
         ],
         compiler_params=pltpu.CompilerParams(vmem_limit_bytes=56 << 20),
+        cost_estimate=pl.CostEstimate(
+            flops=heads * count * count * 768, bytes_accessed=220 << 20, transcendentals=0),
         name="attention_backward",
     )(page_lengths, proj, proj, proj, e, code, d_att, att, rinv)
 
@@ -353,6 +357,39 @@
     return out.reshape(4 * right, heads) / (4 * right)
 
 
+def weight_grads_kernel(n_pair, *refs):
+    x_ref, g_ref, m_ref = refs[:3]
+    gate_ups = refs[3:3 + n_pair]
+    hiddens = refs[3 + n_pair:3 + 2 * n_pair]
+    att_ref, out_ref = refs[3 + 2 * n_pair:]
+    rows_in = (((0,), (0,)), ((), ()))
+    place = 0
+    for left, rights in ((x_ref, gate_ups), (m_ref, (att_ref,)), (g_ref, hiddens)):
+        for right in rights:
+            size = right.shape[1]
+            out_ref[:, place:place + size] = dot(left[...], right[...], rows_in).astype(bf16)
+            place += size
+
+
+def weight_grads(normed_pair, grad_pair, d_middle_low, gate_ups, hiddens, attended_own, tile=256):
+    features = normed_pair.shape[1]
+    rights = list(gate_ups) + list(hiddens) + [attended_own]
+    columns = sum(r.shape[1] for r in rights)
+    left = lambda a: pl.BlockSpec((a.shape[0], tile), lambda i: (0, i))
+    whole = lambda a: pl.BlockSpec(a.shape, lambda i: (0, 0))
+    return pl.pallas_call(
+        functools.partial(weight_grads_kernel, len(gate_ups)),
+        grid=(features // tile,),
+        in_specs=[left(normed_pair), left(grad_pair), left(d_middle_low)] + [whole(r) for r in rights],
+        out_specs=pl.BlockSpec((tile, columns), lambda i: (i, 0)),
+        out_shape=jax.ShapeDtypeStruct((features, columns), bf16),
+        compiler_params=pltpu.CompilerParams(vmem_limit_bytes=56 << 20),
+        cost_estimate=pl.CostEstimate(
+            flops=2 * features * columns * normed_pair.shape[0], bytes_accessed=26 << 20, transcendentals=0),
+        name="weight_grads",
+    )(normed_pair, grad_pair, d_middle_low, *rights)
+
+
 epsilon = 1e-06
 
 
@@ -379,17 +416,25 @@
 
 def norm_back(d_normed, rows, scale, gain):
     shaped = d_normed * gain
-    gain_term = jnp.sum(d_normed * rows * scale, axis=0)
     cubed = scale * scale * scale
-    d_rows = scale * shaped - rows * cubed * jnp.mean(shaped * rows, axis=-1, keepdims=True)
-    return (d_rows, gain_term)
-
-
-def scatter_narrow(array):
-    return lax.psum_scatter(array.astype(bf16), "narrow", scatter_dimension=0, tiled=True).astype(f32)
+    return scale * shaped - rows * cubed * jnp.mean(shaped * rows, axis=-1, keepdims=True)
+
+
+def along(array, shift, ring):
+    return lax.ppermute(array, "narrow", [(i, (i + shift) % ring) for i in range(ring)])
+
+
+def swap(array, ring):
+    return lax.ppermute(array, "narrow", [(i, i ^ 1) for i in range(ring)])
+
+
+def rows_of(array, index, count):
+    return lax.dynamic_slice_in_dim(array, index * count, count, 0)
 
 
 def on_device(
+    wide,
+    ring,
     layer_input,
     out_grad,
     norm_attn_gain,
@@ -408,75 +453,154 @@
     rel_bucket,
     layout_bucket,
 ):
+    tokens, width = layer_input.shape
     head_cols = w_query.shape[1]
     heads = head_cols // DH
-    hidden_cols = w_gate.shape[1]
+    units = w_gate.shape[1]
+    part = width // wide
+    me = lax.axis_index("narrow")
+    my_wide = lax.axis_index("wide")
     gain_attn = norm_attn_gain.astype(f32)
     gain_ffn = norm_ffn_gain.astype(f32)
+    resid = layer_input.astype(f32)
+
+    scale_attn, normed_attn = norm_rows(resid, gain_attn)
+    normed_attn_all = lax.all_gather(normed_attn, "narrow", axis=0, tiled=True)
+
     w_project = jnp.concatenate([w_query, w_key, w_value], axis=1)
     w_gate_up = jnp.concatenate([w_gate, w_up], axis=1)
-    resid = layer_input.astype(f32)
-    grad_all = lax.all_gather(out_grad, "narrow", axis=0, tiled=True)
-
-    scale_attn, normed_attn = norm_rows(resid, gain_attn)
-    normed_attn_all = lax.all_gather(normed_attn, "narrow", axis=0, tiled=True)
+    own_rows_gate_up = rows_of(w_gate_up, my_wide, part)
+    own_rows_project = rows_of(w_project, my_wide, part)
+    down_piece = lax.dynamic_slice_in_dim(down_projection_weight, my_wide * part, part, 1).T
+    out_piece = lax.dynamic_slice_in_dim(w_out, my_wide * part, part, 1).T
+    ffn_piece = jnp.concatenate([own_rows_gate_up, down_piece], axis=1)
+    out_pieces = [out_piece] + [along(out_piece, d, ring) for d in range(1, ring)]
+    ffn_pieces = [along(ffn_piece, d, ring) for d in range(2, ring, 2)]
+    w_first = lax.all_gather(jnp.concatenate(out_pieces + ffn_pieces, axis=1), "wide", axis=0, tiled=True)
+    late_project, late_grad, normed_attn_all = lax.optimization_barrier(
+        (own_rows_project, out_grad, normed_attn_all))
+    project_pieces = [own_rows_project] + [along(late_project, d, ring) for d in range(1, ring)]
+    other_grad = swap(late_grad, ring)
+    out_t = w_first[:, : ring * head_cols]
+    shards = [(w_gate_up, down_projection_weight.T)]
+    for place in range(ring * head_cols, w_first.shape[1], 3 * units):
+        shards.append((w_first[:, place : place + 2 * units], w_first[:, place + 2 * units : place + 3 * units]))
+
     projected = dot(normed_attn_all, w_project).astype(bf16)
     attended, rinv, exps, codes = attention_forward(
         page_lengths, projected, rel_bucket, layout_bucket, bias_words(rel_table, layout_table), key_mask)
-    middle = resid + scatter_narrow(dot(attended, w_out))
+    attended, other_grad, project_pieces = lax.optimization_barrier((attended, other_grad, project_pieces))
+    w_project_all = lax.all_gather(jnp.concatenate(project_pieces, axis=1), "wide", axis=0, tiled=True)
+    grad_pair = jnp.concatenate([out_grad, other_grad], axis=0)
+    mine = [along(rows_of(attended, (me + d) % ring, tokens), d, ring) for d in range(1, ring)]
+    attended_own = jnp.concatenate([rows_of(attended, me, tokens)] + mine, axis=1)
+    middle = resid + contract_cols(attended_own, out_t)
+
     scale_ffn, normed_ffn = norm_rows(middle, gain_ffn)
-    normed_ffn_all = lax.all_gather(normed_ffn, "narrow", axis=0, tiled=True)
-    gate_up = dot(normed_ffn_all, w_gate_up)
-    hidden, pullback = jax.vjp(gated, gate_up[:, :hidden_cols], gate_up[:, hidden_cols:])
-    hidden = hidden.astype(bf16)
-    layer_out = (middle + scatter_narrow(dot(hidden, down_projection_weight))).astype(bf16)
-
-    grad_down = contract_rows(hidden, grad_all)
-    d_hidden = contract_cols(grad_all, down_projection_weight)
-    d_gate, d_up = pullback(d_hidden)
-    d_gate_up = jnp.concatenate([d_gate, d_up], axis=1).astype(bf16)
-    grad_gate_up = contract_rows(normed_ffn_all, d_gate_up)
-    d_normed_ffn = scatter_narrow(contract_cols(d_gate_up, w_gate_up))
-    d_middle_norm, gain_ffn_term = norm_back(d_normed_ffn, middle, scale_ffn, gain_ffn)
-    d_middle = out_grad.astype(f32) + d_middle_norm
-    d_middle_all = lax.all_gather(d_middle.astype(bf16), "narrow", axis=0, tiled=True)
-    grad_wout = contract_rows(attended, d_middle_all)
-    d_attended = contract_cols(d_middle_all, w_out).astype(bf16)
+    normed_pair = jnp.concatenate([normed_ffn, swap(normed_ffn, ring)], axis=0)
+    d_normed = 0.0
+    kept = []
+    for gate_up_weight, down_t in shards:
+        gate_up = dot(normed_pair, gate_up_weight)
+        hidden, pullback = jax.vjp(gated, gate_up[:, :units], gate_up[:, units:])
+        hidden = hidden.astype(bf16)
+        d_hidden = dot(grad_pair, down_t)
+        d_gate, d_up = pullback(d_hidden)
+        d_gate_up = jnp.concatenate([d_gate, d_up], axis=1).astype(bf16)
+        d_normed = d_normed + contract_cols(d_gate_up, gate_up_weight)
+        kept.append((hidden, d_gate_up))
+    own_d_normed, other_d_normed, hiddens = lax.optimization_barrier(
+        (d_normed[:tokens], d_normed[tokens:].astype(bf16), [k[0] for k in kept]))
+    other_d_normed = swap(other_d_normed, ring)
+    out_sum = 0.0
+    for hidden, (_, down_t) in zip(hiddens, shards):
+        out_sum = out_sum + contract_cols(hidden, down_t)
+    other_d_normed, other_out = lax.optimization_barrier((other_d_normed, out_sum[tokens:].astype(bf16)))
+    layer_out = (middle + out_sum[:tokens] + swap(other_out, ring).astype(f32)).astype(bf16)
+    d_normed_ffn = own_d_normed + other_d_normed.astype(f32)
+    d_middle = out_grad.astype(f32) + norm_back(d_normed_ffn, middle, scale_ffn, gain_ffn)
+    d_middle_low = d_middle.astype(bf16)
+    d_attended_own = dot(d_middle_low, out_t).astype(bf16)
+
+    def block(d):
+        return d_attended_own[:, d * head_cols : (d + 1) * head_cols]
+
+    d_attended = jnp.zeros((ring * tokens, head_cols), bf16)
+    d_attended = lax.dynamic_update_slice_in_dim(d_attended, block(0), me * tokens, 0)
+    for d in range(1, ring):
+        d_attended = lax.dynamic_update_slice_in_dim(
+            d_attended, along(block(d), -d, ring), ((me + d) % ring) * tokens, 0)
+
+    ffn_sums = weight_grads(
+        normed_pair, grad_pair, d_middle_low, [k[1] for k in kept], hiddens, attended_own)
+    ffn_sums, d_attended, w_project_all = lax.optimization_barrier((ffn_sums, d_attended, w_project_all))
+    ffn_sums = lax.psum_scatter(ffn_sums, "wide", scatter_dimension=0, tiled=True)
+
     d_query, d_keys, d_values, raw_lay, raw_rel = attention_backward(
         page_lengths, projected, exps, codes, d_attended, attended, rinv)
+    d_project = jnp.concatenate([d_query, d_keys, d_values], axis=1)
+    mine = [along(rows_of(d_project, (me + d) % ring, tokens), d, ring) for d in range(1, ring)]
+    d_project_own = jnp.concatenate([rows_of(d_project, me, tokens)] + mine, axis=1)
+    d_normed_attn = contract_cols(d_project_own, w_project_all)
+    in_grad = d_middle + norm_back(d_normed_attn, resid, scale_attn, gain_attn)
+
     grad_relative = bucket_sums(raw_rel, heads, True, 3)
     grad_layout = bucket_sums(raw_lay, heads, False, 4)
-    d_project = jnp.concatenate([d_query, d_keys, d_values], axis=1)
-    grad_project = contract_rows(normed_attn_all, d_project)
-    d_normed_attn = scatter_narrow(contract_cols(d_project, w_project))
-    d_resid, gain_attn_term = norm_back(d_normed_attn, resid, scale_attn, gain_attn)
-    in_grad = d_middle + d_resid
-
-    def over_wide(array, dim):
-        return lax.psum_scatter(array, "wide", scatter_dimension=dim, tiled=True)
-
-    sum_project = over_wide(grad_project, 0)
-    sum_wout = over_wide(grad_wout, 1)
-    sum_gate_up = over_wide(grad_gate_up, 0)
-    sum_down = over_wide(grad_down, 1)
-    sum_relative = over_wide(grad_relative, 0)
-    sum_layout = over_wide(grad_layout, 0)
-    sum_gain_attn = lax.psum_scatter(gain_attn_term, ("wide", "narrow"), scatter_dimension=0, tiled=True)
-    sum_gain_ffn = lax.psum_scatter(gain_ffn_term, ("wide", "narrow"), scatter_dimension=0, tiled=True)
+    tables = jnp.concatenate(
+        [grad_relative.reshape(wide, -1, heads), grad_layout.reshape(wide, -1, heads)], axis=1)
+    n_rel = grad_relative.shape[0] // wide
+    n_both = tables.shape[1]
+    tables = jnp.pad(tables, ((0, 0), (0, part - n_both), (0, 128 - heads))).reshape(width, 128)
+    last_sums = jnp.concatenate([contract_rows(normed_attn_all, d_project), tables], axis=1)
+    last_sums, ffn_sums = lax.optimization_barrier((last_sums.astype(bf16), ffn_sums))
+    last_sums = lax.psum_scatter(last_sums, "wide", scatter_dimension=0, tiled=True).astype(f32)
+    n_shards = len(kept)
+    first = 2 * units * n_shards
+    second = first + ring * head_cols
+    sum_gate_up = ffn_sums[:, : 2 * units].astype(f32)
+    sum_down = ffn_sums[:, second : second + units].astype(f32)
+    for n in range(1, n_shards):
+        sum_gate_up += along(ffn_sums[:, 2 * units * n : 2 * units * (n + 1)], -2 * n, ring).astype(f32)
+        sum_down += along(ffn_sums[:, second + units * n : second + units * (n + 1)], -2 * n, ring).astype(f32)
+    sum_wout = ffn_sums[:, first : first + head_cols].astype(f32)
+    for d in range(1, ring):
+        place = first + d * head_cols
+        sum_wout += along(ffn_sums[:, place : place + head_cols], -d, ring).astype(f32)
+
+    sum_project = last_sums[:, : 3 * head_cols]
+    sum_tables = last_sums[:n_both, 3 * head_cols : 3 * head_cols + heads]
+
+    gain_terms = jnp.stack(
+        [
+            jnp.sum(own_rows_project.astype(f32) * sum_project, axis=1),
+            jnp.sum(own_rows_gate_up.astype(f32) * sum_gate_up, axis=1),
+        ]
+    )
+    share = part // ring
+
+    def gain_share(index):
+        return lax.dynamic_slice_in_dim(gain_terms, index * share, share, 1)
+
+    gain_sum = gain_share(me)
+    for d in range(1, ring):
+        gain_sum = gain_sum + along(gain_share((me + d) % ring), d, ring)
+    place = my_wide * part + me * share
+    gains = lax.dynamic_slice_in_dim(jnp.stack([gain_attn, gain_ffn]), place, share, 1)
+    gain_grads = gain_sum / gains
     return (
         layer_out,
         in_grad,
-        sum_gain_attn,
+        gain_grads[0],
         sum_project[:, :head_cols],
         sum_project[:, head_cols : 2 * head_cols],
         sum_project[:, 2 * head_cols :],
-        sum_wout,
-        sum_relative,
-        sum_layout,
-        sum_gain_ffn,
-        sum_gate_up[:, :hidden_cols],
-        sum_gate_up[:, hidden_cols:],
-        sum_down,
+        sum_wout.T,
+        sum_tables[:n_rel],
+        sum_tables[n_rel:],
+        gain_grads[1],
+        sum_gate_up[:, :units],
+        sum_gate_up[:, units:],
+        sum_down.T,
     )
 
 
@@ -501,7 +625,7 @@
         P("wide", None),
     )
     return jax.shard_map(
-        on_device,
+        functools.partial(on_device, mesh.shape["wide"], mesh.shape["narrow"]),
         mesh=mesh,
         in_specs=placed,
         out_specs=(

time: 1020 us -> 598 us (0.59)
  the two profiles are of different devices: /device:TPU:0 before, /device:TPU:6 now
where the time goes in v2:
time: 598 us; the launch traced here: 595 us
  waiting for transfers between devices  245 us (41%)
  Pallas kernels  170 us (28%)
  matrix products  61.4 us (10%)
  local copies, waits for them, and re-layouts  42.7 us (7%)
  starting transfers between devices  36.5 us (6%)
  other arithmetic  24.7 us (4%)
  between operations  15.2 us (3%)
    ppermute x24, waiting for transfers between devices, along(): lax.ppermute(array, 'narrow', [(i, (i + shift) % ring) for i in range(rin...  161 us
    pallas_call x1, Pallas kernels, attention_backward(): pl.pallas_call(functools.partial(backward_kernel, width=width, heads=head...  84.8 us
    pallas_call x1, Pallas kernels, attention_forward(): pl.pallas_call(functools.partial(forward_kernel, width=width, heads=heads...  66.9 us
    ppermute x4, waiting for transfers between devices, swap(): return lax.ppermute(array, 'narrow', [(i, i ^ 1) for i in range(ring)])  61.7 us
    ppermute x24, starting transfers between devices, along(): lax.ppermute(array, 'narrow', [(i, (i + shift) % ring) for i in range(rin...  33.5 us
    dot_general x6, matrix products, dot(): return lax.dot_general(a, b, dims, preferred_element_type=f32)  32.9 us
    unnamed x117, local copies, waits for them, and re-layouts  30.7 us
    all_gather x1, waiting for transfers between devices, on_device(): normed_attn_all = lax.all_gather(normed_attn, 'narrow', axis=0, tiled=True)  22.1 us
  transfers between devices with their start and end apart: 33, of which 14 were waited for; matrix products, arithmetic and copies ran while one was open for 18% of the time, Pallas kernels for 29%

profile of v2, /device:TPU:6, one launch (start us, length us, event | category | flops | bytes accessed | tf_op | source)
XLA Modules:
  0.0 595.3 jit_solution(3830599767339122504)
XLA Ops:
  15.2 3.1 copy.102
  28.1 22.5 %collective-permute-done.7 = bf16[128,256]{0,1:T(8,128)(2,1)S(1)} collective-permute-done((bf16[128,256]{0,1:T(8,128)(2,1)S(1)}, bf16[128,256]{0,1:T(8,128)(2,1)S(1)}, u32[]{:S(2)}, u32[]{:S(2)}) %collective-permute-start.7) | collective-permute-done | bytes 65568 | tf_op jit(solution)/shard_map/ppermute | solution.py:424
  50.6 36.9 %collective-permute-done.8 = bf16[128,256]{0,1:T(8,128)(2,1)S(1)} collective-permute-done((bf16[128,256]{0,1:T(8,128)(2,1)S(1)}, bf16[128,256]{0,1:T(8,128)(2,1)S(1)}, u32[]{:S(2)}, u32[]{:S(2)}) %collective-permute-start.8) | collective-permute-done | bytes 65568 | tf_op jit(solution)/shard_map/ppermute | solution.py:424
  98.3 22.1 %all-gather.4.cloned.1.call-done = bf16[2048,1024]{1,0:T(8,128)(2,1)} async-done(((bf16[512,1024]{1,0:T(8,128)(2,1)}), bf16[2048,1024]{1,0:T(8,128)(2,1)}) %all-gather.4.cloned.1.call-update) | async-done | bytes 4194320 | tf_op jit(solution)/shard_map/all_gather | solution.py:468
  120.9 3.6 collective-permute-start.2
  126.5 7.4 %convolution_convert_fusion.q_ref.k_ref.v_ref = bf16[2048,768]{1,0:T(8,128)(2,1)} fusion(bf16[2048,1024]{1,0:T(8,128)(2,1)} %all-gather.4.cloned.1.call-done, bf16[1024,256]{0,1:T(8,128)(2,1)S(1)} %copy.99, bf16[1024,256]{0,1:T(8,128)(2,1)S(1)} %copy.98, bf16[1024,256]{0,1:T(8,128)(2,1)} %copy.97), kind=kOutput, calls=%fused_computation.9 | convolution fusion | flops 3227516928 | bytes 8912896 | tf_op jit(solution)/shard_map/dot_general | solution.py:19
  134.0 66.9 %attention_forward.1 = (bf16[2048,256]{1,0:T(8,128)(2,1)}, f32[2048,256]{1,0:T(8,128)}, bf16[4,2048,2048]{2,1,0:T(8,128)(2,1)}, s16[2048,2048]{1,0:T(8,128)(2,1)}) custom-call(s32[1,4]{1,0:T(1,128)} %len_ref.3, bf16[2048,768]{1,0:T(8,128)(2,1)} %convolution_convert_fusion.q_ref.k_ref.v_ref, bf16[2048,768]{1,0:T(8,128)(2,1)} %convolution_convert_fusion.q_ref.k_ref.v_ref, ...), custom_call_target="tpu_custom_call" | custom-call | flops 4294967296 | bytes 188743680 | tf_op jit(solution)/shard_map/attention_forward/pallas_call | solution.py:132
  206.3 6.3 %collective-permute-done.6 = bf16[512,256]{1,0:T(8,128)(2,1)S(1)} collective-permute-done((bf16[512,256]{1,0:T(8,128)(2,1)S(1)}, bf16[512,256]{1,0:T(8,128)(2,1)S(1)}, u32[]{:S(2)}, u32[]{:S(2)}) %collective-permute-start.6) | collective-permute-done | bytes 262176 | tf_op jit(solution)/shard_map/ppermute | solution.py:424
  212.6 15.9 %collective-permute-done.5 = bf16[512,256]{1,0:T(8,128)(2,1)S(1)} collective-permute-done((bf16[512,256]{1,0:T(8,128)(2,1)S(1)}, bf16[512,256]{1,0:T(8,128)(2,1)S(1)}, u32[]{:S(2)}, u32[]{:S(2)}) %collective-permute-start.5) | collective-permute-done | bytes 262176 | tf_op jit(solution)/shard_map/ppermute | solution.py:424
  229.2 3.5 multiply_reduce_fusion.2
  238.3 22.0 %collective-permute-done.11 = bf16[512,1024]{1,0:T(8,128)(2,1)} collective-permute-done((bf16[512,1024]{1,0:T(8,128)(2,1)}, bf16[512,1024]{1,0:T(8,128)(2,1)}, u32[]{:S(2)}, u32[]{:S(2)}) %collective-permute-start.11) | collective-permute-done | bytes 1048608 | tf_op jit(solution)/shard_map/ppermute | solution.py:428
  260.4 5.7 fusion.42
  266.1 4.1 fusion.6
  271.2 7.8 %fusion.24 = f32[1024,1408]{1,0:T(8,128)} fusion(bf16[1024,3136]{0,1:T(8,128)(2,1)S(1)} %bitcast.71, bf16[512,1024]{1,0:T(8,128)(2,1)} %collective-permute-done.11, bf16[512,1024]{1,0:T(8,128)(2,1)} %multiply_convert_fusion.4), kind=kOutput, calls=%fused_computation.45 | convolution fusion | flops 2956984320 | bytes 10747904 | tf_op jit(solution)/shard_map/dot_general | solution.py:19
  279.0 6.4 %fusion.13 = (bf16[1024,704]{1,0:T(8,128)(2,1)S(1)}, bf16[1024,704]{1,0:T(8,128)(2,1)S(1)}, bf16[1024,704]{1,0:T(8,128)(2,1)S(1)}) fusion(f32[1024,1408]{1,0:T(8,128)} %fusion.24, bf16[1024,1024]{1,0:T(8,128)(2,1)S(1)} %constant_dynamic-update-slice_fusion.5.refs_1_, bf16[1024,3136]{0,1:T(8,128)(2,1)S(1)} %bitcast.71), kind=kOutput, calls=%fused_computation.26 | convolution fusion | flops 1495138304 | bytes 13631488 | tf_op jit(solution)/shard_map/dot_general | solution.py:19
  286.4 3.5 fusion.43
  289.8 3.4 fusion.35
  297.5 21.3 %collective-permute-done.12 = bf16[512,1024]{1,0:T(8,128)(2,1)S(1)} collective-permute-done((bf16[512,1024]{1,0:T(8,128)(2,1)S(1)}, bf16[512,1024]{1,0:T(8,128)(2,1)S(1)}, u32[]{:S(2)}, u32[]{:S(2)}) %collective-permute-start.12) | collective-permute-done | bytes 1048608 | tf_op jit(solution)/shard_map/ppermute | solution.py:428
  321.2 3.1 pad_maximum_fusion.3.refs_0_
  324.8 18.3 %collective-permute-done.13 = bf16[512,1024]{1,0:T(8,128)(2,1)S(1)} collective-permute-done((bf16[512,1024]{1,0:T(8,128)(2,1)S(1)}, bf16[512,1024]{1,0:T(8,128)(2,1)S(1)}, u32[]{:S(2)}, u32[]{:S(2)}) %collective-permute-start.13) | collective-permute-done | bytes 1048608 | tf_op jit(solution)/shard_map/ppermute | solution.py:428
  343.1 2.7 fusion.118
  349.3 18.2 %weight_grads.1 = bf16[1024,5248]{1,0:T(8,128)(2,1)} custom-call(bf16[1024,1024]{1,0:T(8,128)(2,1)} %pad_maximum_fusion.3.refs_0_, bf16[1024,1024]{1,0:T(8,128)(2,1)} %copy-done.24, bf16[512,1024]{1,0:T(8,128)(2,1)} %copy-done.17, bf16[1024,1408]{1,0:T(8,128)(2,1)} %copy-done.13, bf16[1024,1408]{1,0:T(8,128)(2,1)} %copy-done.14, ...), custom_call_target="tpu_custom_call" | custom-call | flops 11005853696 | bytes 27262976 | tf_op jit(solution)/shard_map/weight_grads/pallas_call | solution.py:380
  367.6 3.4 collective-permute-done.15
  372.0 84.8 %attention_backward.1 = (bf16[2048,256]{1,0:T(8,128)(2,1)}, bf16[2048,256]{1,0:T(8,128)(2,1)}, bf16[2048,256]{1,0:T(8,128)(2,1)}, f32[256,256]{1,0:T(8,128)}, f32[256,128]{1,0:T(8,128)}) custom-call(s32[1,4]{1,0:T(1,128)} %len_ref.3, bf16[2048,768]{1,0:T(8,128)(2,1)} %convolution_convert_fusion.q_ref.k_ref.v_ref, ...), custom_call_target="tpu_custom_call" | custom-call | flops 12884901888 | bytes 230686720 | tf_op jit(solution)/shard_map/attention_backward/pallas_call | solution.py:294
  467.7 6.6 %convolution_convert_fusion.1 = bf16[1024,768]{0,1:T(8,128)(2,1)S(1)} fusion(bf16[2048,1024]{1,0:T(8,128)(2,1)} %all-gather.4.cloned.1.call-done, bf16[2048,768]{1,0:T(8,128)(2,1)} %copy-done.7), kind=kOutput, calls=%fused_computation.75 | convolution fusion | flops 3222011904 | bytes 8912896 | tf_op jit(solution)/shard_map/dot_general | solution.py:397
  477.1 7.3 %collective-permute-done.19 = bf16[512,768]{1,0:T(8,128)(2,1)} collective-permute-done((bf16[512,768]{1,0:T(8,128)(2,1)}, bf16[512,768]{1,0:T(8,128)(2,1)}, u32[]{:S(2)}, u32[]{:S(2)}) %collective-permute-start.19) | collective-permute-done | bytes 786464 | tf_op jit(solution)/shard_map/ppermute | solution.py:424
  484.4 45.1 %collective-permute-done.18 = bf16[512,768]{1,0:T(8,128)(2,1)} collective-permute-done((bf16[512,768]{1,0:T(8,128)(2,1)}, bf16[512,768]{1,0:T(8,128)(2,1)}, u32[]{:S(2)}, u32[]{:S(2)}) %collective-permute-start.18) | collective-permute-done | bytes 786464 | tf_op jit(solution)/shard_map/ppermute | solution.py:424
  529.5 7.2 %fusion.32 = (f32[512]{0:T(512)S(1)}, f32[512,1024]{1,0:T(8,128)S(1)}) fusion(bf16[512,1024]{1,0:T(8,128)(2,1)S(1)} %copy-done.2, f32[1024]{0:T(1024)S(1)} %convert_element_type.117, bf16[1024,3072]{0,1:T(8,128)(2,1)} %all-gather.8.cloned.1.call-done, bf16[512,768]{1,0:T(8,128)(2,1)} %collective-permute-done.19, ...), kind=kOutput, calls=%fused_computation.53 | convolution fusion | flops 3235905024 | bytes 12589056 | tf_op jit(solution)/shard_map/dot_general | solution.py:403
  536.8 4.3 collective-permute-start.26
  543.1 2.8 collective-permute-start.24
  548.1 2.9 collective-permute-start.27
  551.8 21.8 %collective-permute-done.27 = bf16[128,704]{1,0:T(8,128)(2,1)S(1)} collective-permute-done((bf16[128,704]{1,0:T(8,128)(2,1)S(1)}, bf16[128,704]{1,0:T(8,128)(2,1)S(1)}, u32[]{:S(2)}, u32[]{:S(2)}) %collective-permute-start.27) | collective-permute-done | bytes 180256 | tf_op jit(solution)/shard_map/ppermute | solution.py:424
  (252 shorter events, 88.9 us)
Async XLA Ops:
  7.2 113.2 %all-gather.4.cloned.1.call-start = ((), (), s32[]{:S(2)}) async-start(), calls=%async_computation.2 | async-start | bytes 5242880 | tf_op jit(solution)/shard_map/all_gather | solution.py:468
  13.2 216.0 %all-gather.6.cloned.1.call-start = ((), (), s32[]{:S(2)}) async-start(), calls=%async_computation.3 | async-start | bytes 7225344 | tf_op jit(solution)/shard_map/all_gather | solution.py:479
  20.5 67.0 %collective-permute-start.10 = (bf16[128,2112]{0,1:T(8,128)(2,1)S(1)}, bf16[128,2112]{0,1:T(8,128)(2,1)S(1)}, u32[]{:S(2)}, u32[]{:S(2)}) collective-permute-start(bf16[128,2112]{0,1:T(8,128)(2,1)S(1)} %copy.104), channel_id=1, source_target_pairs={{0,2},{1,3},{2,0},{3,1},{4,6},{5,7},{6,4},{7,5},{8,10},{9,11},{10,... | collective-permute-start | bytes 1622024 | tf_op jit(solution)/shard_map/ppermute | solution.py:424
  24.0 26.5 %collective-permute-start.7 = (bf16[128,256]{0,1:T(8,128)(2,1)S(1)}, bf16[128,256]{0,1:T(8,128)(2,1)S(1)}, u32[]{:S(2)}, u32[]{:S(2)}) collective-permute-start(bf16[128,256]{0,1:T(8,128)(2,1)S(1)} %get-tuple-element.126), channel_id=1, source_target_pairs={{0,1},{1,2},{2,3},{3,0},{4,5},{5,6},{6,7},{7,4},{8,9},{9,10},{10,1... | collective-permute-start | bytes 196616 | tf_op jit(solution)/shard_map/ppermute | solution.py:424
  25.6 61.8 %collective-permute-start.8 = (bf16[128,256]{0,1:T(8,128)(2,1)S(1)}, bf16[128,256]{0,1:T(8,128)(2,1)S(1)}, u32[]{:S(2)}, u32[]{:S(2)}) collective-permute-start(bf16[128,256]{0,1:T(8,128)(2,1)S(1)} %get-tuple-element.126), channel_id=1, source_target_pairs={{0,2},{1,3},{2,0},{3,1},{4,6},{5,7},{6,4},{7,5},{8,10},{9,11},{10,... | collective-permute-start | bytes 196616 | tf_op jit(solution)/shard_map/ppermute | solution.py:424
  26.0 61.5 %collective-permute-start.9 = (bf16[128,256]{0,1:T(8,128)(2,1)S(1)}, bf16[128,256]{0,1:T(8,128)(2,1)S(1)}, u32[]{:S(2)}, u32[]{:S(2)}) collective-permute-start(bf16[128,256]{0,1:T(8,128)(2,1)S(1)} %get-tuple-element.126), channel_id=1, source_target_pairs={{0,3},{1,0},{2,1},{3,2},{4,7},{5,4},{6,5},{7,6},{8,11},{9,8},{10,9... | collective-permute-start | bytes 196616 | tf_op jit(solution)/shard_map/ppermute | solution.py:424
  88.5 282.6 %all-gather.8.cloned.1.call-start = ((), (), s32[]{:S(2)}) async-start(), calls=%async_computation.4 | async-start | bytes 7077888 | tf_op jit(solution)/shard_map/all_gather | solution.py:493
  120.4 80.5 %collective-permute-start.1 = (bf16[128,768]{0,1:T(8,128)(2,1)}, bf16[128,768]{0,1:T(8,128)(2,1)S(1)}, u32[]{:S(2)}, u32[]{:S(2)}) collective-permute-start(bf16[128,768]{0,1:T(8,128)(2,1)} %constant_dynamic-slice_fusion.13), channel_id=1, source_target_pairs={{0,1},{1,2},{2,3},{3,0},{4,5},{5,6},{6,7},{7,4},{8,9},{9,10},{10,1... | collective-permute-start | bytes 589832 | tf_op jit(solution)/shard_map/ppermute | solution.py:424
  120.9 80.0 %collective-permute-start.2 = (bf16[128,768]{0,1:T(8,128)(2,1)}, bf16[128,768]{0,1:T(8,128)(2,1)S(1)}, u32[]{:S(2)}, u32[]{:S(2)}) collective-permute-start(bf16[128,768]{0,1:T(8,128)(2,1)} %constant_dynamic-slice_fusion.13), channel_id=1, source_target_pairs={{0,2},{1,3},{2,0},{3,1},{4,6},{5,7},{6,4},{7,5},{8,10},{9,11},{10,... | collective-permute-start | bytes 589832 | tf_op jit(solution)/shard_map/ppermute | solution.py:424
  124.5 76.4 %collective-permute-start.3 = (bf16[128,768]{0,1:T(8,128)(2,1)}, bf16[128,768]{0,1:T(8,128)(2,1)S(1)}, u32[]{:S(2)}, u32[]{:S(2)}) collective-permute-start(bf16[128,768]{0,1:T(8,128)(2,1)} %constant_dynamic-slice_fusion.13), channel_id=1, source_target_pairs={{0,3},{1,0},{2,1},{3,2},{4,7},{5,4},{6,5},{7,6},{8,11},{9,8},{10,9... | collective-permute-start | bytes 589832 | tf_op jit(solution)/shard_map/ppermute | solution.py:424
  124.5 76.5 %collective-permute-start = (bf16[512,1024]{1,0:T(8,128)(2,1)S(1)}, bf16[512,1024]{1,0:T(8,128)(2,1)S(1)}, u32[]{:S(2)}, u32[]{:S(2)}) collective-permute-start(bf16[512,1024]{1,0:T(8,128)(2,1)S(1)} %copy-done.8), channel_id=1, source_target_pairs={{0,1},{1,0},{2,3},{3,2},{4,5},{5,4},{6,7},{7,6},{8,9},{9,8},{10,11... | collective-permute-start | bytes 3145736 | tf_op jit(solution)/shard_map/ppermute | solution.py:428
  204.0 8.6 %collective-permute-start.6 = (bf16[512,256]{1,0:T(8,128)(2,1)S(1)}, bf16[512,256]{1,0:T(8,128)(2,1)S(1)}, u32[]{:S(2)}, u32[]{:S(2)}) collective-permute-start(bf16[512,256]{1,0:T(8,128)(2,1)S(1)} %get-tuple-element.148), channel_id=1, source_target_pairs={{0,3},{1,0},{2,1},{3,2},{4,7},{5,4},{6,5},{7,6},{8,11},{9,8},{10,9... | collective-permute-start | bytes 786440 | tf_op jit(solution)/shard_map/ppermute | solution.py:424
  205.4 23.1 %collective-permute-start.5 = (bf16[512,256]{1,0:T(8,128)(2,1)S(1)}, bf16[512,256]{1,0:T(8,128)(2,1)S(1)}, u32[]{:S(2)}, u32[]{:S(2)}) collective-permute-start(bf16[512,256]{1,0:T(8,128)(2,1)S(1)} %get-tuple-element.149), channel_id=1, source_target_pairs={{0,2},{1,3},{2,0},{3,1},{4,6},{5,7},{6,4},{7,5},{8,10},{9,11},{10,... | collective-permute-start | bytes 786440 | tf_op jit(solution)/shard_map/ppermute | solution.py:424
  205.6 23.6 %collective-permute-start.4 = (bf16[512,256]{1,0:T(8,128)(2,1)S(1)}, bf16[512,256]{1,0:T(8,128)(2,1)}, u32[]{:S(2)}, u32[]{:S(2)}) collective-permute-start(bf16[512,256]{1,0:T(8,128)(2,1)S(1)} %get-tuple-element.150), channel_id=1, source_target_pairs={{0,1},{1,2},{2,3},{3,0},{4,5},{5,6},{6,7},{7,4},{8,9},{9,10},{10,1... | collective-permute-start | bytes 786440 | tf_op jit(solution)/shard_map/ppermute | solution.py:424
  234.0 26.3 %collective-permute-start.11 = (bf16[512,1024]{1,0:T(8,128)(2,1)}, bf16[512,1024]{1,0:T(8,128)(2,1)}, u32[]{:S(2)}, u32[]{:S(2)}) collective-permute-start(bf16[512,1024]{1,0:T(8,128)(2,1)} %multiply_convert_fusion.4), channel_id=1, source_target_pairs={{0,1},{1,0},{2,3},{3,2},{4,5},{5,4},{6,7},{7,6},{8,9},{9,8},{10,11... | collective-permute-start | bytes 3145736 | tf_op jit(solution)/shard_map/ppermute | solution.py:428
  235.0 239.6 %reduce-scatter.5.cloned.1.call-start = ((), (), s32[]{:S(2)}) async-start(), calls=%async_computation.5 | async-start | bytes 12091392 | tf_op jit(solution)/shard_map/reduce_scatter | solution.py:537
  293.6 25.2 %collective-permute-start.12 = (bf16[512,1024]{1,0:T(8,128)(2,1)S(1)}, bf16[512,1024]{1,0:T(8,128)(2,1)S(1)}, u32[]{:S(2)}, u32[]{:S(2)}) collective-permute-start(bf16[512,1024]{1,0:T(8,128)(2,1)S(1)} %slice.252), channel_id=1, source_target_pairs={{0,1},{1,0},{2,3},{3,2},{4,5},{5,4},{6,7},{7,6},{8,9},{9,8},{10,11... | collective-permute-start | bytes 3145736 | tf_op jit(solution)/shard_map/ppermute | solution.py:428
  318.8 24.3 %collective-permute-start.13 = (bf16[512,1024]{1,0:T(8,128)(2,1)S(1)}, bf16[512,1024]{1,0:T(8,128)(2,1)S(1)}, u32[]{:S(2)}, u32[]{:S(2)}) collective-permute-start(bf16[512,1024]{1,0:T(8,128)(2,1)S(1)} %slice.251), channel_id=1, source_target_pairs={{0,1},{1,0},{2,3},{3,2},{4,5},{5,4},{6,7},{7,6},{8,9},{9,8},{10,11... | collective-permute-start | bytes 3145736 | tf_op jit(solution)/shard_map/ppermute | solution.py:428
  347.2 20.3 %collective-permute-start.14 = (bf16[512,256]{1,0:T(8,128)(2,1)S(1)}, bf16[512,256]{1,0:T(8,128)(2,1)S(1)}, u32[]{:S(2)}, u32[]{:S(2)}) collective-permute-start(bf16[512,256]{1,0:T(8,128)(2,1)S(1)} %get-tuple-element.145), channel_id=1, source_target_pairs={{0,3},{1,0},{2,1},{3,2},{4,7},{5,4},{6,5},{7,6},{8,11},{9,8},{10,9... | collective-permute-start | bytes 786440 | tf_op jit(solution)/shard_map/ppermute | solution.py:424
  347.3 23.7 %collective-permute-start.15 = (bf16[512,256]{1,0:T(8,128)(2,1)S(1)}, bf16[512,256]{1,0:T(8,128)(2,1)S(1)}, u32[]{:S(2)}, u32[]{:S(2)}) collective-permute-start(bf16[512,256]{1,0:T(8,128)(2,1)S(1)} %get-tuple-element.144), channel_id=1, source_target_pairs={{0,2},{1,3},{2,0},{3,1},{4,6},{5,7},{6,4},{7,5},{8,10},{9,11},{10,... | collective-permute-start | bytes 786440 | tf_op jit(solution)/shard_map/ppermute | solution.py:424
  349.3 21.7 %collective-permute-start.16 = (bf16[512,256]{1,0:T(8,128)(2,1)S(1)}, bf16[512,256]{1,0:T(8,128)(2,1)S(1)}, u32[]{:S(2)}, u32[]{:S(2)}) collective-permute-start(bf16[512,256]{1,0:T(8,128)(2,1)S(1)} %get-tuple-element.143), channel_id=1, source_target_pairs={{0,1},{1,2},{2,3},{3,0},{4,5},{5,6},{6,7},{7,4},{8,9},{9,10},{10,1... | collective-permute-start | bytes 786440 | tf_op jit(solution)/shard_map/ppermute | solution.py:424
  372.0 204.7 %reduce-scatter.7.cloned.1.call-start = ((), (), s32[]{:S(2)}) async-start(), calls=%async_computation.6 | async-start | bytes 2064384
  463.1 21.2 %collective-permute-start.19 = (bf16[512,768]{1,0:T(8,128)(2,1)}, bf16[512,768]{1,0:T(8,128)(2,1)}, u32[]{:S(2)}, u32[]{:S(2)}) collective-permute-start(bf16[512,768]{1,0:T(8,128)(2,1)} %get-tuple-element.134), channel_id=1, source_target_pairs={{0,3},{1,0},{2,1},{3,2},{4,7},{5,4},{6,5},{7,6},{8,11},{9,8},{10,9... | collective-permute-start | bytes 2359304 | tf_op jit(solution)/shard_map/ppermute | solution.py:424
  463.5 66.0 %collective-permute-start.18 = (bf16[512,768]{1,0:T(8,128)(2,1)}, bf16[512,768]{1,0:T(8,128)(2,1)}, u32[]{:S(2)}, u32[]{:S(2)}) collective-permute-start(bf16[512,768]{1,0:T(8,128)(2,1)} %get-tuple-element.135), channel_id=1, source_target_pairs={{0,2},{1,3},{2,0},{3,1},{4,6},{5,7},{6,4},{7,5},{8,10},{9,11},{10,... | collective-permute-start | bytes 2359304 | tf_op jit(solution)/shard_map/ppermute | solution.py:424
  463.9 65.6 %collective-permute-start.17 = (bf16[512,768]{1,0:T(8,128)(2,1)}, bf16[512,768]{1,0:T(8,128)(2,1)}, u32[]{:S(2)}, u32[]{:S(2)}) collective-permute-start(bf16[512,768]{1,0:T(8,128)(2,1)} %get-tuple-element.136), channel_id=1, source_target_pairs={{0,1},{1,2},{2,3},{3,0},{4,5},{5,6},{6,7},{7,4},{8,9},{9,10},{10,1... | collective-permute-start | bytes 2359304 | tf_op jit(solution)/shard_map/ppermute | solution.py:424
  536.8 14.2 %collective-permute-start.26 = (bf16[128,256]{1,0:T(8,128)(2,1)S(1)}, bf16[128,256]{1,0:T(8,128)(2,1)S(1)}, u32[]{:S(2)}, u32[]{:S(2)}) collective-permute-start(bf16[128,256]{1,0:T(8,128)(2,1)S(1)} %get-tuple-element.141), channel_id=1, source_target_pairs={{0,1},{1,2},{2,3},{3,0},{4,5},{5,6},{6,7},{7,4},{8,9},{9,10},{10,1... | collective-permute-start | bytes 196616 | tf_op jit(solution)/shard_map/ppermute | solution.py:424
  541.1 9.9 %collective-permute-start.25 = (bf16[128,256]{1,0:T(8,128)(2,1)S(1)}, bf16[128,256]{1,0:T(8,128)(2,1)S(1)}, u32[]{:S(2)}, u32[]{:S(2)}) collective-permute-start(bf16[128,256]{1,0:T(8,128)(2,1)S(1)} %get-tuple-element.142), channel_id=1, source_target_pairs={{0,2},{1,3},{2,0},{3,1},{4,6},{5,7},{6,4},{7,5},{8,10},{9,11},{10,... | collective-permute-start | bytes 196616 | tf_op jit(solution)/shard_map/ppermute | solution.py:424
  543.1 7.9 %collective-permute-start.24 = (bf16[128,256]{1,0:T(8,128)(2,1)S(1)}, bf16[128,256]{1,0:T(8,128)(2,1)S(1)}, u32[]{:S(2)}, u32[]{:S(2)}) collective-permute-start(bf16[128,256]{1,0:T(8,128)(2,1)S(1)} %get-tuple-element.140), channel_id=1, source_target_pairs={{0,3},{1,0},{2,1},{3,2},{4,7},{5,4},{6,5},{7,6},{8,11},{9,8},{10,9... | collective-permute-start | bytes 196616 | tf_op jit(solution)/shard_map/ppermute | solution.py:424
  548.0 26.6 %collective-permute-start.20 = (bf16[128,1408]{1,0:T(8,128)(2,1)S(1)}, bf16[128,1408]{1,0:T(8,128)(2,1)S(1)}, u32[]{:S(2)}, u32[]{:S(2)}) collective-permute-start(bf16[128,1408]{1,0:T(8,128)(2,1)S(1)} %slice.148), channel_id=1, source_target_pairs={{0,2},{1,3},{2,0},{3,1},{4,6},{5,7},{6,4},{7,5},{8,10},{9,11},{10,... | collective-permute-start | bytes 1081352 | tf_op jit(solution)/shard_map/ppermute | solution.py:424
  548.1 25.5 %collective-permute-start.27 = (bf16[128,704]{1,0:T(8,128)(2,1)S(1)}, bf16[128,704]{1,0:T(8,128)(2,1)S(1)}, u32[]{:S(2)}, u32[]{:S(2)}) collective-permute-start(bf16[128,704]{1,0:T(8,128)(2,1)S(1)} %slice.163), channel_id=1, source_target_pairs={{0,2},{1,3},{2,0},{3,1},{4,6},{5,7},{6,4},{7,5},{8,10},{9,11},{10,... | collective-permute-start | bytes 540680 | tf_op jit(solution)/shard_map/ppermute | solution.py:424
  579.7 6.1 %collective-permute-start.23 = (f32[2,32]{1,0:T(2,128)S(1)}, f32[2,32]{1,0:T(2,128)S(1)}, u32[]{:S(2)}, u32[]{:S(2)}) collective-permute-start(f32[2,32]{1,0:T(2,128)S(1)} %get-tuple-element.163), channel_id=1, source_target_pairs={{0,3},{1,0},{2,1},{3,2},{4,7},{5,4},{6,5},{7,6},{8,11},{9,8},{10,9... | collective-permute-start | bytes 776 | tf_op jit(solution)/shard_map/ppermute | solution.py:424
  582.3 5.4 collective-permute-start.21
  (47 other events, 782.6 us)
Sparse Core Ops, SparseCore 0:
  13.3 107.0 all-gather.3
  122.3 47.5 all-gather.5
  235.1 46.7 all-gather.7
  371.3 80.2 reduce-scatter.4
  477.2 41.4 reduce-scatter.6

commit v3 on v2

v3 whole, which is shorter than its diff:
```python
import functools
import jax
import jax.numpy as jnp
from jax import lax
from jax.experimental import pallas as pl
from jax.experimental.pallas import tpu as pltpu
from jax.sharding import PartitionSpec as P

DH = 64
BIAS_SCALE = 4096.0
LOG2E = 1.4426950408889634
f32 = jnp.float32
bf16 = jnp.bfloat16
NT = (((1,), (1,)), ((), ()))
NN = (((1,), (0,)), ((), ()))


def dot(a, b, dims=NN):
    return lax.dot_general(a, b, dims, preferred_element_type=f32)


def key_window(len_ref, first, last, count, width):
    ends = []
    total = 0
    for p in range(len_ref.shape[1]):
        total = total + len_ref[0, p]
        ends.append(total)
    start = 0
    stop = count
    for e in ends:
        start = jnp.where(e <= first, e, start)
    for e in reversed(ends):
        stop = jnp.where(e > last, e, stop)
    base = (start // 128) * 128
    steps = (stop - base + width - 1) // width
    base = jnp.minimum(base, count - steps * width)
    return ends, base, steps


def for_chunks(base, steps, width, group, body):
    def many(j, carry):
        body(pl.multiple_of(base + j * (group * width), 128), group * width)
        return carry

    def single(j, carry):
        body(pl.multiple_of(base + j * width, 128), width)
        return carry

    if group > 1:
        lax.fori_loop(0, steps // group, many, 0)
    lax.fori_loop((steps // group) * group if group > 1 else 0, steps, single, 0)


def own_half(shape, head):
    lane = lax.broadcasted_iota(jnp.int32, shape, len(shape) - 1)
    return (lane < DH) if head % 2 == 0 else (lane >= DH)


def fill_values(vext, v_ref, heads):
    for h in range(heads):
        vp = v_ref[:, (h // 2) * 128:(h // 2 + 1) * 128]
        vext[h] = jnp.where(own_half(vp.shape, h), vp, jnp.ones_like(vp))


def half_norms(rows):
    lane = lax.broadcasted_iota(jnp.int32, (128, 128), 0)
    column = lax.broadcasted_iota(jnp.int32, (128, 128), 1)
    same = ((lane < DH) == (column < DH)).astype(bf16)
    squares = (rows.astype(f32) * rows.astype(f32)).astype(bf16)
    return jnp.max(dot(squares, same)) * f32(1.02)


def forward_kernel(len_ref, q_ref, k_ref, v_ref, rel_ref, lay_ref, tab_ref, kmask_ref,
                   att_ref, rinv_ref, e_ref, code_ref,
                   s_scr, m_scr, acc_scr, vext, colcode, knorm, *, width, heads, group):
    tq, count = rel_ref.shape
    pairs = heads // 2
    i = pl.program_id(0)
    t0 = i * tq
    ends, base, steps = key_window(len_ref, t0, t0 + tq - 1, count, width)

    @pl.when(i == 0)
    def _():
        fill_values(vext, v_ref, heads)
        pos = lax.broadcasted_iota(jnp.int32, (8, count), 1)
        page = jnp.zeros((8, count), jnp.int32)
        for e in ends:
            page = page + (pos >= e).astype(jnp.int32)
        colcode[...] = jnp.where(kmask_ref[...] == 1, page, -1)
        for p in range(pairs):
            knorm[p] = half_norms(k_ref[:, p * 128:(p + 1) * 128])

    rowpos = lax.broadcasted_iota(jnp.int32, (tq, 128), 0) + t0
    rowpage = jnp.zeros((tq, 128), jnp.int32)
    for e in ends:
        rowpage = rowpage + (rowpos >= e).astype(jnp.int32)
    lanes = lax.broadcasted_iota(jnp.int32, (tq, 128), 1)
    scaled = []
    largest = f32(0.0)
    for h in range(heads):
        qp = q_ref[:, (h // 2) * 128:(h // 2 + 1) * 128]
        scaled.append(jnp.where(own_half(qp.shape, h), qp * bf16(BIAS_SCALE), jnp.zeros_like(qp)))
        if h % 2 == 0:
            largest = jnp.maximum(largest, half_norms(qp) * knorm[h // 2])
    tabs = [[jnp.broadcast_to(tab_ref[2 * p + r:2 * p + r + 1, :], (tq, 128)) for r in range(2)]
            for p in range(pairs)]

    def scores(c0, width, use):
        raw = [dot(scaled[h], k_ref[pl.ds(c0, width), (h // 2) * 128:(h // 2 + 1) * 128], NT)
               for h in range(heads)]
        for half in range(width // 128):
            cc = pl.multiple_of(c0 + half * 128, 128)
            rel = rel_ref[:, pl.ds(cc, 128)]
            lay = lay_ref[:, pl.ds(cc, 128)]
            code_ref[:, pl.ds(cc, 128)] = (rel + lay * 32).astype(jnp.int16)
            col = jnp.broadcast_to(colcode[0:1, pl.ds(cc, 128)], (tq, 128))
            seen = (rowpage == col) | (rowpos == lanes + cc)
            hide = jnp.where(seen, f32(0.0), f32(-1e30))
            for p in range(pairs):
                word = (jnp.take_along_axis(tabs[p][0], rel, axis=1, mode="promise_in_bounds")
                        + jnp.take_along_axis(tabs[p][1], lay, axis=1, mode="promise_in_bounds"))
                parts = ((word & 0xFFFF).astype(f32), (word >> 16).astype(f32))
                for r in range(2):
                    h = 2 * p + r
                    use(h, half, cc, raw[h][:, half * 128:(half + 1) * 128] + parts[r] + hide)

    for h in range(heads):
        acc_scr[h] = jnp.zeros((tq, 128), f32)
    bounded = jnp.sqrt(largest) + 8.0 <= 60.0

    @pl.when(bounded)
    def _():
        def chunk(c0, size):
            pieces = {}

            def use(h, half, cc, s):
                e = jnp.exp2(s * f32(LOG2E / BIAS_SCALE)).astype(bf16)
                e_ref[h, :, pl.ds(cc, 128)] = e
                pieces[h, half] = e

            scores(c0, size, use)
            for h in range(heads):
                e = jnp.concatenate([pieces[h, half] for half in range(size // 128)], axis=1)
                acc_scr[h] += dot(e, vext[h, pl.ds(c0, size), :])

        for_chunks(base, steps, width, group, chunk)

    @pl.when(jnp.logical_not(bounded))
    def _():
        for h in range(heads):
            m_scr[h] = jnp.full((tq, 128), -3e38, f32)

        def first(j, carry):
            def use(h, half, cc, s):
                s_scr[h, :, pl.ds(cc, 128)] = s
                m_scr[h] = jnp.maximum(m_scr[h], s)

            scores(pl.multiple_of(base + j * width, 128), width, use)
            return carry

        lax.fori_loop(0, steps, first, 0)
        for h in range(heads):
            top = jnp.max(m_scr[h], axis=1, keepdims=True)

            def second(j, carry):
                c0 = pl.multiple_of(base + j * width, 128)
                e = jnp.exp2((s_scr[h, :, pl.ds(c0, width)] - top) * f32(LOG2E / BIAS_SCALE)).astype(bf16)
                e_ref[h, :, pl.ds(c0, width)] = e
                acc_scr[h] += dot(e, vext[h, pl.ds(c0, width), :])
                return carry

            lax.fori_loop(0, steps, second, 0)

    low = own_half((tq, 128), 0)
    for p in range(pairs):
        even, odd = acc_scr[2 * p], acc_scr[2 * p + 1]
        rinv = 1.0 / pltpu.roll(jnp.where(low, odd, even), DH, 1)
        att_ref[:, p * 128:(p + 1) * 128] = (jnp.where(low, even, odd) * rinv).astype(bf16)
        rinv_ref[:, p * 128:(p + 1) * 128] = rinv


def attention_forward(page_lengths, proj, rel, lay, tab, kmask, tq=256, width=256, group=1):
    count = proj.shape[0]
    hc = proj.shape[1] // 3
    heads = hc // DH
    grid = (count // tq,)
    return pl.pallas_call(
        functools.partial(forward_kernel, width=width, heads=heads, group=group),
        grid=grid,
        in_specs=[
            pl.BlockSpec(memory_space=pltpu.SMEM),
            pl.BlockSpec((tq, hc), lambda i: (i, 0)),
            pl.BlockSpec((count, hc), lambda i: (0, 1)),
            pl.BlockSpec((count, hc), lambda i: (0, 2)),
            pl.BlockSpec((tq, count), lambda i: (i, 0)),
            pl.BlockSpec((tq, count), lambda i: (i, 0)),
            pl.BlockSpec(tab.shape, lambda i: (0, 0)),
            pl.BlockSpec((1, count), lambda i: (0, 0)),
        ],
        out_specs=[
            pl.BlockSpec((tq, hc), lambda i: (i, 0)),
            pl.BlockSpec((tq, hc), lambda i: (i, 0)),
            pl.BlockSpec((heads, tq, count), lambda i: (0, i, 0)),
            pl.BlockSpec((tq, count), lambda i: (i, 0)),
        ],
        out_shape=[
            jax.ShapeDtypeStruct((count, hc), bf16),
            jax.ShapeDtypeStruct((count, hc), f32),
            jax.ShapeDtypeStruct((heads, count, count), bf16),
            jax.ShapeDtypeStruct((count, count), jnp.int16),
        ],
        scratch_shapes=[
            pltpu.VMEM((heads, tq, count), f32),
            pltpu.VMEM((heads, tq, 128), f32),
            pltpu.VMEM((heads, tq, 128), f32),
            pltpu.VMEM((heads, count, 128), bf16),
            pltpu.VMEM((8, count), jnp.int32),
            pltpu.SMEM((heads // 2,), f32),
        ],
        compiler_params=pltpu.CompilerParams(vmem_limit_bytes=56 << 20),
        cost_estimate=pl.CostEstimate(
            flops=heads * count * count * 256, bytes_accessed=150 << 20, transcendentals=heads * count * count // 2),
        name="attention_forward",
    )(page_lengths, proj, proj, proj, rel, lay, tab, kmask.reshape(1, count))


def bias_words(rel_table, layout_table):
    def pack(table):
        whole = jnp.round(table.astype(f32) * BIAS_SCALE).astype(jnp.int32)
        low = jnp.clip(whole[:, 0::2] + 16384, 0, 32767)
        high = jnp.clip(whole[:, 1::2], -16384, 16383)
        words = (high * 65536 + low).T
        return jnp.pad(words, ((0, 0), (0, 128 - words.shape[1])))
    both = jnp.stack([pack(rel_table), pack(layout_table)], axis=1)
    return both.reshape(-1, 128)


def signs(code, shift, bits):
    return [jnp.where((code & jnp.int16(1 << (shift + b))) == 0, bf16(1.0), bf16(-1.0))
            for b in range(bits)]


def walsh(sign_list):
    out = [None]
    for s in sign_list:
        out = out + [s if o is None else o * s for o in out]
    return out


def backward_kernel(len_ref, q_ref, k_ref, v_ref, e_ref, da_ref, att_ref, rinv_ref,
                    dq_ref, dk_ref, dv_ref, ds_ref,
                    vext, lhs_scr, dat_scr, qt_scr, dq_scr, dkt, dvt, *, width, heads, group):
    tq = q_ref.shape[0]
    count = k_ref.shape[0]
    pairs = heads // 2
    i = pl.program_id(0)
    t0 = i * tq
    ends, base, steps = key_window(len_ref, t0, t0 + tq - 1, count, width)

    @pl.when(i == 0)
    def _():
        fill_values(vext, v_ref, heads)
        dkt[...] = jnp.zeros_like(dkt)
        dvt[...] = jnp.zeros_like(dvt)

    low = own_half((tq, 128), 0)
    lane = lax.broadcasted_iota(jnp.int32, (tq, 128), 1)
    first_part = (lane & 32) == 0
    for p in range(pairs):
        cols = slice(p * 128, (p + 1) * 128)
        da = (da_ref[:, cols].astype(f32) * rinv_ref[:, cols]).astype(bf16)
        daf = da.astype(f32)
        prod = daf * att_ref[:, cols].astype(f32)
        for r in range(2):
            own = low if r == 0 else jnp.logical_not(low)
            delta = jnp.sum(jnp.where(own, prod, 0.0), axis=1, keepdims=True) * f32(-1.0 / 32)
            high = delta.astype(bf16).astype(f32)
            rest = delta - high
            lhs_scr[2 * p + r] = jnp.where(own, daf, jnp.where(first_part, high, rest)).astype(bf16)
        dat_scr[p] = daf.T.astype(bf16)
        qt_scr[p] = q_ref[:, cols].astype(f32).T.astype(bf16)
        dq_scr[p] = jnp.zeros((tq, 128), f32)

    def chunk(c0, size):
        here = pl.ds(c0, size)
        for p in range(pairs):
            kp = k_ref[here, p * 128:(p + 1) * 128]
            dqs = []
            for r in range(2):
                h = 2 * p + r
                rows = slice(r * DH, (r + 1) * DH)
                e = e_ref[h, :, here]
                d = dot(lhs_scr[h], vext[h, here, :], NT)
                ds = (e.astype(f32) * d).astype(bf16)
                ds_ref[h, :, here] = ds
                dqs.append(dot(ds, kp))
                dkt[p, rows, here] += dot(qt_scr[p, rows, :], ds)
                dvt[p, rows, here] += dot(dat_scr[p, rows, :], e)
            dq_scr[p] += jnp.where(low, dqs[0], dqs[1])

    for_chunks(base, steps, width, group, chunk)
    for p in range(pairs):
        dq_ref[:, p * 128:(p + 1) * 128] = dq_scr[p].astype(bf16)

    @pl.when(i == pl.num_programs(0) - 1)
    def _():
        for p in range(pairs):
            for c in range(0, count, 256):
                dk_ref[c:c + 256, p * 128:(p + 1) * 128] = dkt[p, :, c:c + 256].T.astype(bf16)
                dv_ref[c:c + 256, p * 128:(p + 1) * 128] = dvt[p, :, c:c + 256].T.astype(bf16)


def attention_backward(page_lengths, proj, e, d_att, att, rinv, tq=256, width=256, group=2):
    count = proj.shape[0]
    hc = proj.shape[1] // 3
    heads = hc // DH
    pairs = heads // 2
    grid = (count // tq,)
    tile = lambda i: (i, 0)
    fixed = lambda i: (0, 0)
    return pl.pallas_call(
        functools.partial(backward_kernel, width=width, heads=heads, group=group),
        grid=grid,
        in_specs=[
            pl.BlockSpec(memory_space=pltpu.SMEM),
            pl.BlockSpec((tq, hc), tile),
            pl.BlockSpec((count, hc), lambda i: (0, 1)),
            pl.BlockSpec((count, hc), lambda i: (0, 2)),
            pl.BlockSpec((heads, tq, count), lambda i: (0, i, 0)),
            pl.BlockSpec((tq, hc), tile),
            pl.BlockSpec((tq, hc), tile),
            pl.BlockSpec((tq, hc), tile),
        ],
        out_specs=[
            pl.BlockSpec((tq, hc), tile),
            pl.BlockSpec((count, hc), fixed),
            pl.BlockSpec((count, hc), fixed),
            pl.BlockSpec((heads, tq, count), lambda i: (0, i, 0)),
        ],
        out_shape=[
            jax.ShapeDtypeStruct((count, hc), bf16),
            jax.ShapeDtypeStruct((count, hc), bf16),
            jax.ShapeDtypeStruct((count, hc), bf16),
            jax.ShapeDtypeStruct((heads, count, count), bf16),
        ],
        scratch_shapes=[
            pltpu.VMEM((heads, count, 128), bf16),
            pltpu.VMEM((heads, tq, 128), bf16),
            pltpu.VMEM((pairs, 128, tq), bf16),
            pltpu.VMEM((pairs, 128, tq), bf16),
            pltpu.VMEM((pairs, tq, 128), f32),
            pltpu.VMEM((pairs, 128, count), f32),
            pltpu.VMEM((pairs, 128, count), f32),
        ],
        compiler_params=pltpu.CompilerParams(vmem_limit_bytes=56 << 20),
        cost_estimate=pl.CostEstimate(
            flops=heads * count * count * 512, bytes_accessed=150 << 20, transcendentals=0),
        name="attention_backward",
    )(page_lengths, proj, proj, proj, e, d_att, att, rinv)


def table_kernel(len_ref, ds_ref, code_ref, hl_ref, hr_ref, *bufs, width, parts):
    heads, tq, count = ds_ref.shape
    i = pl.program_id(0)
    t0 = i * tq
    ends, base, steps = key_window(len_ref, t0, t0 + tq - 1, count, width)

    @pl.when(i == 0)
    def _():
        hl_ref[...] = jnp.zeros_like(hl_ref)
        hr_ref[...] = jnp.zeros_like(hr_ref)

    one = jnp.ones((16, width), bf16)

    def chunk(j, carry):
        c0 = pl.multiple_of(base + j * width, 128)
        here = pl.ds(c0, width)
        blocks = tq // 16 // parts
        for part in range(parts):
            left, blay, brel = bufs[3 * part:3 * part + 3]
            for b in range(blocks):
                at = 16 * (part * blocks + b)
                rows = slice(at, at + 16)
                span = slice(b * width, (b + 1) * width)
                code = code_ref[rows, here]
                rel_signs = signs(code, 0, 5)
                lay_signs = signs(code, 5, 6)
                left_lay = walsh(lay_signs[:2])[1:]
                for h in range(heads):
                    ds = ds_ref[h, rows, here]
                    for a, func in enumerate(left_lay + [None, rel_signs[0]]):
                        place = 16 * (a * heads + h)
                        left[place:place + 16, span] = ds if func is None else ds * func
                for n, func in enumerate(walsh(lay_signs[2:])):
                    blay[16 * n:16 * (n + 1), span] = one if func is None else func
                for n, func in enumerate(walsh(rel_signs[1:])):
                    brel[16 * n:16 * (n + 1), span] = one if func is None else func
            hl_ref[...] += dot(left[:64 * heads, :], blay[...], NT)
            hr_ref[...] += dot(left[48 * heads:80 * heads, :], brel[...], NT)
        return carry

    lax.fori_loop(0, steps, chunk, 0)


def table_grads(page_lengths, ds, code, tq=256, width=256, parts=2):
    heads, count, _ = ds.shape
    deep = tq // 16 * width // parts
    fixed = lambda i: (0, 0)
    return pl.pallas_call(
        functools.partial(table_kernel, width=width, parts=parts),
        grid=(count // tq,),
        in_specs=[
            pl.BlockSpec(memory_space=pltpu.SMEM),
            pl.BlockSpec((heads, tq, count), lambda i: (0, i, 0)),
            pl.BlockSpec((tq, count), lambda i: (i, 0)),
        ],
        out_specs=[
            pl.BlockSpec((64 * heads, 256), fixed),
            pl.BlockSpec((32 * heads, 256), fixed),
        ],
        out_shape=[
            jax.ShapeDtypeStruct((64 * heads, 256), f32),
            jax.ShapeDtypeStruct((32 * heads, 256), f32),
        ],
        scratch_shapes=[
            pltpu.VMEM((80 * heads, deep), bf16),
            pltpu.VMEM((256, deep), bf16),
            pltpu.VMEM((256, deep), bf16),
        ] * parts,
        compiler_params=pltpu.CompilerParams(vmem_limit_bytes=56 << 20),
        cost_estimate=pl.CostEstimate(
            flops=heads * count * count * 512, bytes_accessed=150 << 20, transcendentals=0),
        name="table_grads",
    )(page_lengths, ds, code)


def bucket_sums(raw, heads):
    right = raw.shape[1] // 16
    left = raw.shape[0] // (16 * heads)
    cube = raw.reshape(left, heads, 16, right, 16)
    traced = jnp.sum(cube * jnp.eye(16, dtype=f32)[None, None, :, None, :], axis=(2, 4))
    if left == 4:
        traced = jnp.concatenate([traced[3:], traced[:3]], axis=0)

    def table(n):
        v = lax.iota(jnp.int32, n)
        both = v[:, None] & v[None, :]
        return (1 - 2 * (lax.population_count(both) & 1)).astype(f32)

    out = jnp.einsum("ahn,ax,ny->yxh", traced, table(left), table(right), precision=lax.Precision.HIGHEST)
    return out.reshape(left * right, heads) / (left * right)


TANH_SLOPE = 0.7978845608028654
CUBE = 0.044715


def feed_forward_kernel(skip, shards, x_ref, g_ref, wg_ref, wu_ref, wd_ref, far_ref, *outs):
    units = wg_ref.shape[0]
    step = pad_lanes(units)
    dn_ref = outs[-1]
    x = x_ref[...]
    g = g_ref[...]
    total = None
    for s in range(shards):
        if s == 0:
            wg, wu = wg_ref[...], wu_ref[...]
            d_hidden = dot(g, wd_ref[...], NT)
            ahead, back = NT, NN
        else:
            at = skip + 3 * step * (s - 1)
            wg = far_ref[:, at:at + units]
            wu = far_ref[:, at + step:at + step + units]
            d_hidden = dot(g, far_ref[:, at + 2 * step:at + 2 * step + units])
            ahead, back = NN, NT
        gate = dot(x, wg, ahead)
        up = dot(x, wu, ahead)
        square = gate * gate
        t = jnp.tanh(TANH_SLOPE * gate * (1.0 + CUBE * square))
        half = 0.5 + 0.5 * t
        gelu = gate * half
        slope = half + (0.5 * TANH_SLOPE) * gate * (1.0 - t * t) * (1.0 + (3 * CUBE) * square)
        d_gate = (d_hidden * up * slope).astype(bf16)
        d_up = (d_hidden * gelu).astype(bf16)
        outs[3 * s][...] = (gelu * up).astype(bf16)
        outs[3 * s + 1][...] = d_gate
        outs[3 * s + 2][...] = d_up
        value = dot(d_gate, wg, back) + dot(d_up, wu, back)
        total = value if total is None else total + value
    dn_ref[...] = total


def feed_forward(x, g, w_gate_t, w_up_t, w_down, far, skip, tile=256):
    tokens, features = x.shape
    units = w_down.shape[0]
    shards = 1 + (far.shape[1] - skip) // (3 * pad_lanes(units))
    tile = min(tile, tokens)
    rows = lambda n: pl.BlockSpec((tile, n), lambda i: (i, 0))
    whole = lambda a: pl.BlockSpec(a.shape, lambda i: (0, 0))
    return pl.pallas_call(
        functools.partial(feed_forward_kernel, skip, shards),
        grid=(tokens // tile,),
        in_specs=[rows(features), rows(features), whole(w_gate_t), whole(w_up_t), whole(w_down), whole(far)],
        out_specs=[rows(units)] * (3 * shards) + [rows(features)],
        out_shape=[jax.ShapeDtypeStruct((tokens, units), bf16)] * (3 * shards)
        + [jax.ShapeDtypeStruct((tokens, features), f32)],
        compiler_params=pltpu.CompilerParams(vmem_limit_bytes=56 << 20),
        cost_estimate=pl.CostEstimate(
            flops=10 * tokens * features * units * shards, bytes_accessed=14 << 20,
            transcendentals=tokens * units * shards),
        name="feed_forward",
    )(x, g, w_gate_t, w_up_t, w_down, far)


def pad_lanes(n):
    return (n + 127) // 128 * 128


def weight_grads_kernel(skip, n_left, n_right, *refs):
    lefts = refs[:2 * n_left]
    rights = refs[2 * n_left:-1]
    out_ref = refs[-1]
    rows_in = (((0,), (0,)), ((), ()))
    place = skip
    for n, left in enumerate(n_right):
        a, b = rights[2 * n], rights[2 * n + 1]
        size = a.shape[1]
        value = dot(lefts[2 * left][...], a[...], rows_in) + dot(lefts[2 * left + 1][...], b[...], rows_in)
        out_ref[:, place:place + size] = value.astype(bf16)
        if pad_lanes(size) > size:
            out_ref[:, place + size:place + pad_lanes(size)] = jnp.zeros(
                (out_ref.shape[0], pad_lanes(size) - size), bf16)
        place += pad_lanes(size)


def weight_grads(lefts, rights, groups, skip, tile=256):
    features = lefts[0].shape[1]
    columns = skip + sum(pad_lanes(r.shape[1]) for r in rights[::2])
    column = lambda a: pl.BlockSpec((a.shape[0], tile), lambda i: (0, i))
    whole = lambda a: pl.BlockSpec(a.shape, lambda i: (0, 0))
    return pl.pallas_call(
        functools.partial(weight_grads_kernel, skip, len(lefts) // 2, groups),
        grid=(features // tile,),
        in_specs=[column(a) for a in lefts] + [whole(a) for a in rights],
        out_specs=pl.BlockSpec((tile, columns), lambda i: (i, 0)),
        out_shape=jax.ShapeDtypeStruct((features, columns), bf16),
        compiler_params=pltpu.CompilerParams(vmem_limit_bytes=56 << 20),
        cost_estimate=pl.CostEstimate(
            flops=4 * features * columns * lefts[0].shape[0], bytes_accessed=26 << 20, transcendentals=0),
        name="weight_grads",
    )(*lefts, *rights)


epsilon = 1e-06


def contract_rows(left, right):
    return lax.dot_general(
        left, right, (((0,), (0,)), ((), ())), preferred_element_type=jnp.float32
    )


def contract_cols(left, right):
    return lax.dot_general(
        left, right, (((1,), (1,)), ((), ())), preferred_element_type=jnp.float32
    )


def norm_rows(rows, gain):
    scale = lax.rsqrt(jnp.mean(rows * rows, axis=-1, keepdims=True) + epsilon)
    return (scale, (rows * scale * gain).astype(jnp.bfloat16))


def norm_back(d_normed, rows, scale, gain):
    shaped = d_normed * gain
    cubed = scale * scale * scale
    return scale * shaped - rows * cubed * jnp.mean(shaped * rows, axis=-1, keepdims=True)


def along(array, shift, ring):
    return lax.ppermute(array, "narrow", [(i, (i + shift) % ring) for i in range(ring)])


def swap(array, ring):
    return lax.ppermute(array, "narrow", [(i, i ^ 1) for i in range(ring)])


def rows_of(array, index, count):
    return lax.dynamic_slice_in_dim(array, index * count, count, 0)


def on_device(
    wide,
    ring,
    layer_input,
    out_grad,
    norm_attn_gain,
    w_query,
    w_key,
    w_value,
    w_out,
    rel_table,
    layout_table,
    norm_ffn_gain,
    w_gate,
    w_up,
    down_projection_weight,
    page_lengths,
    key_mask,
    rel_bucket,
    layout_bucket,
):
    tokens, width = layer_input.shape
    head_cols = w_query.shape[1]
    heads = head_cols // DH
    units = w_gate.shape[1]
    padded = pad_lanes(units)
    part = width // wide
    me = lax.axis_index("narrow")
    my_wide = lax.axis_index("wide")
    gain_attn = norm_attn_gain.astype(f32)
    gain_ffn = norm_ffn_gain.astype(f32)
    resid = layer_input.astype(f32)

    scale_attn, normed_attn = norm_rows(resid, gain_attn)
    normed_attn_all = lax.all_gather(normed_attn, "narrow", axis=0, tiled=True)

    w_project = jnp.concatenate([w_query, w_key, w_value], axis=1)
    own_rows_gate = rows_of(w_gate, my_wide, part)
    own_rows_up = rows_of(w_up, my_wide, part)
    own_rows_project = rows_of(w_project, my_wide, part)
    down_piece = lax.dynamic_slice_in_dim(down_projection_weight, my_wide * part, part, 1).T
    out_piece = lax.dynamic_slice_in_dim(w_out, my_wide * part, part, 1).T
    ffn_piece = jnp.concatenate(
        [jnp.pad(piece, ((0, 0), (0, padded - units))) for piece in (own_rows_gate, own_rows_up, down_piece)], axis=1)
    normed_attn_all, out_piece, ffn_piece = lax.optimization_barrier((normed_attn_all, out_piece, ffn_piece))
    ffn_pieces = [along(ffn_piece, d, ring) for d in range(2, ring, 2)]
    out_pieces = [out_piece] + [along(out_piece, d, ring) for d in range(1, ring)]
    w_first = lax.all_gather(jnp.concatenate(out_pieces + ffn_pieces, axis=1), "wide", axis=0, tiled=True)
    late_project, late_grad, ffn_pieces = lax.optimization_barrier((own_rows_project, out_grad, ffn_pieces))
    project_pieces = [own_rows_project] + [along(late_project, d, ring) for d in range(1, ring)]
    other_grad = swap(late_grad, ring)
    out_t = w_first[:, : ring * head_cols]

    projected = dot(normed_attn_all, w_project).astype(bf16)
    attended, rinv, exps, codes = attention_forward(
        page_lengths, projected, rel_bucket, layout_bucket, bias_words(rel_table, layout_table), key_mask)
    attended, other_grad, project_pieces = lax.optimization_barrier((attended, other_grad, project_pieces))
    w_project_all = lax.all_gather(jnp.concatenate(project_pieces, axis=1), "wide", axis=0, tiled=True)
    mine = [along(rows_of(attended, (me + d) % ring, tokens), d, ring) for d in range(1, ring)]
    attended_own = jnp.concatenate([rows_of(attended, me, tokens)] + mine, axis=1)
    middle = resid + contract_cols(attended_own, out_t)

    scale_ffn, normed_ffn = norm_rows(middle, gain_ffn)
    other_normed = swap(normed_ffn, ring)
    ffn_weights = (w_gate.T, w_up.T, down_projection_weight, w_first, ring * head_cols)
    own = feed_forward(normed_ffn, out_grad, *ffn_weights)
    other = feed_forward(other_normed, other_grad, *ffn_weights)
    shards = (len(own) - 1) // 3
    other_d_normed = swap(other[-1].astype(bf16), ring)
    rights, groups = [], []
    for s in range(shards):
        for n in range(1, 4):
            rights += [own[3 * s + n % 3], other[3 * s + n % 3]]
            groups.append(n // 3)
    sums = weight_grads(
        (normed_ffn, other_normed, out_grad, other_grad), rights, tuple(groups), ring * head_cols)
    sums, other_d_normed = lax.optimization_barrier((sums, other_d_normed))
    d_normed_ffn = own[-1] + other_d_normed.astype(f32)
    d_middle = out_grad.astype(f32) + norm_back(d_normed_ffn, middle, scale_ffn, gain_ffn)
    d_middle_low = d_middle.astype(bf16)
    d_attended_own = dot(d_middle_low, out_t).astype(bf16)

    def block(d):
        return d_attended_own[:, d * head_cols : (d + 1) * head_cols]

    d_attended = jnp.zeros((ring * tokens, head_cols), bf16)
    d_attended = lax.dynamic_update_slice_in_dim(d_attended, block(0), me * tokens, 0)
    for d in range(1, ring):
        d_attended = lax.dynamic_update_slice_in_dim(
            d_attended, along(block(d), -d, ring), ((me + d) % ring) * tokens, 0)

    d_middle_late, attended_late, hiddens = lax.optimization_barrier(
        (d_middle_low, attended_own, [(own[3 * s], other[3 * s]) for s in range(shards)]))
    sums = lax.dynamic_update_slice(sums, contract_rows(d_middle_late, attended_late).astype(bf16), (0, 0))
    own_out, other_out = 0.0, 0.0
    for s, (own_hidden, other_hidden) in enumerate(hiddens):
        if s == 0:
            down, dims = down_projection_weight, NN
        else:
            at = ring * head_cols + 3 * padded * (s - 1) + 2 * padded
            down, dims = w_first[:, at : at + units], NT
        own_out = own_out + dot(own_hidden, down, dims)
        other_out = other_out + dot(other_hidden, down, dims)
    other_out = other_out.astype(bf16)
    sums, d_attended, w_project_all, other_out, own_out = lax.optimization_barrier(
        (sums, d_attended, w_project_all, other_out, own_out))
    ffn_sums = lax.psum_scatter(sums, "wide", scatter_dimension=0, tiled=True)
    other_out = swap(other_out, ring)

    d_query, d_keys, d_values, d_scores = attention_backward(
        page_lengths, projected, exps, d_attended, attended, rinv)
    d_project = jnp.concatenate([d_query, d_keys, d_values], axis=1)
    d_project, other_out, middle_late = lax.optimization_barrier((d_project, other_out, middle))
    layer_out = (middle_late + own_out + other_out.astype(f32)).astype(bf16)
    mine = [along(rows_of(d_project, (me + d) % ring, tokens), d, ring) for d in range(1, ring)]
    last_sums = contract_rows(normed_attn_all, d_project).astype(bf16)
    last_sums, ffn_sums = lax.optimization_barrier((last_sums, ffn_sums))
    sum_project = lax.psum_scatter(last_sums, "wide", scatter_dimension=0, tiled=True).astype(f32)

    last_sums, d_scores = lax.optimization_barrier((last_sums, d_scores))
    raw_lay, raw_rel = table_grads(page_lengths, d_scores, codes)
    raw_lay, raw_rel, mine, sum_project = lax.optimization_barrier((raw_lay, raw_rel, mine, sum_project))
    d_project_own = jnp.concatenate([rows_of(d_project, me, tokens)] + mine, axis=1)
    d_normed_attn = contract_cols(d_project_own, w_project_all)
    in_grad = d_middle + norm_back(d_normed_attn, resid, scale_attn, gain_attn)
    grad_relative = bucket_sums(raw_rel, heads)
    grad_layout = bucket_sums(raw_lay, heads)
    tables = jnp.concatenate(
        [grad_relative.reshape(wide, -1, heads), grad_layout.reshape(wide, -1, heads)], axis=1)
    n_rel = grad_relative.shape[0] // wide
    reach = wide // 2
    while reach >= 1:
        bit = (my_wide // reach) % 2
        keep = lax.dynamic_slice_in_dim(tables, bit * reach, reach, 0)
        give = lax.dynamic_slice_in_dim(tables, (1 - bit) * reach, reach, 0)
        tables = keep + lax.ppermute(give, "wide", [(i, i ^ reach) for i in range(wide)])
        reach //= 2
    sum_tables = tables[0]

    first = ring * head_cols

    def stripe(shard, n):
        at = first + padded * (3 * shard + n)
        return ffn_sums[:, at : at + units]

    sum_gate, sum_up, sum_down = [stripe(0, n).astype(f32) for n in range(3)]
    for s in range(1, shards):
        at = first + 3 * padded * s
        block = along(ffn_sums[:, at : at + 3 * padded], -2 * s, ring).astype(f32)
        sum_gate += block[:, :units]
        sum_up += block[:, padded : padded + units]
        sum_down += block[:, 2 * padded : 2 * padded + units]
    sum_wout = ffn_sums[:, :head_cols].astype(f32)
    for d in range(1, ring):
        sum_wout += along(ffn_sums[:, d * head_cols : (d + 1) * head_cols], -d, ring).astype(f32)

    gain_terms = jnp.stack(
        [
            jnp.sum(own_rows_project.astype(f32) * sum_project, axis=1),
            jnp.sum(own_rows_gate.astype(f32) * sum_gate + own_rows_up.astype(f32) * sum_up, axis=1),
        ]
    )
    share = part // ring

    def gain_share(index):
        return lax.dynamic_slice_in_dim(gain_terms, index * share, share, 1)

    gain_sum = gain_share(me)
    for d in range(1, ring):
        gain_sum = gain_sum + along(gain_share((me + d) % ring), d, ring)
    place = my_wide * part + me * share
    gains = lax.dynamic_slice_in_dim(jnp.stack([gain_attn, gain_ffn]), place, share, 1)
    gain_grads = gain_sum / gains
    return (
        layer_out,
        in_grad,
        gain_grads[0],
        sum_project[:, :head_cols],
        sum_project[:, head_cols : 2 * head_cols],
        sum_project[:, 2 * head_cols :],
        sum_wout.T,
        sum_tables[:n_rel],
        sum_tables[n_rel:],
        gain_grads[1],
        sum_gate,
        sum_up,
        sum_down.T,
    )


def solution(mesh):
    placed = (
        P(("wide", "narrow"), None),
        P(("wide", "narrow"), None),
        P(),
        P(None, "narrow"),
        P(None, "narrow"),
        P(None, "narrow"),
        P("narrow", None),
        P(None, "narrow"),
        P(None, "narrow"),
        P(),
        P(None, "narrow"),
        P(None, "narrow"),
        P("narrow", None),
        P("wide", None),
        P("wide"),
        P("wide", None),
        P("wide", None),
    )
    return jax.shard_map(
        functools.partial(on_device, mesh.shape["wide"], mesh.shape["narrow"]),
        mesh=mesh,
        in_specs=placed,
        out_specs=(
            P(("wide", "narrow"), None),
            P(("wide", "narrow"), None),
            P(("wide", "narrow")),
            P("wide", "narrow"),
            P("wide", "narrow"),
            P("wide", "narrow"),
            P("narrow", "wide"),
            P("wide", "narrow"),
            P("wide", "narrow"),
            P(("wide", "narrow")),
            P("wide", "narrow"),
            P("wide", "narrow"),
            P("narrow", "wide"),
        ),
        check_vma=False,
    )
```

time: 598 us -> 592 us (0.990)
  the two profiles are of different devices: /device:TPU:6 before, /device:TPU:0 now
where the time goes in v3:
time: 592 us; the launch traced here: 584 us
  waiting for transfers between devices  223 us (38%)
  Pallas kernels  200 us (34%)
  starting transfers between devices  61.2 us (10%)
  matrix products  33.7 us (6%)
  local copies, waits for them, and re-layouts  27.5 us (5%)
  other arithmetic  25 us (4%)
  between operations  14.9 us (3%)
    ppermute x23, waiting for transfers between devices, along(): lax.ppermute(array, 'narrow', [(i, (i + shift) % ring) for i in range(rin...  98.2 us
    all_gather x1, waiting for transfers between devices, on_device(): normed_attn_all = lax.all_gather(normed_attn, 'narrow', axis=0, tiled=True)  80.9 us
    pallas_call x1, Pallas kernels, table_grads(): pl.pallas_call(functools.partial(table_kernel, width=width, parts=parts),...  56.8 us
    ppermute x23, starting transfers between devices, along(): lax.ppermute(array, 'narrow', [(i, (i + shift) % ring) for i in range(rin...  51.7 us
    pallas_call x1, Pallas kernels, attention_forward(): pl.pallas_call(functools.partial(forward_kernel, width=width, heads=heads...  51.4 us
    pallas_call x1, Pallas kernels, attention_backward(): pl.pallas_call(functools.partial(backward_kernel, width=width, heads=head...  43.3 us
    pallas_call x2, Pallas kernels, feed_forward(): pl.pallas_call(functools.partial(feed_forward_kernel, skip, shards), grid...  31.1 us
    reduce_scatter x1, waiting for transfers between devices, on_device(): ffn_sums = lax.psum_scatter(sums, 'wide', scatter_dimension=0, tiled=True)  31 us
  transfers between devices with their start and end apart: 35, of which 14 were waited for; matrix products, arithmetic and copies ran while one was open for 12% of the time, Pallas kernels for 34%

profile of v3, /device:TPU:0, one launch (start us, length us, event | category | flops | bytes accessed | tf_op | source)
XLA Modules:
  0.0 584.4 jit_solution(10321113282233919405)
XLA Ops:
  9.5 2.5 fusion.10
  14.8 80.9 %all-gather.4.cloned.1.call-done = bf16[2048,1024]{1,0:T(8,128)(2,1)} async-done(((bf16[512,1024]{1,0:T(8,128)(2,1)}), bf16[2048,1024]{1,0:T(8,128)(2,1)}) %all-gather.4.cloned.1.call-update) | async-done | bytes 4194320 | tf_op jit(solution)/shard_map/all_gather | solution.py:626
  98.6 2.9 collective-permute-start.10
  101.5 11.0 %collective-permute-done.8 = bf16[128,256]{1,0:T(8,128)(2,1)S(1)} collective-permute-done((bf16[128,256]{1,0:T(8,128)(2,1)S(1)}, bf16[128,256]{1,0:T(8,128)(2,1)S(1)}, u32[]{:S(2)}, u32[]{:S(2)}) %collective-permute-start.8) | collective-permute-done | bytes 65568 | tf_op jit(solution)/shard_map/ppermute | solution.py:581
  112.5 14.5 %collective-permute-done.9 = bf16[128,256]{1,0:T(8,128)(2,1)S(1)} collective-permute-done((bf16[128,256]{1,0:T(8,128)(2,1)S(1)}, bf16[128,256]{1,0:T(8,128)(2,1)S(1)}, u32[]{:S(2)}, u32[]{:S(2)}) %collective-permute-start.9) | collective-permute-done | bytes 65568 | tf_op jit(solution)/shard_map/ppermute | solution.py:581
  132.3 7.3 %convolution_convert_fusion.q_ref.k_ref.v_ref = bf16[2048,768]{1,0:T(8,128)(2,1)} fusion(bf16[2048,1024]{1,0:T(8,128)(2,1)} %all-gather.4.cloned.1.call-done, bf16[1024,768]{1,0:T(8,128)(2,1)S(1)} %constant_dynamic-update-slice_fusion), kind=kOutput, calls=%fused_computation.5 | convolution fusion | flops 3222798336 | bytes 8912896 | tf_op jit(solution)/shard_map/dot_general | solution.py:19
  140.0 2.5 collective-permute-start.3
  142.5 2.5 collective-permute-start.4
  145.0 51.4 %attention_forward.1 = (bf16[2048,256]{1,0:T(8,128)(2,1)}, f32[2048,256]{1,0:T(8,128)}, bf16[4,2048,2048]{2,1,0:T(8,128)(2,1)}, s16[2048,2048]{1,0:T(8,128)(2,1)}) custom-call(s32[1,4]{1,0:T(1,128)} %len_ref.5, bf16[2048,768]{1,0:T(8,128)(2,1)} %convolution_convert_fusion.q_ref.k_ref.v_ref, bf16[2048,768]{1,0:T(8,128)(2,1)} %convolution_convert_fusion.q_ref.k_ref.v_ref, ...), custom_call_target="tpu_custom_call" | custom-call | flops 4294967296 | bytes 157286400 | tf_op jit(solution)/shard_map/attention_forward/pallas_call | solution.py:187
  199.4 3.1 collective-permute-start.7
  202.5 7.3 %collective-permute-done.5 = bf16[512,256]{1,0:T(8,128)(2,1)S(1)} collective-permute-done((bf16[512,256]{1,0:T(8,128)(2,1)S(1)}, bf16[512,256]{1,0:T(8,128)(2,1)S(1)}, u32[]{:S(2)}, u32[]{:S(2)}) %collective-permute-start.5) | collective-permute-done | bytes 262176 | tf_op jit(solution)/shard_map/ppermute | solution.py:581
  209.8 8.1 %collective-permute-done.6 = bf16[512,256]{1,0:T(8,128)(2,1)S(1)} collective-permute-done((bf16[512,256]{1,0:T(8,128)(2,1)S(1)}, bf16[512,256]{1,0:T(8,128)(2,1)S(1)}, u32[]{:S(2)}, u32[]{:S(2)}) %collective-permute-start.6) | collective-permute-done | bytes 262176 | tf_op jit(solution)/shard_map/ppermute | solution.py:581
  217.9 3.4 multiply_reduce_fusion.2
  221.5 5.3 collective-permute-start.11
  228.9 15.7 %feed_forward.2 = (bf16[512,704]{1,0:T(8,128)(2,1)}, bf16[512,704]{1,0:T(8,128)(2,1)}, bf16[512,704]{1,0:T(8,128)(2,1)}, bf16[512,704]{1,0:T(8,128)(2,1)}, bf16[...) custom-call(bf16[512,1024]{1,0:T(8,128)(2,1)} %copy-done.12, bf16[512,1024]{1,0:T(8,128)(2,1)} %refs_2_.1, ...), custom_call_target="tpu_custom_call" | custom-call | flops 7381975040 | bytes 14680064 | tf_op jit(solution)/shard_map/feed_forward/pallas_call | solution.py:500
  244.7 4.7 collective-permute-done.11.x_ref.refs_1_
  250.3 15.4 %feed_forward.3 = (bf16[512,704]{1,0:T(8,128)(2,1)}, bf16[512,704]{1,0:T(8,128)(2,1)}, bf16[512,704]{1,0:T(8,128)(2,1)}, bf16[512,704]{1,0:T(8,128)(2,1)}, bf16[...) custom-call(bf16[512,1024]{1,0:T(8,128)(2,1)} %copy-done.25, bf16[512,1024]{1,0:T(8,128)(2,1)} %copy-done.24, ...), custom_call_target="tpu_custom_call" | custom-call | flops 7381975040 | bytes 14680064 | tf_op jit(solution)/shard_map/feed_forward/pallas_call | solution.py:500
  269.2 17.0 %weight_grads.1 = bf16[1024,5632]{1,0:T(8,128)(2,1)} custom-call(bf16[512,1024]{1,0:T(8,128)(2,1)} %copy-done.12, bf16[512,1024]{1,0:T(8,128)(2,1)} %copy-done.25, bf16[512,1024]{1,0:T(8,128)(2,1)} %refs_2_.1, bf16[512,1024]{1,0:T(8,128)(2,1)} %copy-done.24, bf16[512,704]{1,0:T(8,128)(2,1)} %get-tuple-element.82.refs_4_, ...), custom_call_target="tpu_custom_call" | custom-call | flops 11811160064 | bytes 27262976 | tf_op jit(solution)/shard_map/weight_grads/pallas_call | solution.py:541
  286.2 4.8 collective-permute-done.12
  298.6 2.8 collective-permute-start.14
  308.1 2.7 convert_dynamic-update-slice_fusion
  312.5 9.4 %collective-permute-done.14 = bf16[512,256]{1,0:T(8,128)(2,1)} collective-permute-done((bf16[512,256]{1,0:T(8,128)(2,1)S(1)}, bf16[512,256]{1,0:T(8,128)(2,1)}, u32[]{:S(2)}, u32[]{:S(2)}) %collective-permute-start.14) | collective-permute-done | bytes 262176 | tf_op jit(solution)/shard_map/ppermute | solution.py:581
  324.4 43.3 %attention_backward.1 = (bf16[2048,256]{1,0:T(8,128)(2,1)}, bf16[2048,256]{1,0:T(8,128)(2,1)}, bf16[2048,256]{1,0:T(8,128)(2,1)}, bf16[4,2048,2048]{2,1,0:T(8,128)(2,1)}) custom-call(s32[1,4]{1,0:T(1,128)} %len_ref.5, bf16[2048,768]{1,0:T(8,128)(2,1)} %convolution_convert_fusion.q_ref.k_ref.v_ref, ...), custom_call_target="tpu_custom_call" | custom-call | flops 8589934592 | bytes 157286400 | tf_op jit(solution)/shard_map/attention_backward/pallas_call | solution.py:321
  371.5 4.7 convolution_convert_fusion.1
  376.2 31.0 %reduce-scatter.3.cloned.1.call-done = bf16[128,5632]{1,0:T(8,128)(2,1)} async-done(((bf16[1024,5632]{1,0:T(8,128)(2,1)}), bf16[128,5632]{1,0:T(8,128)(2,1)}) %reduce-scatter.3.cloned.1.call-update) | async-done | bytes 1441808 | tf_op jit(solution)/shard_map/reduce_scatter | solution.py:698
  407.3 3.8 constant_dynamic-slice_fusion.13
  418.5 2.8 add_convert_fusion
  421.4 46.0 %collective-permute-done.24 = bf16[128,256]{1,0:T(8,128)(2,1)S(1)} collective-permute-done((bf16[128,256]{1,0:T(8,128)(2,1)S(1)}, bf16[128,256]{1,0:T(8,128)(2,1)S(1)}, u32[]{:S(2)}, u32[]{:S(2)}) %collective-permute-start.24) | collective-permute-done | bytes 65568 | tf_op jit(solution)/shard_map/ppermute | solution.py:581
  467.5 20.4 %collective-permute-start.26 = (bf16[128,256]{1,0:T(8,128)(2,1)S(1)}, bf16[128,256]{1,0:T(8,128)(2,1)S(1)}, u32[]{:S(2)}, u32[]{:S(2)}) collective-permute-start(bf16[128,256]{1,0:T(8,128)(2,1)S(1)} %get-tuple-element.170), channel_id=1, source_target_pairs={{0,1},{1,2},{2,3},{3,0},{4,5},{5,6},{6,7},{7,4},{8,9},{9,10},{10,1... | collective-permute-start | bytes 196616 | tf_op jit(solution)/shard_map/ppermute | solution.py:581
  488.6 56.8 %table_grads.1 = (f32[256,256]{1,0:T(8,128)}, f32[128,256]{1,0:T(8,128)}) custom-call(s32[1,4]{1,0:T(1,128)} %len_ref.5, bf16[4,2048,2048]{2,1,0:T(8,128)(2,1)} %get-tuple-element.121.ds_ref, s16[2048,2048]{1,0:T(8,128)(2,1)} %get-tuple-element.122.code_ref), custom_call_target="tpu_custom_call" | custom-call | flops 8589934592 | bytes 157286400 | tf_op jit(solution)/shard_map/table_grads/pallas_call | solution.py:409
  556.1 7.3 %fusion.14 = (f32[512]{0:T(512)S(1)}, f32[512,1024]{1,0:T(8,128)S(1)}) fusion(bf16[512,1024]{1,0:T(8,128)(2,1)S(1)} %copy-done.3, f32[1024]{0:T(1024)S(1)} %convert_element_type.123, bf16[1024,3072]{1,0:T(8,128)(2,1)} %all-gather.8.cloned.1.call-done, bf16[512,768]{1,0:T(8,128)(2,1)} %collective-permute-done.19, ...), kind=kOutput, calls=%fused_computation.21 | convolution fusion | flops 3235905024 | bytes 12589056 | tf_op jit(solution)/shard_map/dot_general | solution.py:564
  568.4 2.9 collective-permute-start.23
  (214 shorter events, 75.6 us)
Async XLA Ops:
  7.2 88.4 %all-gather.4.cloned.1.call-start = ((), (), s32[]{:S(2)}) async-start(), calls=%async_computation.2 | async-start | bytes 5242880 | tf_op jit(solution)/shard_map/all_gather | solution.py:626
  12.0 205.9 %all-gather.6.cloned.1.call-start = ((), (), s32[]{:S(2)}) async-start(), calls=%async_computation.3 | async-start | bytes 7667712 | tf_op jit(solution)/shard_map/all_gather | solution.py:639
  95.6 31.3 %collective-permute-start = (bf16[128,2304]{1,0:T(8,128)(2,1)S(1)}, bf16[128,2304]{1,0:T(8,128)(2,1)S(1)}, u32[]{:S(2)}, u32[]{:S(2)}) collective-permute-start(bf16[128,2304]{1,0:T(8,128)(2,1)S(1)} %fusion.31), channel_id=1, source_target_pairs={{0,2},{1,3},{2,0},{3,1},{4,6},{5,7},{6,4},{7,5},{8,10},{9,11},{10,... | collective-permute-start | bytes 1769480 | tf_op jit(solution)/shard_map/ppermute | solution.py:581
  96.6 15.9 %collective-permute-start.8 = (bf16[128,256]{1,0:T(8,128)(2,1)S(1)}, bf16[128,256]{1,0:T(8,128)(2,1)S(1)}, u32[]{:S(2)}, u32[]{:S(2)}) collective-permute-start(bf16[128,256]{1,0:T(8,128)(2,1)S(1)} %bitcast.60), channel_id=1, source_target_pairs={{0,1},{1,2},{2,3},{3,0},{4,5},{5,6},{6,7},{7,4},{8,9},{9,10},{10,1... | collective-permute-start | bytes 196616 | tf_op jit(solution)/shard_map/ppermute | solution.py:581
  96.8 30.1 %collective-permute-start.9 = (bf16[128,256]{1,0:T(8,128)(2,1)S(1)}, bf16[128,256]{1,0:T(8,128)(2,1)S(1)}, u32[]{:S(2)}, u32[]{:S(2)}) collective-permute-start(bf16[128,256]{1,0:T(8,128)(2,1)S(1)} %bitcast.61), channel_id=1, source_target_pairs={{0,2},{1,3},{2,0},{3,1},{4,6},{5,7},{6,4},{7,5},{8,10},{9,11},{10,... | collective-permute-start | bytes 196616 | tf_op jit(solution)/shard_map/ppermute | solution.py:581
  98.6 28.4 %collective-permute-start.10 = (bf16[128,256]{1,0:T(8,128)(2,1)S(1)}, bf16[128,256]{1,0:T(8,128)(2,1)S(1)}, u32[]{:S(2)}, u32[]{:S(2)}) collective-permute-start(bf16[128,256]{1,0:T(8,128)(2,1)S(1)} %bitcast.62), channel_id=1, source_target_pairs={{0,3},{1,0},{2,1},{3,2},{4,7},{5,4},{6,5},{7,6},{8,11},{9,8},{10,9... | collective-permute-start | bytes 196616 | tf_op jit(solution)/shard_map/ppermute | solution.py:581
  128.0 196.2 %all-gather.8.cloned.1.call-start = ((), (), s32[]{:S(2)}) async-start(), calls=%async_computation.4 | async-start | bytes 7077888 | tf_op jit(solution)/shard_map/all_gather | solution.py:649
  130.4 66.0 %collective-permute-start.1 = (bf16[512,1024]{1,0:T(8,128)(2,1)S(1)}, bf16[512,1024]{1,0:T(8,128)(2,1)S(1)}, u32[]{:S(2)}, u32[]{:S(2)}) collective-permute-start(bf16[512,1024]{1,0:T(8,128)(2,1)S(1)} %copy-done.9), channel_id=1, source_target_pairs={{0,1},{1,0},{2,3},{3,2},{4,5},{5,4},{6,7},{7,6},{8,9},{9,8},{10,11... | collective-permute-start | bytes 3145736 | tf_op jit(solution)/shard_map/ppermute | solution.py:585
  139.6 56.8 %collective-permute-start.2 = (bf16[128,768]{1,0:T(8,128)(2,1)S(1)}, bf16[128,768]{1,0:T(8,128)(2,1)S(1)}, u32[]{:S(2)}, u32[]{:S(2)}) collective-permute-start(bf16[128,768]{1,0:T(8,128)(2,1)S(1)} %constant_dynamic-slice_fusion.18), channel_id=1, source_target_pairs={{0,1},{1,2},{2,3},{3,0},{4,5},{5,6},{6,7},{7,4},{8,9},{9,10},{10,1... | collective-permute-start | bytes 589832 | tf_op jit(solution)/shard_map/ppermute | solution.py:581
  140.0 56.4 %collective-permute-start.3 = (bf16[128,768]{1,0:T(8,128)(2,1)S(1)}, bf16[128,768]{1,0:T(8,128)(2,1)S(1)}, u32[]{:S(2)}, u32[]{:S(2)}) collective-permute-start(bf16[128,768]{1,0:T(8,128)(2,1)S(1)} %constant_dynamic-slice_fusion.18), channel_id=1, source_target_pairs={{0,2},{1,3},{2,0},{3,1},{4,6},{5,7},{6,4},{7,5},{8,10},{9,11},{10,... | collective-permute-start | bytes 589832 | tf_op jit(solution)/shard_map/ppermute | solution.py:581
  142.5 53.9 %collective-permute-start.4 = (bf16[128,768]{1,0:T(8,128)(2,1)S(1)}, bf16[128,768]{1,0:T(8,128)(2,1)S(1)}, u32[]{:S(2)}, u32[]{:S(2)}) collective-permute-start(bf16[128,768]{1,0:T(8,128)(2,1)S(1)} %constant_dynamic-slice_fusion.18), channel_id=1, source_target_pairs={{0,3},{1,0},{2,1},{3,2},{4,7},{5,4},{6,5},{7,6},{8,11},{9,8},{10,9... | collective-permute-start | bytes 589832 | tf_op jit(solution)/shard_map/ppermute | solution.py:581
  198.4 208.7 %reduce-scatter.3.cloned.1.call-start = ((), (), s32[]{:S(2)}) async-start(), calls=%async_computation.5 | async-start | bytes 12976128 | tf_op jit(solution)/shard_map/reduce_scatter | solution.py:698
  198.6 11.1 %collective-permute-start.5 = (bf16[512,256]{1,0:T(8,128)(2,1)S(1)}, bf16[512,256]{1,0:T(8,128)(2,1)S(1)}, u32[]{:S(2)}, u32[]{:S(2)}) collective-permute-start(bf16[512,256]{1,0:T(8,128)(2,1)S(1)} %get-tuple-element.179), channel_id=1, source_target_pairs={{0,1},{1,2},{2,3},{3,0},{4,5},{5,6},{6,7},{7,4},{8,9},{9,10},{10,1... | collective-permute-start | bytes 786440 | tf_op jit(solution)/shard_map/ppermute | solution.py:581
  198.7 19.2 %collective-permute-start.6 = (bf16[512,256]{1,0:T(8,128)(2,1)S(1)}, bf16[512,256]{1,0:T(8,128)(2,1)S(1)}, u32[]{:S(2)}, u32[]{:S(2)}) collective-permute-start(bf16[512,256]{1,0:T(8,128)(2,1)S(1)} %get-tuple-element.178), channel_id=1, source_target_pairs={{0,2},{1,3},{2,0},{3,1},{4,6},{5,7},{6,4},{7,5},{8,10},{9,11},{10,... | collective-permute-start | bytes 786440 | tf_op jit(solution)/shard_map/ppermute | solution.py:581
  199.4 18.5 %collective-permute-start.7 = (bf16[512,256]{1,0:T(8,128)(2,1)S(1)}, bf16[512,256]{1,0:T(8,128)(2,1)}, u32[]{:S(2)}, u32[]{:S(2)}) collective-permute-start(bf16[512,256]{1,0:T(8,128)(2,1)S(1)} %get-tuple-element.177), channel_id=1, source_target_pairs={{0,3},{1,0},{2,1},{3,2},{4,7},{5,4},{6,5},{7,6},{8,11},{9,8},{10,9... | collective-permute-start | bytes 786440 | tf_op jit(solution)/shard_map/ppermute | solution.py:581
  221.5 27.8 %collective-permute-start.11 = (bf16[512,1024]{1,0:T(8,128)(2,1)S(1)}, bf16[512,1024]{1,0:T(8,128)(2,1)S(1)}, u32[]{:S(2)}, u32[]{:S(2)}) collective-permute-start(bf16[512,1024]{1,0:T(8,128)(2,1)S(1)} %multiply_convert_fusion.x_ref.refs_0_), channel_id=1, source_target_pairs={{0,1},{1,0},{2,3},{3,2},{4,5},{5,4},{6,7},{7,6},{8,9},{9,8},{10,11... | collective-permute-start | bytes 3145736 | tf_op jit(solution)/shard_map/ppermute | solution.py:585
  267.4 23.6 %collective-permute-start.12 = (bf16[512,1024]{1,0:T(8,128)(2,1)S(1)}, bf16[512,1024]{1,0:T(8,128)(2,1)S(1)}, u32[]{:S(2)}, u32[]{:S(2)}) collective-permute-start(bf16[512,1024]{1,0:T(8,128)(2,1)S(1)} %convert_element_type.132), channel_id=1, source_target_pairs={{0,1},{1,0},{2,3},{3,2},{4,5},{5,4},{6,7},{7,6},{8,9},{9,8},{10,11... | collective-permute-start | bytes 3145736 | tf_op jit(solution)/shard_map/ppermute | solution.py:585
  298.5 12.3 %collective-permute-start.13 = (bf16[512,256]{1,0:T(8,128)(2,1)S(1)}, bf16[512,256]{1,0:T(8,128)(2,1)}, u32[]{:S(2)}, u32[]{:S(2)}) collective-permute-start(bf16[512,256]{1,0:T(8,128)(2,1)S(1)} %get-tuple-element.174), channel_id=1, source_target_pairs={{0,3},{1,0},{2,1},{3,2},{4,7},{5,4},{6,5},{7,6},{8,11},{9,8},{10,9... | collective-permute-start | bytes 786440 | tf_op jit(solution)/shard_map/ppermute | solution.py:581
  298.6 23.2 %collective-permute-start.14 = (bf16[512,256]{1,0:T(8,128)(2,1)S(1)}, bf16[512,256]{1,0:T(8,128)(2,1)}, u32[]{:S(2)}, u32[]{:S(2)}) collective-permute-start(bf16[512,256]{1,0:T(8,128)(2,1)S(1)} %get-tuple-element.173), channel_id=1, source_target_pairs={{0,2},{1,3},{2,0},{3,1},{4,6},{5,7},{6,4},{7,5},{8,10},{9,11},{10,... | collective-permute-start | bytes 786440 | tf_op jit(solution)/shard_map/ppermute | solution.py:581
  301.4 22.1 %collective-permute-start.15 = (bf16[512,256]{1,0:T(8,128)(2,1)S(1)}, bf16[512,256]{1,0:T(8,128)(2,1)S(1)}, u32[]{:S(2)}, u32[]{:S(2)}) collective-permute-start(bf16[512,256]{1,0:T(8,128)(2,1)S(1)} %get-tuple-element.172), channel_id=1, source_target_pairs={{0,1},{1,2},{2,3},{3,0},{4,5},{5,6},{6,7},{7,4},{8,9},{9,10},{10,1... | collective-permute-start | bytes 786440 | tf_op jit(solution)/shard_map/ppermute | solution.py:581
  324.3 226.1 %reduce-scatter.5.cloned.1.call-start = ((), (), s32[]{:S(2)}) async-start(), calls=%async_computation.6 | async-start | bytes 1769472 | tf_op jit(solution)/shard_map/reduce_scatter | solution.py:709
  324.3 45.5 %collective-permute-start.16 = (bf16[512,1024]{1,0:T(8,128)(2,1)}, bf16[512,1024]{1,0:T(8,128)(2,1)}, u32[]{:S(2)}, u32[]{:S(2)}) collective-permute-start(bf16[512,1024]{1,0:T(8,128)(2,1)} %add_convert_fusion.1), channel_id=1, source_target_pairs={{0,1},{1,0},{2,3},{3,2},{4,5},{5,4},{6,7},{7,6},{8,9},{9,8},{10,11... | collective-permute-start | bytes 3145736 | tf_op jit(solution)/shard_map/ppermute | solution.py:585
  411.1 140.3 %collective-permute-start.17 = (bf16[512,768]{1,0:T(8,128)(2,1)}, bf16[512,768]{1,0:T(8,128)(2,1)}, u32[]{:S(2)}, u32[]{:S(2)}) collective-permute-start(bf16[512,768]{1,0:T(8,128)(2,1)} %get-tuple-element.167), channel_id=1, source_target_pairs={{0,1},{1,2},{2,3},{3,0},{4,5},{5,6},{6,7},{7,4},{8,9},{9,10},{10,1... | collective-permute-start | bytes 2359304 | tf_op jit(solution)/shard_map/ppermute | solution.py:581
  412.6 138.8 %collective-permute-start.18 = (bf16[512,768]{1,0:T(8,128)(2,1)}, bf16[512,768]{1,0:T(8,128)(2,1)}, u32[]{:S(2)}, u32[]{:S(2)}) collective-permute-start(bf16[512,768]{1,0:T(8,128)(2,1)} %get-tuple-element.166), channel_id=1, source_target_pairs={{0,2},{1,3},{2,0},{3,1},{4,6},{5,7},{6,4},{7,5},{8,10},{9,11},{10,... | collective-permute-start | bytes 2359304 | tf_op jit(solution)/shard_map/ppermute | solution.py:581
  415.0 136.4 %collective-permute-start.19 = (bf16[512,768]{1,0:T(8,128)(2,1)}, bf16[512,768]{1,0:T(8,128)(2,1)}, u32[]{:S(2)}, u32[]{:S(2)}) collective-permute-start(bf16[512,768]{1,0:T(8,128)(2,1)} %get-tuple-element.165), channel_id=1, source_target_pairs={{0,3},{1,0},{2,1},{3,2},{4,7},{5,4},{6,5},{7,6},{8,11},{9,8},{10,9... | collective-permute-start | bytes 2359304 | tf_op jit(solution)/shard_map/ppermute | solution.py:581
  416.4 51.0 %collective-permute-start.24 = (bf16[128,256]{1,0:T(8,128)(2,1)S(1)}, bf16[128,256]{1,0:T(8,128)(2,1)S(1)}, u32[]{:S(2)}, u32[]{:S(2)}) collective-permute-start(bf16[128,256]{1,0:T(8,128)(2,1)S(1)} %get-tuple-element.169), channel_id=1, source_target_pairs={{0,3},{1,0},{2,1},{3,2},{4,7},{5,4},{6,5},{7,6},{8,11},{9,8},{10,9... | collective-permute-start | bytes 196616 | tf_op jit(solution)/shard_map/ppermute | solution.py:581
  417.0 71.6 %collective-permute-start.25 = (bf16[128,256]{1,0:T(8,128)(2,1)S(1)}, bf16[128,256]{1,0:T(8,128)(2,1)S(1)}, u32[]{:S(2)}, u32[]{:S(2)}) collective-permute-start(bf16[128,256]{1,0:T(8,128)(2,1)S(1)} %get-tuple-element.171), channel_id=1, source_target_pairs={{0,2},{1,3},{2,0},{3,1},{4,6},{5,7},{6,4},{7,5},{8,10},{9,11},{10,... | collective-permute-start | bytes 196616 | tf_op jit(solution)/shard_map/ppermute | solution.py:581
  467.5 77.9 %collective-permute-start.26 = (bf16[128,256]{1,0:T(8,128)(2,1)S(1)}, bf16[128,256]{1,0:T(8,128)(2,1)S(1)}, u32[]{:S(2)}, u32[]{:S(2)}) collective-permute-start(bf16[128,256]{1,0:T(8,128)(2,1)S(1)} %get-tuple-element.170), channel_id=1, source_target_pairs={{0,1},{1,2},{2,3},{3,0},{4,5},{5,6},{6,7},{7,4},{8,9},{9,10},{10,1... | collective-permute-start | bytes 196616 | tf_op jit(solution)/shard_map/ppermute | solution.py:581
  488.6 57.6 %collective-permute-start.20 = (bf16[128,2304]{1,0:T(8,128)(2,1)S(1)}, bf16[128,2304]{1,0:T(8,128)(2,1)S(1)}, u32[]{:S(2)}, u32[]{:S(2)}) collective-permute-start(bf16[128,2304]{1,0:T(8,128)(2,1)S(1)} %slice.107), channel_id=1, source_target_pairs={{0,2},{1,3},{2,0},{3,1},{4,6},{5,7},{6,4},{7,5},{8,10},{9,11},{10,... | collective-permute-start | bytes 1769480 | tf_op jit(solution)/shard_map/ppermute | solution.py:581
  556.1 15.2 %collective-permute-start.27 = (f32[4,12,4]{1,0,2:T(4,128)S(1)}, f32[4,12,4]{1,0,2:T(4,128)S(1)}, u32[]{:S(2)}, u32[]{:S(2)}) collective-permute-start(f32[4,12,4]{1,0,2:T(4,128)S(1)} %fusion.33), channel_id=1, source_target_pairs={{0,16},{4,20},{8,24},{12,28},{16,0},{20,4},{24,8},{28,12},{1,17},{... | collective-permute-start | bytes 2312 | tf_op jit(solution)/shard_map/ppermute | solution.py:727
  565.4 6.0 %collective-permute-start.21 = (f32[2,32]{1,0:T(2,128)S(1)}, f32[2,32]{1,0:T(2,128)S(1)}, u32[]{:S(2)}, u32[]{:S(2)}) collective-permute-start(f32[2,32]{1,0:T(2,128)S(1)} %get-tuple-element.189), channel_id=1, source_target_pairs={{0,1},{1,2},{2,3},{3,0},{4,5},{5,6},{6,7},{7,4},{8,9},{9,10},{10,1... | collective-permute-start | bytes 776 | tf_op jit(solution)/shard_map/ppermute | solution.py:581
  566.0 5.4 collective-permute-start.22
  (34 other events, 383.2 us)
Sparse Core Ops, SparseCore 0:
  12.1 83.4 all-gather.3
  128.1 49.3 all-gather.5
  198.5 41.9 all-gather.7
  324.4 82.6 reduce-scatter.2
  410.8 38.4 reduce-scatter.4

commit v4 on v3

--- a/solution.py
+++ b/solution.py
@@ -71,10 +71,11 @@
 
 
 def forward_kernel(len_ref, q_ref, k_ref, v_ref, rel_ref, lay_ref, tab_ref, kmask_ref,
-                   att_ref, rinv_ref, e_ref, code_ref,
-                   s_scr, m_scr, acc_scr, vext, colcode, knorm, *, width, heads, group):
+                   att_ref, rinv_ref, e_ref, *rest, width, group, pair):
+    code_ref = rest[0] if len(rest) == 7 else None
+    s_scr, m_scr, acc_scr, vext, colcode, knorm = rest[-6:]
     tq, count = rel_ref.shape
-    pairs = heads // 2
+    heads, pairs = 2, 1
     i = pl.program_id(0)
     t0 = i * tq
     ends, base, steps = key_window(len_ref, t0, t0 + tq - 1, count, width)
@@ -102,7 +103,7 @@
         scaled.append(jnp.where(own_half(qp.shape, h), qp * bf16(BIAS_SCALE), jnp.zeros_like(qp)))
         if h % 2 == 0:
             largest = jnp.maximum(largest, half_norms(qp) * knorm[h // 2])
-    tabs = [[jnp.broadcast_to(tab_ref[2 * p + r:2 * p + r + 1, :], (tq, 128)) for r in range(2)]
+    tabs = [[jnp.broadcast_to(tab_ref[2 * (pair + p) + r:2 * (pair + p) + r + 1, :], (tq, 128)) for r in range(2)]
             for p in range(pairs)]
 
     def scores(c0, width, use):
@@ -112,7 +113,8 @@
             cc = pl.multiple_of(c0 + half * 128, 128)
             rel = rel_ref[:, pl.ds(cc, 128)]
             lay = lay_ref[:, pl.ds(cc, 128)]
-            code_ref[:, pl.ds(cc, 128)] = (rel + lay * 32).astype(jnp.int16)
+            if code_ref is not None:
+                code_ref[:, pl.ds(cc, 128)] = (rel + lay * 32).astype(jnp.int16)
             col = jnp.broadcast_to(colcode[0:1, pl.ds(cc, 128)], (tq, 128))
             seen = (rowpage == col) | (rowpos == lanes + cc)
             hide = jnp.where(seen, f32(0.0), f32(-1e30))
@@ -179,47 +181,44 @@
         rinv_ref[:, p * 128:(p + 1) * 128] = rinv
 
 
-def attention_forward(page_lengths, proj, rel, lay, tab, kmask, tq=256, width=256, group=1):
+def attention_forward(page_lengths, proj, rel, lay, tab, kmask, pair, tq=256, width=256, group=1):
     count = proj.shape[0]
-    hc = proj.shape[1] // 3
-    heads = hc // DH
-    grid = (count // tq,)
+    pairs = proj.shape[1] // (3 * 128)
+    tile = lambda i: (i, 0)
     return pl.pallas_call(
-        functools.partial(forward_kernel, width=width, heads=heads, group=group),
-        grid=grid,
+        functools.partial(forward_kernel, width=width, group=group, pair=pair),
+        grid=(count // tq,),
         in_specs=[
             pl.BlockSpec(memory_space=pltpu.SMEM),
-            pl.BlockSpec((tq, hc), lambda i: (i, 0)),
-            pl.BlockSpec((count, hc), lambda i: (0, 1)),
-            pl.BlockSpec((count, hc), lambda i: (0, 2)),
-            pl.BlockSpec((tq, count), lambda i: (i, 0)),
-            pl.BlockSpec((tq, count), lambda i: (i, 0)),
+            pl.BlockSpec((tq, 128), lambda i: (i, pair)),
+            pl.BlockSpec((count, 128), lambda i: (0, pairs + pair)),
+            pl.BlockSpec((count, 128), lambda i: (0, 2 * pairs + pair)),
+            pl.BlockSpec((tq, count), tile),
+            pl.BlockSpec((tq, count), tile),
             pl.BlockSpec(tab.shape, lambda i: (0, 0)),
             pl.BlockSpec((1, count), lambda i: (0, 0)),
         ],
         out_specs=[
-            pl.BlockSpec((tq, hc), lambda i: (i, 0)),
-            pl.BlockSpec((tq, hc), lambda i: (i, 0)),
-            pl.BlockSpec((heads, tq, count), lambda i: (0, i, 0)),
-            pl.BlockSpec((tq, count), lambda i: (i, 0)),
-        ],
+            pl.BlockSpec((tq, 128), tile),
+            pl.BlockSpec((tq, 128), tile),
+            pl.BlockSpec((2, tq, count), lambda i: (0, i, 0)),
+        ] + [pl.BlockSpec((tq, count), tile)] * (pair == 0),
         out_shape=[
-            jax.ShapeDtypeStruct((count, hc), bf16),
-            jax.ShapeDtypeStruct((count, hc), f32),
-            jax.ShapeDtypeStruct((heads, count, count), bf16),
-            jax.ShapeDtypeStruct((count, count), jnp.int16),
-        ],
+            jax.ShapeDtypeStruct((count, 128), bf16),
+            jax.ShapeDtypeStruct((count, 128), f32),
+            jax.ShapeDtypeStruct((2, count, count), bf16),
+        ] + [jax.ShapeDtypeStruct((count, count), jnp.int16)] * (pair == 0),
         scratch_shapes=[
-            pltpu.VMEM((heads, tq, count), f32),
-            pltpu.VMEM((heads, tq, 128), f32),
-            pltpu.VMEM((heads, tq, 128), f32),
-            pltpu.VMEM((heads, count, 128), bf16),
+            pltpu.VMEM((2, tq, count), f32),
+            pltpu.VMEM((2, tq, 128), f32),
+            pltpu.VMEM((2, tq, 128), f32),
+            pltpu.VMEM((2, count, 128), bf16),
             pltpu.VMEM((8, count), jnp.int32),
-            pltpu.SMEM((heads // 2,), f32),
+            pltpu.SMEM((1,), f32),
         ],
         compiler_params=pltpu.CompilerParams(vmem_limit_bytes=56 << 20),
         cost_estimate=pl.CostEstimate(
-            flops=heads * count * count * 256, bytes_accessed=150 << 20, transcendentals=heads * count * count // 2),
+            flops=count * count * 512, bytes_accessed=80 << 20, transcendentals=count * count),
         name="attention_forward",
     )(page_lengths, proj, proj, proj, rel, lay, tab, kmask.reshape(1, count))
 
@@ -247,12 +246,13 @@
     return out
 
 
-def backward_kernel(len_ref, q_ref, k_ref, v_ref, e_ref, da_ref, att_ref, rinv_ref,
-                    dq_ref, dk_ref, dv_ref, ds_ref,
-                    vext, lhs_scr, dat_scr, qt_scr, dq_scr, dkt, dvt, *, width, heads, group):
+def backward_kernel(len_ref, q_ref, k_ref, v_ref, da_ref, *refs, width, heads, group):
     tq = q_ref.shape[0]
     count = k_ref.shape[0]
     pairs = heads // 2
+    e_refs, att_refs, rinv_refs = refs[:pairs], refs[pairs:2 * pairs], refs[2 * pairs:3 * pairs]
+    dq_ref, dk_ref, dv_ref, ds_ref = refs[3 * pairs:3 * pairs + 4]
+    vext, lhs_scr, dat_scr, qt_scr, dq_scr, dkt, dvt = refs[3 * pairs + 4:]
     i = pl.program_id(0)
     t0 = i * tq
     ends, base, steps = key_window(len_ref, t0, t0 + tq - 1, count, width)
@@ -268,9 +268,9 @@
     first_part = (lane & 32) == 0
     for p in range(pairs):
         cols = slice(p * 128, (p + 1) * 128)
-        da = (da_ref[:, cols].astype(f32) * rinv_ref[:, cols]).astype(bf16)
+        da = (da_ref[:, cols].astype(f32) * rinv_refs[p][...]).astype(bf16)
         daf = da.astype(f32)
-        prod = daf * att_ref[:, cols].astype(f32)
+        prod = daf * att_refs[p][...].astype(f32)
         for r in range(2):
             own = low if r == 0 else jnp.logical_not(low)
             delta = jnp.sum(jnp.where(own, prod, 0.0), axis=1, keepdims=True) * f32(-1.0 / 32)
@@ -289,7 +289,7 @@
             for r in range(2):
                 h = 2 * p + r
                 rows = slice(r * DH, (r + 1) * DH)
-                e = e_ref[h, :, here]
+                e = e_refs[p][r, :, here]
                 d = dot(lhs_scr[h], vext[h, here, :], NT)
                 ds = (e.astype(f32) * d).astype(bf16)
                 ds_ref[h, :, here] = ds
@@ -310,7 +310,7 @@
                 dv_ref[c:c + 256, p * 128:(p + 1) * 128] = dvt[p, :, c:c + 256].T.astype(bf16)
 
 
-def attention_backward(page_lengths, proj, e, d_att, att, rinv, tq=256, width=256, group=2):
+def attention_backward(page_lengths, proj, exps, d_att, atts, rinvs, tq=256, width=256, group=2):
     count = proj.shape[0]
     hc = proj.shape[1] // 3
     heads = hc // DH
@@ -326,11 +326,8 @@
             pl.BlockSpec((tq, hc), tile),
             pl.BlockSpec((count, hc), lambda i: (0, 1)),
             pl.BlockSpec((count, hc), lambda i: (0, 2)),
-            pl.BlockSpec((heads, tq, count), lambda i: (0, i, 0)),
             pl.BlockSpec((tq, hc), tile),
-            pl.BlockSpec((tq, hc), tile),
-            pl.BlockSpec((tq, hc), tile),
-        ],
+        ] + [pl.BlockSpec((2, tq, count), lambda i: (0, i, 0))] * pairs + [pl.BlockSpec((tq, 128), tile)] * (2 * pairs),
         out_specs=[
             pl.BlockSpec((tq, hc), tile),
             pl.BlockSpec((count, hc), fixed),
@@ -356,7 +353,7 @@
         cost_estimate=pl.CostEstimate(
             flops=heads * count * count * 512, bytes_accessed=150 << 20, transcendentals=0),
         name="attention_backward",
-    )(page_lengths, proj, proj, proj, e, d_att, att, rinv)
+    )(page_lengths, proj, proj, proj, d_att, *exps, *atts, *rinvs)
 
 
 def table_kernel(len_ref, ds_ref, code_ref, hl_ref, hr_ref, *bufs, width, parts):
@@ -633,22 +630,40 @@
     out_piece = lax.dynamic_slice_in_dim(w_out, my_wide * part, part, 1).T
     ffn_piece = jnp.concatenate(
         [jnp.pad(piece, ((0, 0), (0, padded - units))) for piece in (own_rows_gate, own_rows_up, down_piece)], axis=1)
-    normed_attn_all, out_piece, ffn_piece = lax.optimization_barrier((normed_attn_all, out_piece, ffn_piece))
+    normed_attn_all, out_piece, ffn_piece, late_grad = lax.optimization_barrier(
+        (normed_attn_all, out_piece, ffn_piece, out_grad))
     ffn_pieces = [along(ffn_piece, d, ring) for d in range(2, ring, 2)]
     out_pieces = [out_piece] + [along(out_piece, d, ring) for d in range(1, ring)]
-    w_first = lax.all_gather(jnp.concatenate(out_pieces + ffn_pieces, axis=1), "wide", axis=0, tiled=True)
-    late_project, late_grad, ffn_pieces = lax.optimization_barrier((own_rows_project, out_grad, ffn_pieces))
+    other_grad = swap(late_grad, ring)
+
+    projected = dot(normed_attn_all, w_project).astype(bf16)
+    words = bias_words(rel_table, layout_table)
+    pairs = head_cols // 128
+    bucket_args = (rel_bucket, layout_bucket, words, key_mask)
+    *first_pair, codes = attention_forward(page_lengths, projected, *bucket_args, 0)
+    first_pair[0], out_pieces, ffn_pieces, other_grad, late_project = lax.optimization_barrier(
+        (first_pair[0], out_pieces, ffn_pieces, other_grad, own_rows_project))
+    first_weights = jnp.concatenate(out_pieces + ffn_pieces, axis=1)
+
+    def to_owners(a):
+        return [rows_of(a, me, tokens)] + [
+            along(rows_of(a, (me + d) % ring, tokens), d, ring) for d in range(1, ring)]
+
+    sent = [to_owners(first_pair[0])]
     project_pieces = [own_rows_project] + [along(late_project, d, ring) for d in range(1, ring)]
-    other_grad = swap(late_grad, ring)
+    results = [first_pair]
+    if pairs > 1:
+        late_projected, first_weights = lax.optimization_barrier((projected, first_weights))
+        results += [list(attention_forward(page_lengths, late_projected, *bucket_args, p)) for p in range(1, pairs)]
+    w_first = lax.all_gather(first_weights, "wide", axis=0, tiled=True)
     out_t = w_first[:, : ring * head_cols]
-
-    projected = dot(normed_attn_all, w_project).astype(bf16)
-    attended, rinv, exps, codes = attention_forward(
-        page_lengths, projected, rel_bucket, layout_bucket, bias_words(rel_table, layout_table), key_mask)
-    attended, other_grad, project_pieces = lax.optimization_barrier((attended, other_grad, project_pieces))
+    if pairs > 1:
+        results[1][0], project_pieces, sent[0] = lax.optimization_barrier((results[1][0], project_pieces, sent[0]))
     w_project_all = lax.all_gather(jnp.concatenate(project_pieces, axis=1), "wide", axis=0, tiled=True)
-    mine = [along(rows_of(attended, (me + d) % ring, tokens), d, ring) for d in range(1, ring)]
-    attended_own = jnp.concatenate([rows_of(attended, me, tokens)] + mine, axis=1)
+    attended = [r[0] for r in results]
+    sent += [to_owners(a) for a in attended[1:]]
+    mine = [pieces[d] for d in range(ring) for pieces in sent]
+    attended_own = jnp.concatenate(mine, axis=1)
     middle = resid + contract_cols(attended_own, out_t)
 
     scale_ffn, normed_ffn = norm_rows(middle, gain_ffn)
@@ -699,18 +714,18 @@
     other_out = swap(other_out, ring)
 
     d_query, d_keys, d_values, d_scores = attention_backward(
-        page_lengths, projected, exps, d_attended, attended, rinv)
+        page_lengths, projected, [r[2] for r in results], d_attended, attended, [r[1] for r in results])
     d_project = jnp.concatenate([d_query, d_keys, d_values], axis=1)
     d_project, other_out, middle_late = lax.optimization_barrier((d_project, other_out, middle))
     layer_out = (middle_late + own_out + other_out.astype(f32)).astype(bf16)
     mine = [along(rows_of(d_project, (me + d) % ring, tokens), d, ring) for d in range(1, ring)]
     last_sums = contract_rows(normed_attn_all, d_project).astype(bf16)
-    last_sums, ffn_sums = lax.optimization_barrier((last_sums, ffn_sums))
-    sum_project = lax.psum_scatter(last_sums, "wide", scatter_dimension=0, tiled=True).astype(f32)
 
     last_sums, d_scores = lax.optimization_barrier((last_sums, d_scores))
     raw_lay, raw_rel = table_grads(page_lengths, d_scores, codes)
-    raw_lay, raw_rel, mine, sum_project = lax.optimization_barrier((raw_lay, raw_rel, mine, sum_project))
+    raw_lay, raw_rel, mine, ffn_sums, last_sums = lax.optimization_barrier(
+        (raw_lay, raw_rel, mine, ffn_sums, last_sums))
+    sum_project = lax.psum_scatter(last_sums, "wide", scatter_dimension=0, tiled=True).astype(f32)
     d_project_own = jnp.concatenate([rows_of(d_project, me, tokens)] + mine, axis=1)
     d_normed_attn = contract_cols(d_project_own, w_project_all)
     in_grad = d_middle + norm_back(d_normed_attn, resid, scale_attn, gain_attn)

time: 592 us -> 493 us (0.83)
  waiting for transfers between devices: 223 us -> 104 us
  Pallas kernels: 200 us -> 214 us
  local copies, waits for them, and re-layouts: 27.5 us -> 38.7 us
    ppermute x23 -> x26, waiting for transfers between devices: 98.2 us -> 6 us  [along(): lax.ppermute(array, 'narrow', [(i, (i + shift) % ring) for i in range(rin...]
    reduce_scatter x1, waiting for transfers between devices: 31 us -> 0.02 us  [on_device(): ffn_sums = lax.psum_scatter(sums, 'wide', scatter_dimension=0, tiled=True)]
    reduce_scatter x1, waiting for transfers between devices: 0.01 us -> 18.6 us  [on_device(): lax.psum_scatter(last_sums, 'wide', scatter_dimension=0, tiled=True)]
    pallas_call x1 -> x2, Pallas kernels: 51.4 us -> 69 us  [attention_forward(): pl.pallas_call(functools.partial(forward_kernel, width=width, group=group...]
    ppermute x3, starting transfers between devices: 0.15 us -> 13.4 us  [on_device(): lax.ppermute(give, 'wide', [(i, i ^ reach) for i in range(wide)])]
    ppermute x23 -> x26, starting transfers between devices: 51.7 us -> 41.9 us  [along(): lax.ppermute(array, 'narrow', [(i, (i + shift) % ring) for i in range(rin...]
    ppermute x4, waiting for transfers between devices: 9.47 us -> 0.01 us  [swap(): return lax.ppermute(array, 'narrow', [(i, i ^ 1) for i in range(ring)])]
    unnamed x76 -> x84, local copies, waits for them, and re-layouts: 10.7 us -> 15.8 us
  transfers between devices with their start and end apart: 35 -> 38, of which waited for: 14 -> 8; matrix products, arithmetic and copies ran while one was open for 12% -> 16% of each run, Pallas kernels for 34% -> 44%
where the time goes in v4:
time: 493 us; the launch traced here: 490 us
  Pallas kernels  214 us (43%)
  waiting for transfers between devices  104 us (21%)
  starting transfers between devices  59.8 us (12%)
  local copies, waits for them, and re-layouts  38.7 us (8%)
  matrix products  35.5 us (7%)
  other arithmetic  22.5 us (5%)
  between operations  15.1 us (3%)
    all_gather x1, waiting for transfers between devices, on_device(): normed_attn_all = lax.all_gather(normed_attn, 'narrow', axis=0, tiled=True)  77.6 us
    pallas_call x2, Pallas kernels, attention_forward(): pl.pallas_call(functools.partial(forward_kernel, width=width, group=group...  69 us
    pallas_call x1, Pallas kernels, table_grads(): pl.pallas_call(functools.partial(table_kernel, width=width, parts=parts),...  56.6 us
    ppermute x26, starting transfers between devices, along(): lax.ppermute(array, 'narrow', [(i, (i + shift) % ring) for i in range(rin...  41.9 us
    pallas_call x1, Pallas kernels, attention_backward(): pl.pallas_call(functools.partial(backward_kernel, width=width, heads=head...  40.8 us
    pallas_call x2, Pallas kernels, feed_forward(): pl.pallas_call(functools.partial(feed_forward_kernel, skip, shards), grid...  31.1 us
    reduce_scatter x1, waiting for transfers between devices, on_device(): lax.psum_scatter(last_sums, 'wide', scatter_dimension=0, tiled=True)  18.6 us
    pallas_call x1, Pallas kernels, weight_grads(): pl.pallas_call(functools.partial(weight_grads_kernel, skip, len(lefts) //...  16.8 us
  transfers between devices with their start and end apart: 38, of which 8 were waited for; matrix products, arithmetic and copies ran while one was open for 16% of the time, Pallas kernels for 44%

profile of v4, /device:TPU:0, one launch (start us, length us, event | category | flops | bytes accessed | tf_op | source)
XLA Modules:
  0.0 489.8 jit_solution(3579190026927952597)
XLA Ops:
  10.1 2.5 fusion.10
  18.6 77.6 %all-gather.4.cloned.1.call-done = bf16[2048,1024]{1,0:T(8,128)(2,1)} async-done(((bf16[512,1024]{1,0:T(8,128)(2,1)}), bf16[2048,1024]{1,0:T(8,128)(2,1)}) %all-gather.4.cloned.1.call-update) | async-done | bytes 4194320 | tf_op jit(solution)/shard_map/all_gather | solution.py:623
  97.2 2.1 collective-permute-start
  103.1 7.8 %convolution_convert_fusion.q_ref.k_ref.v_ref = bf16[2048,768]{1,0:T(8,128)(2,1)} fusion(bf16[2048,1024]{1,0:T(8,128)(2,1)} %all-gather.4.cloned.1.call-done, bf16[1024,768]{1,0:T(8,128)(2,1)} %copy-done.15), kind=kOutput, calls=%fused_computation.5 | convolution fusion | flops 3222798336 | bytes 8912896 | tf_op jit(solution)/shard_map/dot_general | solution.py:19
  110.9 35.1 %attention_forward.2 = (bf16[2048,128]{1,0:T(8,128)(2,1)}, f32[2048,128]{1,0:T(8,128)}, bf16[2,2048,2048]{2,1,0:T(8,128)(2,1)}, s16[2048,2048]{1,0:T(8,128)(2,1)}) custom-call(s32[1,4]{1,0:T(1,128)} %len_ref.7, bf16[2048,768]{1,0:T(8,128)(2,1)} %convolution_convert_fusion.q_ref.k_ref.v_ref, bf16[2048,768]{1,0:T(8,128)(2,1)} %convolution_convert_fusion.q_ref.k_ref.v_ref, ...), custom_call_target="tpu_custom_call" | custom-call | flops 2147483648 | bytes 83886080 | tf_op jit(solution)/shard_map/attention_forward/pallas_call | solution.py:188
  151.8 1.9 collective-permute-start.7
  154.8 7.0 %collective-permute-start.9 = (bf16[512,128]{1,0:T(8,128)(2,1)S(1)}, bf16[512,128]{1,0:T(8,128)(2,1)S(1)}, u32[]{:S(2)}, u32[]{:S(2)}) collective-permute-start(bf16[512,128]{1,0:T(8,128)(2,1)S(1)} %get-tuple-element.211), channel_id=1, source_target_pairs={{0,2},{1,3},{2,0},{3,1},{4,6},{5,7},{6,4},{7,5},{8,10},{9,11},{10,... | collective-permute-start | bytes 393224 | tf_op jit(solution)/shard_map/ppermute | solution.py:578
  161.8 33.9 %attention_forward.3 = (bf16[2048,128]{1,0:T(8,128)(2,1)}, f32[2048,128]{1,0:T(8,128)}, bf16[2,2048,2048]{2,1,0:T(8,128)(2,1)}) custom-call(s32[1,4]{1,0:T(1,128)} %len_ref.7, bf16[2048,768]{1,0:T(8,128)(2,1)} %convolution_convert_fusion.q_ref.k_ref.v_ref, bf16[2048,768]{1,0:T(8,128)(2,1)} %convolution_convert_fusion.q_ref.k_ref.v_ref, ...), custom_call_target="tpu_custom_call" | custom-call | flops 2147483648 | bytes 83886080 | tf_op jit(solution)/shard_map/attention_forward/pallas_call | solution.py:188
  199.2 2.9 collective-permute-start.12
  202.7 3.6 collective-permute-done.11
  209.9 3.3 multiply_reduce_fusion.2
  213.5 1.8 collective-permute-start.14
  215.3 15.6 %feed_forward.2 = (bf16[512,704]{1,0:T(8,128)(2,1)}, bf16[512,704]{1,0:T(8,128)(2,1)}, bf16[512,704]{1,0:T(8,128)(2,1)}, bf16[512,704]{1,0:T(8,128)(2,1)}, bf16[...) custom-call(bf16[512,1024]{1,0:T(8,128)(2,1)} %copy-done.11, bf16[512,1024]{1,0:T(8,128)(2,1)} %refs_2_.1, ...), custom_call_target="tpu_custom_call" | custom-call | flops 7381975040 | bytes 14680064 | tf_op jit(solution)/shard_map/feed_forward/pallas_call | solution.py:497
  231.9 15.5 %feed_forward.3 = (bf16[512,704]{1,0:T(8,128)(2,1)}, bf16[512,704]{1,0:T(8,128)(2,1)}, bf16[512,704]{1,0:T(8,128)(2,1)}, bf16[512,704]{1,0:T(8,128)(2,1)}, bf16[...) custom-call(bf16[512,1024]{1,0:T(8,128)(2,1)} %copy-done.26, bf16[512,1024]{1,0:T(8,128)(2,1)} %copy-done.25, ...), custom_call_target="tpu_custom_call" | custom-call | flops 7381975040 | bytes 14680064 | tf_op jit(solution)/shard_map/feed_forward/pallas_call | solution.py:497
  247.4 1.7 convert_element_type.132
  250.1 16.8 %weight_grads.1 = bf16[1024,5632]{1,0:T(8,128)(2,1)} custom-call(bf16[512,1024]{1,0:T(8,128)(2,1)} %copy-done.11, bf16[512,1024]{1,0:T(8,128)(2,1)} %copy-done.26, bf16[512,1024]{1,0:T(8,128)(2,1)} %refs_2_.1, bf16[512,1024]{1,0:T(8,128)(2,1)} %copy-done.25, bf16[512,704]{1,0:T(8,128)(2,1)} %get-tuple-element.109.refs_4_, ...), custom_call_target="tpu_custom_call" | custom-call | flops 11811160064 | bytes 27262976 | tf_op jit(solution)/shard_map/weight_grads/pallas_call | solution.py:538
  268.2 2.0 fusion.91
  274.6 3.2 collective-permute-start.16
  281.9 2.0 add_convert_fusion.1
  283.9 2.3 convolution_add_fusion
  286.2 3.9 convert_dynamic-update-slice_fusion
  298.0 40.8 %attention_backward.1 = (bf16[2048,256]{1,0:T(8,128)(2,1)}, bf16[2048,256]{1,0:T(8,128)(2,1)}, bf16[2048,256]{1,0:T(8,128)(2,1)}, bf16[4,2048,2048]{2,1,0:T(8,128)(2,1)}) custom-call(s32[1,4]{1,0:T(1,128)} %len_ref.7, bf16[2048,768]{1,0:T(8,128)(2,1)} %convolution_convert_fusion.q_ref.k_ref.v_ref, ...), custom_call_target="tpu_custom_call" | custom-call | flops 8589934592 | bytes 157286400 | tf_op jit(solution)/shard_map/attention_backward/pallas_call | solution.py:321
  338.8 2.0 pad_maximum_fusion
  346.7 5.0 %convolution_convert_fusion.1 = bf16[1024,768]{1,0:T(8,128)(2,1)} fusion(bf16[2048,1024]{1,0:T(8,128)(2,1)S(1)} %copy-done.24, bf16[2048,768]{1,0:T(8,128)(2,1)S(1)} %pad_maximum_fusion), kind=kOutput, calls=%fused_computation.37 | convolution fusion | flops 3222011904 | bytes 8912896 | tf_op jit(solution)/shard_map/dot_general | solution.py:555
  351.6 3.5 add_convert_fusion
  355.1 56.6 %table_grads.1 = (f32[256,256]{1,0:T(8,128)}, f32[128,256]{1,0:T(8,128)}) custom-call(s32[1,4]{1,0:T(1,128)} %len_ref.7, bf16[4,2048,2048]{2,1,0:T(8,128)(2,1)} %get-tuple-element.149.ds_ref, s16[2048,2048]{1,0:T(8,128)(2,1)} %get-tuple-element.150.code_ref), custom_call_target="tpu_custom_call" | custom-call | flops 8589934592 | bytes 157286400 | tf_op jit(solution)/shard_map/table_grads/pallas_call | solution.py:406
  418.4 2.1 collective-permute-start.27
  423.5 7.2 %fusion.14 = (f32[512]{0:T(512)S(1)}, f32[512,1024]{1,0:T(8,128)S(1)}) fusion(bf16[512,1024]{1,0:T(8,128)(2,1)S(1)} %copy-done.2, f32[1024]{0:T(1024)S(1)} %convert_element_type.123, bf16[1024,3072]{1,0:T(8,128)(2,1)} %all-gather.8.cloned.1.call-done, bf16[512,768]{1,0:T(8,128)(2,1)} %collective-permute-done.22, ...), kind=kOutput, calls=%fused_computation.21 | convolution fusion | flops 3235905024 | bytes 12589056 | tf_op jit(solution)/shard_map/dot_general | solution.py:561
  430.8 13.3 %collective-permute-start.31 = (f32[2,12,4]{1,0,2:T(2,128)S(1)}, f32[2,12,4]{1,0,2:T(2,128)S(1)}, u32[]{:S(2)}, u32[]{:S(2)}) collective-permute-start(f32[2,12,4]{1,0,2:T(2,128)S(1)} %constant_dynamic-slice_fusion.3), channel_id=1, source_target_pairs={{0,8},{4,12},{8,0},{12,4},{16,24},{20,28},{24,16},{28,20},{1,9},{5... | collective-permute-start | bytes 1160 | tf_op jit(solution)/shard_map/ppermute | solution.py:742
  445.8 1.9 fusion.13
  455.0 18.6 %reduce-scatter.5.cloned.1.call-done = bf16[128,768]{1,0:T(8,128)(2,1)} async-done(((bf16[1024,768]{1,0:T(8,128)(2,1)}), bf16[128,768]{1,0:T(8,128)(2,1)}) %reduce-scatter.5.cloned.1.call-update) | async-done | bytes 196624 | tf_op jit(solution)/shard_map/reduce_scatter | solution.py:728
  476.3 2.4 collective-permute-start.25
  (229 shorter events, 79.0 us)
Async XLA Ops:
  7.2 89.1 %all-gather.4.cloned.1.call-start = ((), (), s32[]{:S(2)}) async-start(), calls=%async_computation.2 | async-start | bytes 5242880 | tf_op jit(solution)/shard_map/all_gather | solution.py:623
  12.6 197.3 %all-gather.6.cloned.1.call-start = ((), (), s32[]{:S(2)}) async-start(), calls=%async_computation.3 | async-start | bytes 7667712 | tf_op jit(solution)/shard_map/all_gather | solution.py:658
  96.3 49.8 %collective-permute-start.4 = (bf16[512,1024]{1,0:T(8,128)(2,1)S(1)}, bf16[512,1024]{1,0:T(8,128)(2,1)S(1)}, u32[]{:S(2)}, u32[]{:S(2)}) collective-permute-start(bf16[512,1024]{1,0:T(8,128)(2,1)S(1)} %copy-done.9), channel_id=1, source_target_pairs={{0,1},{1,0},{2,3},{3,2},{4,5},{5,4},{6,7},{7,6},{8,9},{9,8},{10,11... | collective-permute-start | bytes 3145736 | tf_op jit(solution)/shard_map/ppermute | solution.py:582
  97.2 48.8 %collective-permute-start = (bf16[128,256]{1,0:T(8,128)(2,1)S(1)}, bf16[128,256]{1,0:T(8,128)(2,1)S(1)}, u32[]{:S(2)}, u32[]{:S(2)}) collective-permute-start(bf16[128,256]{1,0:T(8,128)(2,1)S(1)} %bitcast.59), channel_id=1, source_target_pairs={{0,1},{1,2},{2,3},{3,0},{4,5},{5,6},{6,7},{7,4},{8,9},{9,10},{10,1... | collective-permute-start | bytes 196616 | tf_op jit(solution)/shard_map/ppermute | solution.py:578
  99.3 46.7 %collective-permute-start.1 = (bf16[128,256]{1,0:T(8,128)(2,1)S(1)}, bf16[128,256]{1,0:T(8,128)(2,1)S(1)}, u32[]{:S(2)}, u32[]{:S(2)}) collective-permute-start(bf16[128,256]{1,0:T(8,128)(2,1)S(1)} %bitcast.60), channel_id=1, source_target_pairs={{0,2},{1,3},{2,0},{3,1},{4,6},{5,7},{6,4},{7,5},{8,10},{9,11},{10,... | collective-permute-start | bytes 196616 | tf_op jit(solution)/shard_map/ppermute | solution.py:578
  100.2 45.8 %collective-permute-start.2 = (bf16[128,256]{1,0:T(8,128)(2,1)S(1)}, bf16[128,256]{1,0:T(8,128)(2,1)S(1)}, u32[]{:S(2)}, u32[]{:S(2)}) collective-permute-start(bf16[128,256]{1,0:T(8,128)(2,1)S(1)} %bitcast.61), channel_id=1, source_target_pairs={{0,3},{1,0},{2,1},{3,2},{4,7},{5,4},{6,5},{7,6},{8,11},{9,8},{10,9... | collective-permute-start | bytes 196616 | tf_op jit(solution)/shard_map/ppermute | solution.py:578
  101.7 44.3 %collective-permute-start.3 = (bf16[128,2304]{1,0:T(8,128)(2,1)S(1)}, bf16[128,2304]{1,0:T(8,128)(2,1)S(1)}, u32[]{:S(2)}, u32[]{:S(2)}) collective-permute-start(bf16[128,2304]{1,0:T(8,128)(2,1)S(1)} %fusion.33), channel_id=1, source_target_pairs={{0,2},{1,3},{2,0},{3,1},{4,6},{5,7},{6,4},{7,5},{8,10},{9,11},{10,... | collective-permute-start | bytes 1769480 | tf_op jit(solution)/shard_map/ppermute | solution.py:578
  148.0 148.3 %all-gather.8.cloned.1.call-start = ((), (), s32[]{:S(2)}) async-start(), calls=%async_computation.4 | async-start | bytes 7077888 | tf_op jit(solution)/shard_map/all_gather | solution.py:662
  149.7 45.9 %collective-permute-start.5 = (bf16[128,768]{1,0:T(8,128)(2,1)S(1)}, bf16[128,768]{1,0:T(8,128)(2,1)S(1)}, u32[]{:S(2)}, u32[]{:S(2)}) collective-permute-start(bf16[128,768]{1,0:T(8,128)(2,1)S(1)} %constant_dynamic-slice_fusion.21), channel_id=1, source_target_pairs={{0,1},{1,2},{2,3},{3,0},{4,5},{5,6},{6,7},{7,4},{8,9},{9,10},{10,1... | collective-permute-start | bytes 589832 | tf_op jit(solution)/shard_map/ppermute | solution.py:578
  150.2 45.4 %collective-permute-start.6 = (bf16[128,768]{1,0:T(8,128)(2,1)S(1)}, bf16[128,768]{1,0:T(8,128)(2,1)S(1)}, u32[]{:S(2)}, u32[]{:S(2)}) collective-permute-start(bf16[128,768]{1,0:T(8,128)(2,1)S(1)} %constant_dynamic-slice_fusion.21), channel_id=1, source_target_pairs={{0,2},{1,3},{2,0},{3,1},{4,6},{5,7},{6,4},{7,5},{8,10},{9,11},{10,... | collective-permute-start | bytes 589832 | tf_op jit(solution)/shard_map/ppermute | solution.py:578
  151.8 43.9 %collective-permute-start.7 = (bf16[128,768]{1,0:T(8,128)(2,1)S(1)}, bf16[128,768]{1,0:T(8,128)(2,1)S(1)}, u32[]{:S(2)}, u32[]{:S(2)}) collective-permute-start(bf16[128,768]{1,0:T(8,128)(2,1)S(1)} %constant_dynamic-slice_fusion.21), channel_id=1, source_target_pairs={{0,3},{1,0},{2,1},{3,2},{4,7},{5,4},{6,5},{7,6},{8,11},{9,8},{10,9... | collective-permute-start | bytes 589832 | tf_op jit(solution)/shard_map/ppermute | solution.py:578
  153.7 41.9 %collective-permute-start.8 = (bf16[512,128]{1,0:T(8,128)(2,1)S(1)}, bf16[512,128]{1,0:T(8,128)(2,1)S(1)}, u32[]{:S(2)}, u32[]{:S(2)}) collective-permute-start(bf16[512,128]{1,0:T(8,128)(2,1)S(1)} %get-tuple-element.212), channel_id=1, source_target_pairs={{0,1},{1,2},{2,3},{3,0},{4,5},{5,6},{6,7},{7,4},{8,9},{9,10},{10,1... | collective-permute-start | bytes 393224 | tf_op jit(solution)/shard_map/ppermute | solution.py:578
  154.8 40.9 %collective-permute-start.9 = (bf16[512,128]{1,0:T(8,128)(2,1)S(1)}, bf16[512,128]{1,0:T(8,128)(2,1)S(1)}, u32[]{:S(2)}, u32[]{:S(2)}) collective-permute-start(bf16[512,128]{1,0:T(8,128)(2,1)S(1)} %get-tuple-element.211), channel_id=1, source_target_pairs={{0,2},{1,3},{2,0},{3,1},{4,6},{5,7},{6,4},{7,5},{8,10},{9,11},{10,... | collective-permute-start | bytes 393224 | tf_op jit(solution)/shard_map/ppermute | solution.py:578
  196.7 215.0 %reduce-scatter.3.cloned.1.call-start = ((), (), s32[]{:S(2)}) async-start(), calls=%async_computation.5 | async-start | bytes 12976128 | tf_op jit(solution)/shard_map/reduce_scatter | solution.py:713
  198.1 8.2 %collective-permute-start.11 = (bf16[512,128]{1,0:T(8,128)(2,1)S(1)}, bf16[512,128]{1,0:T(8,128)(2,1)S(1)}, u32[]{:S(2)}, u32[]{:S(2)}) collective-permute-start(bf16[512,128]{1,0:T(8,128)(2,1)S(1)} %get-tuple-element.208), channel_id=1, source_target_pairs={{0,1},{1,2},{2,3},{3,0},{4,5},{5,6},{6,7},{7,4},{8,9},{9,10},{10,1... | collective-permute-start | bytes 393224 | tf_op jit(solution)/shard_map/ppermute | solution.py:578
  199.2 8.6 %collective-permute-start.12 = (bf16[512,128]{1,0:T(8,128)(2,1)S(1)}, bf16[512,128]{1,0:T(8,128)(2,1)S(1)}, u32[]{:S(2)}, u32[]{:S(2)}) collective-permute-start(bf16[512,128]{1,0:T(8,128)(2,1)S(1)} %get-tuple-element.207), channel_id=1, source_target_pairs={{0,2},{1,3},{2,0},{3,1},{4,6},{5,7},{6,4},{7,5},{8,10},{9,11},{10,... | collective-permute-start | bytes 393224 | tf_op jit(solution)/shard_map/ppermute | solution.py:578
  213.5 17.4 %collective-permute-start.14 = (bf16[512,1024]{1,0:T(8,128)(2,1)S(1)}, bf16[512,1024]{1,0:T(8,128)(2,1)S(1)}, u32[]{:S(2)}, u32[]{:S(2)}) collective-permute-start(bf16[512,1024]{1,0:T(8,128)(2,1)S(1)} %multiply_convert_fusion.x_ref.refs_0_), channel_id=1, source_target_pairs={{0,1},{1,0},{2,3},{3,2},{4,5},{5,4},{6,7},{7,6},{8,9},{9,8},{10,11... | collective-permute-start | bytes 3145736 | tf_op jit(solution)/shard_map/ppermute | solution.py:582
  249.1 17.8 %collective-permute-start.15 = (bf16[512,1024]{1,0:T(8,128)(2,1)S(1)}, bf16[512,1024]{1,0:T(8,128)(2,1)S(1)}, u32[]{:S(2)}, u32[]{:S(2)}) collective-permute-start(bf16[512,1024]{1,0:T(8,128)(2,1)S(1)} %convert_element_type.132), channel_id=1, source_target_pairs={{0,1},{1,0},{2,3},{3,2},{4,5},{5,4},{6,7},{7,6},{8,9},{9,8},{10,11... | collective-permute-start | bytes 3145736 | tf_op jit(solution)/shard_map/ppermute | solution.py:582
  274.6 15.6 %collective-permute-start.16 = (bf16[512,256]{1,0:T(8,128)(2,1)}, bf16[512,256]{1,0:T(8,128)(2,1)}, u32[]{:S(2)}, u32[]{:S(2)}) collective-permute-start(bf16[512,256]{1,0:T(8,128)(2,1)} %get-tuple-element.204), channel_id=1, source_target_pairs={{0,3},{1,0},{2,1},{3,2},{4,7},{5,4},{6,5},{7,6},{8,11},{9,8},{10,9... | collective-permute-start | bytes 786440 | tf_op jit(solution)/shard_map/ppermute | solution.py:578
  277.7 14.1 %collective-permute-start.17 = (bf16[512,256]{1,0:T(8,128)(2,1)}, bf16[512,256]{1,0:T(8,128)(2,1)}, u32[]{:S(2)}, u32[]{:S(2)}) collective-permute-start(bf16[512,256]{1,0:T(8,128)(2,1)} %get-tuple-element.203), channel_id=1, source_target_pairs={{0,2},{1,3},{2,0},{3,1},{4,6},{5,7},{6,4},{7,5},{8,10},{9,11},{10,... | collective-permute-start | bytes 786440 | tf_op jit(solution)/shard_map/ppermute | solution.py:578
  277.7 16.9 %collective-permute-start.18 = (bf16[512,256]{1,0:T(8,128)(2,1)}, bf16[512,256]{1,0:T(8,128)(2,1)}, u32[]{:S(2)}, u32[]{:S(2)}) collective-permute-start(bf16[512,256]{1,0:T(8,128)(2,1)} %get-tuple-element.202), channel_id=1, source_target_pairs={{0,1},{1,2},{2,3},{3,0},{4,5},{5,6},{6,7},{7,4},{8,9},{9,10},{10,1... | collective-permute-start | bytes 786440 | tf_op jit(solution)/shard_map/ppermute | solution.py:578
  296.3 177.2 %reduce-scatter.5.cloned.1.call-start = ((), (), s32[]{:S(2)}) async-start(), calls=%async_computation.6 | async-start | bytes 1769472 | tf_op jit(solution)/shard_map/reduce_scatter | solution.py:728
  296.5 44.3 %collective-permute-start.19 = (bf16[512,1024]{1,0:T(8,128)(2,1)}, bf16[512,1024]{1,0:T(8,128)(2,1)}, u32[]{:S(2)}, u32[]{:S(2)}) collective-permute-start(bf16[512,1024]{1,0:T(8,128)(2,1)} %add_convert_fusion.1), channel_id=1, source_target_pairs={{0,1},{1,0},{2,3},{3,2},{4,5},{5,4},{6,7},{7,6},{8,9},{9,8},{10,11... | collective-permute-start | bytes 3145736 | tf_op jit(solution)/shard_map/ppermute | solution.py:582
  342.6 69.1 %collective-permute-start.20 = (bf16[512,768]{1,0:T(8,128)(2,1)}, bf16[512,768]{1,0:T(8,128)(2,1)}, u32[]{:S(2)}, u32[]{:S(2)}) collective-permute-start(bf16[512,768]{1,0:T(8,128)(2,1)} %get-tuple-element.197), channel_id=1, source_target_pairs={{0,1},{1,2},{2,3},{3,0},{4,5},{5,6},{6,7},{7,4},{8,9},{9,10},{10,1... | collective-permute-start | bytes 2359304 | tf_op jit(solution)/shard_map/ppermute | solution.py:578
  343.6 68.1 %collective-permute-start.21 = (bf16[512,768]{1,0:T(8,128)(2,1)}, bf16[512,768]{1,0:T(8,128)(2,1)}, u32[]{:S(2)}, u32[]{:S(2)}) collective-permute-start(bf16[512,768]{1,0:T(8,128)(2,1)} %get-tuple-element.196), channel_id=1, source_target_pairs={{0,2},{1,3},{2,0},{3,1},{4,6},{5,7},{6,4},{7,5},{8,10},{9,11},{10,... | collective-permute-start | bytes 2359304 | tf_op jit(solution)/shard_map/ppermute | solution.py:578
  345.1 66.6 %collective-permute-start.22 = (bf16[512,768]{1,0:T(8,128)(2,1)}, bf16[512,768]{1,0:T(8,128)(2,1)}, u32[]{:S(2)}, u32[]{:S(2)}) collective-permute-start(bf16[512,768]{1,0:T(8,128)(2,1)} %get-tuple-element.195), channel_id=1, source_target_pairs={{0,3},{1,0},{2,1},{3,2},{4,7},{5,4},{6,5},{7,6},{8,11},{9,8},{10,9... | collective-permute-start | bytes 2359304 | tf_op jit(solution)/shard_map/ppermute | solution.py:578
  418.4 12.3 %collective-permute-start.30 = (f32[4,12,4]{1,0,2:T(4,128)S(1)}, f32[4,12,4]{1,0,2:T(4,128)S(1)}, u32[]{:S(2)}, u32[]{:S(2)}) collective-permute-start(f32[4,12,4]{1,0,2:T(4,128)S(1)} %fusion.35), channel_id=1, source_target_pairs={{0,16},{4,20},{8,24},{12,28},{16,0},{20,4},{24,8},{28,12},{1,17},{... | collective-permute-start | bytes 2312 | tf_op jit(solution)/shard_map/ppermute | solution.py:742
  418.4 30.6 %collective-permute-start.27 = (bf16[128,256]{1,0:T(8,128)(2,1)S(1)}, bf16[128,256]{1,0:T(8,128)(2,1)S(1)}, u32[]{:S(2)}, u32[]{:S(2)}) collective-permute-start(bf16[128,256]{1,0:T(8,128)(2,1)S(1)} %get-tuple-element.199), channel_id=1, source_target_pairs={{0,3},{1,0},{2,1},{3,2},{4,7},{5,4},{6,5},{7,6},{8,11},{9,8},{10,9... | collective-permute-start | bytes 196616 | tf_op jit(solution)/shard_map/ppermute | solution.py:578
  420.5 28.5 %collective-permute-start.28 = (bf16[128,256]{1,0:T(8,128)(2,1)S(1)}, bf16[128,256]{1,0:T(8,128)(2,1)S(1)}, u32[]{:S(2)}, u32[]{:S(2)}) collective-permute-start(bf16[128,256]{1,0:T(8,128)(2,1)S(1)} %get-tuple-element.201), channel_id=1, source_target_pairs={{0,2},{1,3},{2,0},{3,1},{4,6},{5,7},{6,4},{7,5},{8,10},{9,11},{10,... | collective-permute-start | bytes 196616 | tf_op jit(solution)/shard_map/ppermute | solution.py:578
  420.6 28.5 %collective-permute-start.29 = (bf16[128,256]{1,0:T(8,128)(2,1)S(1)}, bf16[128,256]{1,0:T(8,128)(2,1)S(1)}, u32[]{:S(2)}, u32[]{:S(2)}) collective-permute-start(bf16[128,256]{1,0:T(8,128)(2,1)S(1)} %get-tuple-element.200), channel_id=1, source_target_pairs={{0,1},{1,2},{2,3},{3,0},{4,5},{5,6},{6,7},{7,4},{8,9},{9,10},{10,1... | collective-permute-start | bytes 196616 | tf_op jit(solution)/shard_map/ppermute | solution.py:578
  422.3 28.4 %collective-permute-start.23 = (bf16[128,2304]{1,0:T(8,128)(2,1)}, bf16[128,2304]{1,0:T(8,128)(2,1)S(1)}, u32[]{:S(2)}, u32[]{:S(2)}) collective-permute-start(bf16[128,2304]{1,0:T(8,128)(2,1)} %slice.107), channel_id=1, source_target_pairs={{0,2},{1,3},{2,0},{3,1},{4,6},{5,7},{6,4},{7,5},{8,10},{9,11},{10,... | collective-permute-start | bytes 1769480 | tf_op jit(solution)/shard_map/ppermute | solution.py:578
  430.8 14.9 %collective-permute-start.31 = (f32[2,12,4]{1,0,2:T(2,128)S(1)}, f32[2,12,4]{1,0,2:T(2,128)S(1)}, u32[]{:S(2)}, u32[]{:S(2)}) collective-permute-start(f32[2,12,4]{1,0,2:T(2,128)S(1)} %constant_dynamic-slice_fusion.3), channel_id=1, source_target_pairs={{0,8},{4,12},{8,0},{12,4},{16,24},{20,28},{24,16},{28,20},{1,9},{5... | collective-permute-start | bytes 1160 | tf_op jit(solution)/shard_map/ppermute | solution.py:742
  (38 other events, 318.8 us)
Sparse Core Ops, SparseCore 0:
  12.8 83.4 all-gather.3
  148.1 45.9 all-gather.5
  196.8 44.7 all-gather.7
  296.4 97.9 reduce-scatter.2
  423.6 49.8 reduce-scatter.4

commit v5 on v4

--- a/solution.py
+++ b/solution.py
@@ -70,32 +70,91 @@
     return jnp.max(dot(squares, same)) * f32(1.02)
 
 
-def forward_kernel(len_ref, q_ref, k_ref, v_ref, rel_ref, lay_ref, tab_ref, kmask_ref,
-                   att_ref, rinv_ref, e_ref, *rest, width, group, pair):
-    code_ref = rest[0] if len(rest) == 7 else None
-    s_scr, m_scr, acc_scr, vext, colcode, knorm = rest[-6:]
+HIDDEN_PAIR = -(1 << 31)
+
+
+def pair_bias_kernel(len_ref, rel_ref, lay_ref, tab_ref, kmask_ref, word_ref, code_ref, colcode, *, width, group):
     tq, count = rel_ref.shape
-    heads, pairs = 2, 1
+    pairs = word_ref.shape[0]
     i = pl.program_id(0)
     t0 = i * tq
     ends, base, steps = key_window(len_ref, t0, t0 + tq - 1, count, width)
 
     @pl.when(i == 0)
     def _():
-        fill_values(vext, v_ref, heads)
         pos = lax.broadcasted_iota(jnp.int32, (8, count), 1)
         page = jnp.zeros((8, count), jnp.int32)
         for e in ends:
             page = page + (pos >= e).astype(jnp.int32)
         colcode[...] = jnp.where(kmask_ref[...] == 1, page, -1)
-        for p in range(pairs):
-            knorm[p] = half_norms(k_ref[:, p * 128:(p + 1) * 128])
 
     rowpos = lax.broadcasted_iota(jnp.int32, (tq, 128), 0) + t0
     rowpage = jnp.zeros((tq, 128), jnp.int32)
     for e in ends:
         rowpage = rowpage + (rowpos >= e).astype(jnp.int32)
     lanes = lax.broadcasted_iota(jnp.int32, (tq, 128), 1)
+    tabs = [jnp.broadcast_to(tab_ref[n:n + 1, :], (tq, 128)) for n in range(2 * pairs)]
+
+    def chunk(c0, size):
+        for half in range(size // 128):
+            cc = pl.multiple_of(c0 + half * 128, 128)
+            here = pl.ds(cc, 128)
+            rel = rel_ref[:, here]
+            lay = lay_ref[:, here]
+            code_ref[:, here] = (rel + lay * 32).astype(jnp.int16)
+            col = jnp.broadcast_to(colcode[0:1, here], (tq, 128))
+            seen = (rowpage == col) | (rowpos == lanes + cc)
+            for p in range(pairs):
+                word = (jnp.take_along_axis(tabs[2 * p], rel, axis=1, mode="promise_in_bounds")
+                        + jnp.take_along_axis(tabs[2 * p + 1], lay, axis=1, mode="promise_in_bounds"))
+                word_ref[p, :, here] = jnp.where(seen, word, HIDDEN_PAIR)
+
+    for_chunks(base, steps, width, group, chunk)
+
+
+def pair_bias(page_lengths, rel, lay, tab, kmask, tq=256, width=256, group=2):
+    count = rel.shape[0]
+    pairs = tab.shape[0] // 2
+    tile = lambda i: (i, 0)
+    return pl.pallas_call(
+        functools.partial(pair_bias_kernel, width=width, group=group),
+        grid=(count // tq,),
+        in_specs=[
+            pl.BlockSpec(memory_space=pltpu.SMEM),
+            pl.BlockSpec((tq, count), tile),
+            pl.BlockSpec((tq, count), tile),
+            pl.BlockSpec(tab.shape, lambda i: (0, 0)),
+            pl.BlockSpec((1, count), lambda i: (0, 0)),
+        ],
+        out_specs=[
+            pl.BlockSpec((pairs, tq, count), lambda i: (0, i, 0)),
+            pl.BlockSpec((tq, count), tile),
+        ],
+        out_shape=[
+            jax.ShapeDtypeStruct((pairs, count, count), jnp.int32),
+            jax.ShapeDtypeStruct((count, count), jnp.int16),
+        ],
+        scratch_shapes=[pltpu.VMEM((8, count), jnp.int32)],
+        compiler_params=pltpu.CompilerParams(vmem_limit_bytes=56 << 20),
+        cost_estimate=pl.CostEstimate(flops=count * count * 1024, bytes_accessed=120 << 20, transcendentals=0),
+        name="pair_bias",
+    )(page_lengths, rel, lay, tab, kmask.reshape(1, count))
+
+
+def forward_kernel(len_ref, q_ref, k_ref, v_ref, word_ref, att_ref, rinv_ref, e_ref,
+                   s_scr, m_scr, acc_scr, vext, knorm, *, width, group):
+    tq, count = word_ref.shape[1:]
+    heads, pairs = 2, 1
+    i = pl.program_id(0)
+    t0 = i * tq
+    ends, base, steps = key_window(len_ref, t0, t0 + tq - 1, count, width)
+
+    @pl.when(i == 0)
+    def _():
+        fill_values(vext, v_ref, heads)
+        for p in range(pairs):
+            knorm[p] = half_norms(k_ref[:, p * 128:(p + 1) * 128])
+
     scaled = []
     largest = f32(0.0)
     for h in range(heads):
@@ -103,28 +162,17 @@
         scaled.append(jnp.where(own_half(qp.shape, h), qp * bf16(BIAS_SCALE), jnp.zeros_like(qp)))
         if h % 2 == 0:
             largest = jnp.maximum(largest, half_norms(qp) * knorm[h // 2])
-    tabs = [[jnp.broadcast_to(tab_ref[2 * (pair + p) + r:2 * (pair + p) + r + 1, :], (tq, 128)) for r in range(2)]
-            for p in range(pairs)]
-
     def scores(c0, width, use):
         raw = [dot(scaled[h], k_ref[pl.ds(c0, width), (h // 2) * 128:(h // 2 + 1) * 128], NT)
                for h in range(heads)]
         for half in range(width // 128):
             cc = pl.multiple_of(c0 + half * 128, 128)
-            rel = rel_ref[:, pl.ds(cc, 128)]
-            lay = lay_ref[:, pl.ds(cc, 128)]
-            if code_ref is not None:
-                code_ref[:, pl.ds(cc, 128)] = (rel + lay * 32).astype(jnp.int16)
-            col = jnp.broadcast_to(colcode[0:1, pl.ds(cc, 128)], (tq, 128))
-            seen = (rowpage == col) | (rowpos == lanes + cc)
-            hide = jnp.where(seen, f32(0.0), f32(-1e30))
-            for p in range(pairs):
-                word = (jnp.take_along_axis(tabs[p][0], rel, axis=1, mode="promise_in_bounds")
-                        + jnp.take_along_axis(tabs[p][1], lay, axis=1, mode="promise_in_bounds"))
-                parts = ((word & 0xFFFF).astype(f32), (word >> 16).astype(f32))
-                for r in range(2):
-                    h = 2 * p + r
-                    use(h, half, cc, raw[h][:, half * 128:(half + 1) * 128] + parts[r] + hide)
+            word = word_ref[0, :, pl.ds(cc, 128)]
+            hidden = word == HIDDEN_PAIR
+            parts = ((word & 0xFFFF).astype(f32), (word >> 16).astype(f32))
+            for h in range(heads):
+                bias = jnp.where(hidden, f32(-1e30), parts[h])
+                use(h, half, cc, raw[h][:, half * 128:(half + 1) * 128] + bias)
 
     for h in range(heads):
         acc_scr[h] = jnp.zeros((tq, 128), f32)
@@ -181,53 +229,49 @@
         rinv_ref[:, p * 128:(p + 1) * 128] = rinv
 
 
-def attention_forward(page_lengths, proj, rel, lay, tab, kmask, pair, tq=256, width=256, group=1):
+def attention_forward(page_lengths, proj, words, pair, tq=256, width=256, group=2):
     count = proj.shape[0]
     pairs = proj.shape[1] // (3 * 128)
     tile = lambda i: (i, 0)
     return pl.pallas_call(
-        functools.partial(forward_kernel, width=width, group=group, pair=pair),
+        functools.partial(forward_kernel, width=width, group=group),
         grid=(count // tq,),
         in_specs=[
             pl.BlockSpec(memory_space=pltpu.SMEM),
             pl.BlockSpec((tq, 128), lambda i: (i, pair)),
             pl.BlockSpec((count, 128), lambda i: (0, pairs + pair)),
             pl.BlockSpec((count, 128), lambda i: (0, 2 * pairs + pair)),
-            pl.BlockSpec((tq, count), tile),
-            pl.BlockSpec((tq, count), tile),
-            pl.BlockSpec(tab.shape, lambda i: (0, 0)),
-            pl.BlockSpec((1, count), lambda i: (0, 0)),
+            pl.BlockSpec((1, tq, count), lambda i: (pair, i, 0)),
         ],
         out_specs=[
             pl.BlockSpec((tq, 128), tile),
             pl.BlockSpec((tq, 128), tile),
             pl.BlockSpec((2, tq, count), lambda i: (0, i, 0)),
-        ] + [pl.BlockSpec((tq, count), tile)] * (pair == 0),
+        ],
         out_shape=[
             jax.ShapeDtypeStruct((count, 128), bf16),
             jax.ShapeDtypeStruct((count, 128), f32),
             jax.ShapeDtypeStruct((2, count, count), bf16),
-        ] + [jax.ShapeDtypeStruct((count, count), jnp.int16)] * (pair == 0),
+        ],
         scratch_shapes=[
             pltpu.VMEM((2, tq, count), f32),
             pltpu.VMEM((2, tq, 128), f32),
             pltpu.VMEM((2, tq, 128), f32),
             pltpu.VMEM((2, count, 128), bf16),
-            pltpu.VMEM((8, count), jnp.int32),
             pltpu.SMEM((1,), f32),
         ],
         compiler_params=pltpu.CompilerParams(vmem_limit_bytes=56 << 20),
         cost_estimate=pl.CostEstimate(
             flops=count * count * 512, bytes_accessed=80 << 20, transcendentals=count * count),
         name="attention_forward",
-    )(page_lengths, proj, proj, proj, rel, lay, tab, kmask.reshape(1, count))
+    )(page_lengths, proj, proj, proj, words)
 
 
 def bias_words(rel_table, layout_table):
     def pack(table):
         whole = jnp.round(table.astype(f32) * BIAS_SCALE).astype(jnp.int32)
         low = jnp.clip(whole[:, 0::2] + 16384, 0, 32767)
-        high = jnp.clip(whole[:, 1::2], -16384, 16383)
+        high = jnp.clip(whole[:, 1::2], -16383, 16383)
         words = (high * 65536 + low).T
         return jnp.pad(words, ((0, 0), (0, 128 - words.shape[1])))
     both = jnp.stack([pack(rel_table), pack(layout_table)], axis=1)
@@ -452,73 +496,65 @@
 CUBE = 0.044715
 
 
-def feed_forward_kernel(skip, shards, x_ref, g_ref, wg_ref, wu_ref, wd_ref, far_ref, *outs):
-    units = wg_ref.shape[0]
-    step = pad_lanes(units)
-    dn_ref = outs[-1]
+def feed_forward_kernel(far, x_ref, g_ref, *refs):
+    weights, (hidden_ref, d_gate_ref, d_up_ref, dn_ref) = refs[:-4], refs[-4:]
+    units = hidden_ref.shape[1]
+    if far:
+        step = pad_lanes(units)
+        gate_weight, up_weight, down = [weights[0][:, n * step:n * step + units] for n in range(3)]
+        ahead, back = NN, NT
+    else:
+        gate_weight, up_weight, down = [w[...] for w in weights]
+        ahead, back = NT, NN
     x = x_ref[...]
-    g = g_ref[...]
-    total = None
-    for s in range(shards):
-        if s == 0:
-            wg, wu = wg_ref[...], wu_ref[...]
-            d_hidden = dot(g, wd_ref[...], NT)
-            ahead, back = NT, NN
-        else:
-            at = skip + 3 * step * (s - 1)
-            wg = far_ref[:, at:at + units]
-            wu = far_ref[:, at + step:at + step + units]
-            d_hidden = dot(g, far_ref[:, at + 2 * step:at + 2 * step + units])
-            ahead, back = NN, NT
-        gate = dot(x, wg, ahead)
-        up = dot(x, wu, ahead)
-        square = gate * gate
-        t = jnp.tanh(TANH_SLOPE * gate * (1.0 + CUBE * square))
-        half = 0.5 + 0.5 * t
-        gelu = gate * half
-        slope = half + (0.5 * TANH_SLOPE) * gate * (1.0 - t * t) * (1.0 + (3 * CUBE) * square)
-        d_gate = (d_hidden * up * slope).astype(bf16)
-        d_up = (d_hidden * gelu).astype(bf16)
-        outs[3 * s][...] = (gelu * up).astype(bf16)
-        outs[3 * s + 1][...] = d_gate
-        outs[3 * s + 2][...] = d_up
-        value = dot(d_gate, wg, back) + dot(d_up, wu, back)
-        total = value if total is None else total + value
-    dn_ref[...] = total
-
-
-def feed_forward(x, g, w_gate_t, w_up_t, w_down, far, skip, tile=256):
+    d_hidden = dot(g_ref[...], down, ahead)
+    gate = dot(x, gate_weight, ahead)
+    up = dot(x, up_weight, ahead)
+    square = gate * gate
+    t = jnp.tanh(TANH_SLOPE * gate * (1.0 + CUBE * square))
+    half = 0.5 + 0.5 * t
+    gelu = gate * half
+    slope = half + (0.5 * TANH_SLOPE) * gate * (1.0 - t * t) * (1.0 + (3 * CUBE) * square)
+    d_gate = (d_hidden * up * slope).astype(bf16)
+    d_up = (d_hidden * gelu).astype(bf16)
+    hidden_ref[...] = (gelu * up).astype(bf16)
+    d_gate_ref[...] = d_gate
+    d_up_ref[...] = d_up
+    dn_ref[...] = dot(d_gate, gate_weight, back) + dot(d_up, up_weight, back)
+
+
+def feed_forward(x, g, units, weights, shard=None, tile=256):
     tokens, features = x.shape
-    units = w_down.shape[0]
-    shards = 1 + (far.shape[1] - skip) // (3 * pad_lanes(units))
     tile = min(tile, tokens)
     rows = lambda n: pl.BlockSpec((tile, n), lambda i: (i, 0))
-    whole = lambda a: pl.BlockSpec(a.shape, lambda i: (0, 0))
+    if shard is None:
+        weight_specs = [pl.BlockSpec(w.shape, lambda i: (0, 0)) for w in weights]
+    else:
+        weight_specs = [pl.BlockSpec((features, 3 * pad_lanes(units)), lambda i: (0, shard))]
     return pl.pallas_call(
-        functools.partial(feed_forward_kernel, skip, shards),
+        functools.partial(feed_forward_kernel, shard is not None),
         grid=(tokens // tile,),
-        in_specs=[rows(features), rows(features), whole(w_gate_t), whole(w_up_t), whole(w_down), whole(far)],
-        out_specs=[rows(units)] * (3 * shards) + [rows(features)],
-        out_shape=[jax.ShapeDtypeStruct((tokens, units), bf16)] * (3 * shards)
+        in_specs=[rows(features), rows(features)] + weight_specs,
+        out_specs=[rows(units)] * 3 + [rows(features)],
+        out_shape=[jax.ShapeDtypeStruct((tokens, units), bf16)] * 3
         + [jax.ShapeDtypeStruct((tokens, features), f32)],
         compiler_params=pltpu.CompilerParams(vmem_limit_bytes=56 << 20),
         cost_estimate=pl.CostEstimate(
-            flops=10 * tokens * features * units * shards, bytes_accessed=14 << 20,
-            transcendentals=tokens * units * shards),
+            flops=10 * tokens * features * units, bytes_accessed=10 << 20, transcendentals=tokens * units),
         name="feed_forward",
-    )(x, g, w_gate_t, w_up_t, w_down, far)
+    )(x, g, *weights)
 
 
 def pad_lanes(n):
     return (n + 127) // 128 * 128
 
 
-def weight_grads_kernel(skip, n_left, n_right, *refs):
+def weight_grads_kernel(n_left, n_right, *refs):
     lefts = refs[:2 * n_left]
     rights = refs[2 * n_left:-1]
     out_ref = refs[-1]
     rows_in = (((0,), (0,)), ((), ()))
-    place = skip
+    place = 0
     for n, left in enumerate(n_right):
         a, b = rights[2 * n], rights[2 * n + 1]
         size = a.shape[1]
@@ -530,13 +566,13 @@
         place += pad_lanes(size)
 
 
-def weight_grads(lefts, rights, groups, skip, tile=256):
+def weight_grads(lefts, rights, groups, tile=256):
     features = lefts[0].shape[1]
-    columns = skip + sum(pad_lanes(r.shape[1]) for r in rights[::2])
+    columns = sum(pad_lanes(r.shape[1]) for r in rights[::2])
     column = lambda a: pl.BlockSpec((a.shape[0], tile), lambda i: (0, i))
     whole = lambda a: pl.BlockSpec(a.shape, lambda i: (0, 0))
     return pl.pallas_call(
-        functools.partial(weight_grads_kernel, skip, len(lefts) // 2, groups),
+        functools.partial(weight_grads_kernel, len(lefts) // 2, groups),
         grid=(features // tile,),
         in_specs=[column(a) for a in lefts] + [whole(a) for a in rights],
         out_specs=pl.BlockSpec((tile, columns), lambda i: (i, 0)),
@@ -630,20 +666,20 @@
     out_piece = lax.dynamic_slice_in_dim(w_out, my_wide * part, part, 1).T
     ffn_piece = jnp.concatenate(
         [jnp.pad(piece, ((0, 0), (0, padded - units))) for piece in (own_rows_gate, own_rows_up, down_piece)], axis=1)
-    normed_attn_all, out_piece, ffn_piece, late_grad = lax.optimization_barrier(
-        (normed_attn_all, out_piece, ffn_piece, out_grad))
+    out_pieces = [out_piece] + [along(out_piece, d, ring) for d in range(1, ring)]
+    words, codes = pair_bias(page_lengths, rel_bucket, layout_bucket, bias_words(rel_table, layout_table), key_mask)
+    normed_attn_all, ffn_piece, late_grad, words = lax.optimization_barrier(
+        (normed_attn_all, ffn_piece, out_grad, words))
     ffn_pieces = [along(ffn_piece, d, ring) for d in range(2, ring, 2)]
-    out_pieces = [out_piece] + [along(out_piece, d, ring) for d in range(1, ring)]
+    out_t = lax.all_gather(jnp.concatenate(out_pieces, axis=1), "wide", axis=0, tiled=True)
     other_grad = swap(late_grad, ring)
 
     projected = dot(normed_attn_all, w_project).astype(bf16)
-    words = bias_words(rel_table, layout_table)
     pairs = head_cols // 128
-    bucket_args = (rel_bucket, layout_bucket, words, key_mask)
-    *first_pair, codes = attention_forward(page_lengths, projected, *bucket_args, 0)
-    first_pair[0], out_pieces, ffn_pieces, other_grad, late_project = lax.optimization_barrier(
-        (first_pair[0], out_pieces, ffn_pieces, other_grad, own_rows_project))
-    first_weights = jnp.concatenate(out_pieces + ffn_pieces, axis=1)
+    first_pair = list(attention_forward(page_lengths, projected, words, 0))
+    first_pair[0], ffn_pieces, other_grad, late_project = lax.optimization_barrier(
+        (first_pair[0], ffn_pieces, other_grad, own_rows_project))
+    far_pieces = jnp.concatenate(ffn_pieces, axis=1)
 
     def to_owners(a):
         return [rows_of(a, me, tokens)] + [
@@ -653,10 +689,9 @@
     project_pieces = [own_rows_project] + [along(late_project, d, ring) for d in range(1, ring)]
     results = [first_pair]
     if pairs > 1:
-        late_projected, first_weights = lax.optimization_barrier((projected, first_weights))
-        results += [list(attention_forward(page_lengths, late_projected, *bucket_args, p)) for p in range(1, pairs)]
-    w_first = lax.all_gather(first_weights, "wide", axis=0, tiled=True)
-    out_t = w_first[:, : ring * head_cols]
+        late_projected, far_pieces = lax.optimization_barrier((projected, far_pieces))
+        results += [list(attention_forward(page_lengths, late_projected, words, p)) for p in range(1, pairs)]
+    far = lax.all_gather(far_pieces, "wide", axis=0, tiled=True)
     if pairs > 1:
         results[1][0], project_pieces, sent[0] = lax.optimization_barrier((results[1][0], project_pieces, sent[0]))
     w_project_all = lax.all_gather(jnp.concatenate(project_pieces, axis=1), "wide", axis=0, tiled=True)
@@ -668,20 +703,22 @@
 
     scale_ffn, normed_ffn = norm_rows(middle, gain_ffn)
     other_normed = swap(normed_ffn, ring)
-    ffn_weights = (w_gate.T, w_up.T, down_projection_weight, w_first, ring * head_cols)
-    own = feed_forward(normed_ffn, out_grad, *ffn_weights)
-    other = feed_forward(other_normed, other_grad, *ffn_weights)
-    shards = (len(own) - 1) // 3
-    other_d_normed = swap(other[-1].astype(bf16), ring)
+    near = (w_gate.T, w_up.T, down_projection_weight)
+    shards = ring // 2
+    own = [feed_forward(normed_ffn, out_grad, units, near)]
+    other = [feed_forward(other_normed, other_grad, units, near)]
+    other += [feed_forward(other_normed, other_grad, units, (far,), s) for s in range(shards - 1)]
+    other_d_normed = swap(sum(o[3] for o in other).astype(bf16), ring)
+    own += [feed_forward(normed_ffn, out_grad, units, (far,), s) for s in range(shards - 1)]
     rights, groups = [], []
     for s in range(shards):
         for n in range(1, 4):
-            rights += [own[3 * s + n % 3], other[3 * s + n % 3]]
+            rights += [own[s][n % 3], other[s][n % 3]]
             groups.append(n // 3)
-    sums = weight_grads(
-        (normed_ffn, other_normed, out_grad, other_grad), rights, tuple(groups), ring * head_cols)
+    sums = weight_grads((normed_ffn, other_normed, out_grad, other_grad), rights, tuple(groups))
     sums, other_d_normed = lax.optimization_barrier((sums, other_d_normed))
-    d_normed_ffn = own[-1] + other_d_normed.astype(f32)
+    ffn_sums = lax.psum_scatter(sums, "wide", scatter_dimension=0, tiled=True)
+    d_normed_ffn = sum(o[3] for o in own) + other_d_normed.astype(f32)
     d_middle = out_grad.astype(f32) + norm_back(d_normed_ffn, middle, scale_ffn, gain_ffn)
     d_middle_low = d_middle.astype(bf16)
     d_attended_own = dot(d_middle_low, out_t).astype(bf16)
@@ -696,21 +733,20 @@
             d_attended, along(block(d), -d, ring), ((me + d) % ring) * tokens, 0)
 
     d_middle_late, attended_late, hiddens = lax.optimization_barrier(
-        (d_middle_low, attended_own, [(own[3 * s], other[3 * s]) for s in range(shards)]))
-    sums = lax.dynamic_update_slice(sums, contract_rows(d_middle_late, attended_late).astype(bf16), (0, 0))
+        (d_middle_low, attended_own, [(own[s][0], other[s][0]) for s in range(shards)]))
+    wout_sums = contract_rows(d_middle_late, attended_late).astype(bf16)
     own_out, other_out = 0.0, 0.0
     for s, (own_hidden, other_hidden) in enumerate(hiddens):
         if s == 0:
             down, dims = down_projection_weight, NN
         else:
-            at = ring * head_cols + 3 * padded * (s - 1) + 2 * padded
-            down, dims = w_first[:, at : at + units], NT
+            at = 3 * padded * (s - 1) + 2 * padded
+            down, dims = far[:, at : at + units], NT
         own_out = own_out + dot(own_hidden, down, dims)
         other_out = other_out + dot(other_hidden, down, dims)
     other_out = other_out.astype(bf16)
-    sums, d_attended, w_project_all, other_out, own_out = lax.optimization_barrier(
-        (sums, d_attended, w_project_all, other_out, own_out))
-    ffn_sums = lax.psum_scatter(sums, "wide", scatter_dimension=0, tiled=True)
+    wout_sums, d_attended, w_project_all, other_out, own_out = lax.optimization_barrier(
+        (wout_sums, d_attended, w_project_all, other_out, own_out))
     other_out = swap(other_out, ring)
 
     d_query, d_keys, d_values, d_scores = attention_backward(
@@ -719,13 +755,14 @@
     d_project, other_out, middle_late = lax.optimization_barrier((d_project, other_out, middle))
     layer_out = (middle_late + own_out + other_out.astype(f32)).astype(bf16)
     mine = [along(rows_of(d_project, (me + d) % ring, tokens), d, ring) for d in range(1, ring)]
-    last_sums = contract_rows(normed_attn_all, d_project).astype(bf16)
-
-    last_sums, d_scores = lax.optimization_barrier((last_sums, d_scores))
+    last_sums = jnp.concatenate([contract_rows(normed_attn_all, d_project).astype(bf16), wout_sums], axis=1)
+    last_sums, ffn_sums = lax.optimization_barrier((last_sums, ffn_sums))
+    last_sums = lax.psum_scatter(last_sums, "wide", scatter_dimension=0, tiled=True)
+    sum_project = last_sums[:, : 3 * head_cols].astype(f32)
+    wout_sums = last_sums[:, 3 * head_cols :]
+
     raw_lay, raw_rel = table_grads(page_lengths, d_scores, codes)
-    raw_lay, raw_rel, mine, ffn_sums, last_sums = lax.optimization_barrier(
-        (raw_lay, raw_rel, mine, ffn_sums, last_sums))
-    sum_project = lax.psum_scatter(last_sums, "wide", scatter_dimension=0, tiled=True).astype(f32)
+    raw_lay, raw_rel, mine = lax.optimization_barrier((raw_lay, raw_rel, mine))
     d_project_own = jnp.concatenate([rows_of(d_project, me, tokens)] + mine, axis=1)
     d_normed_attn = contract_cols(d_project_own, w_project_all)
     in_grad = d_middle + norm_back(d_normed_attn, resid, scale_attn, gain_attn)
@@ -743,22 +780,20 @@
         reach //= 2
     sum_tables = tables[0]
 
-    first = ring * head_cols
-
     def stripe(shard, n):
-        at = first + padded * (3 * shard + n)
+        at = padded * (3 * shard + n)
         return ffn_sums[:, at : at + units]
 
     sum_gate, sum_up, sum_down = [stripe(0, n).astype(f32) for n in range(3)]
     for s in range(1, shards):
-        at = first + 3 * padded * s
+        at = 3 * padded * s
         block = along(ffn_sums[:, at : at + 3 * padded], -2 * s, ring).astype(f32)
         sum_gate += block[:, :units]
         sum_up += block[:, padded : padded + units]
         sum_down += block[:, 2 * padded : 2 * padded + units]
-    sum_wout = ffn_sums[:, :head_cols].astype(f32)
+    sum_wout = wout_sums[:, :head_cols].astype(f32)
     for d in range(1, ring):
-        sum_wout += along(ffn_sums[:, d * head_cols : (d + 1) * head_cols], -d, ring).astype(f32)
+        sum_wout += along(wout_sums[:, d * head_cols : (d + 1) * head_cols], -d, ring).astype(f32)
 
     gain_terms = jnp.stack(
         [

time: 493 us -> 504 us (1.022); the launches traced: 490 us -> 496 us
  starting transfers between devices: 59.8 us -> 47 us
  Pallas kernels: 214 us -> 224 us
  other arithmetic: 22.5 us -> 31.9 us
    ppermute x26, waiting for transfers between devices: 6 us -> 58.3 us  [along(): lax.ppermute(array, 'narrow', [(i, (i + shift) % ring) for i in range(rin...]
    all_gather x1, waiting for transfers between devices: 77.6 us -> 28 us  [on_device(): normed_attn_all = lax.all_gather(normed_attn, 'narrow', axis=0, tiled=True)]
    pallas_call x3 -> x6, Pallas kernels: 47.9 us -> 88.9 us  [the longest x1 36.4 us: pair_bias(): pl.pallas_call(functools.partial(pair_bias_kernel, width=width, group=gro...]
    pallas_call x2, Pallas kernels: 69 us -> 43.5 us  [attention_forward(): pl.pallas_call(functools.partial(forward_kernel, width=width, group=group...]
    reduce_scatter x1, waiting for transfers between devices: 18.6 us -> 0.01 us  [on_device(): lax.psum_scatter(last_sums, 'wide', scatter_dimension=0, tiled=True)]
    ppermute x4, waiting for transfers between devices: 0.01 us -> 16.4 us  [swap(): return lax.ppermute(array, 'narrow', [(i, i ^ 1) for i in range(ring)])]
    ppermute x3, starting transfers between devices: 13.4 us -> 0.15 us  [on_device(): lax.ppermute(give, 'wide', [(i, i ^ reach) for i in range(wide)])]
    unnamed x84 -> x89, local copies, waits for them, and re-layouts: 15.8 us -> 14.9 us
  transfers between devices with their start and end apart: 38 -> 39, of which waited for: 8 -> 16; matrix products, arithmetic and copies ran while one was open for 16% -> 18% of each run, Pallas kernels for 44% -> 45%
where the time goes in v5:
time: 504 us; the launch traced here: 496 us
  Pallas kernels  224 us (44%)
  waiting for transfers between devices  106 us (21%)
  starting transfers between devices  47 us (9%)
  local copies, waits for them, and re-layouts  36.6 us (7%)
  matrix products  34.4 us (7%)
  other arithmetic  31.9 us (6%)
  between operations  15.1 us (3%)
    ppermute x26, waiting for transfers between devices, along(): lax.ppermute(array, 'narrow', [(i, (i + shift) % ring) for i in range(rin...  58.3 us
    pallas_call x1, Pallas kernels, table_grads(): pl.pallas_call(functools.partial(table_kernel, width=width, parts=parts),...  52.2 us
    pallas_call x2, Pallas kernels, attention_forward(): pl.pallas_call(functools.partial(forward_kernel, width=width, group=group...  43.5 us
    pallas_call x1, Pallas kernels, attention_backward(): pl.pallas_call(functools.partial(backward_kernel, width=width, heads=head...  39.5 us
    ppermute x26, starting transfers between devices, along(): lax.ppermute(array, 'narrow', [(i, (i + shift) % ring) for i in range(rin...  39.3 us
    pallas_call x1, Pallas kernels, pair_bias(): pl.pallas_call(functools.partial(pair_bias_kernel, width=width, group=gro...  36.4 us
    pallas_call x4, Pallas kernels, feed_forward(): pl.pallas_call(functools.partial(feed_forward_kernel, shard is not None),...  36.2 us
    all_gather x1, waiting for transfers between devices, on_device(): normed_attn_all = lax.all_gather(normed_attn, 'narrow', axis=0, tiled=True)  28 us
  transfers between devices with their start and end apart: 39, of which 16 were waited for; matrix products, arithmetic and copies ran while one was open for 18% of the time, Pallas kernels for 45%

profile of v5, /device:TPU:0, one launch (start us, length us, event | category | flops | bytes accessed | tf_op | source)
XLA Modules:
  0.0 495.6 jit_solution(5265335297208936375)
XLA Ops:
  12.2 5.1 %collective-permute-start.13 = (bf16[128,256]{0,1:T(8,128)(2,1)S(1)}, bf16[128,256]{0,1:T(8,128)(2,1)S(1)}, u32[]{:S(2)}, u32[]{:S(2)}) collective-permute-start(bf16[128,256]{0,1:T(8,128)(2,1)S(1)} %dynamic-slice_bitcast_fusion), channel_id=1, source_target_pairs={{0,3},{1,0},{2,1},{3,2},{4,7},{5,4},{6,5},{7,6},{8,11},{9,8},{10,9... | collective-permute-start | bytes 196616 | tf_op jit(solution)/shard_map/ppermute | solution.py:614
  19.8 4.0 collective-permute-done.12
  31.3 36.4 %pair_bias.1 = (s32[2,2048,2048]{2,1,0:T(8,128)}, s16[2048,2048]{1,0:T(8,128)(2,1)}) custom-call(s32[1,4]{1,0:T(1,128)} %len_ref.9, s32[2048,2048]{1,0:T(8,128)} %rel_ref.1, s32[2048,2048]{1,0:T(8,128)} %lay_ref.1, s32[4,128]{1,0:T(4,128)} %bitcast.71, s32[1,2048]{1,0:T(1,128)} %bitcast.70), custom_call_target="tpu_custom_call" | custom-call | flops 4294967296 | bytes 125829120 | tf_op jit(solution)/shard_map/pair_bias/pallas_call | solution.py:119
  67.7 28.0 %all-gather.5.cloned.1.call-done = bf16[2048,1024]{1,0:T(8,128)(2,1)} async-done(((bf16[512,1024]{1,0:T(8,128)(2,1)}), bf16[2048,1024]{1,0:T(8,128)(2,1)}) %all-gather.5.cloned.1.call-update) | async-done | bytes 4194320 | tf_op jit(solution)/shard_map/all_gather | solution.py:659
  97.8 7.7 %convolution_convert_fusion.q_ref.k_ref.v_ref = bf16[2048,768]{1,0:T(8,128)(2,1)} fusion(bf16[2048,1024]{1,0:T(8,128)(2,1)} %all-gather.5.cloned.1.call-done, bf16[1024,768]{1,0:T(8,128)(2,1)} %constant_dynamic-update-slice_fusion), kind=kOutput, calls=%fused_computation.6 | convolution fusion | flops 3222798336 | bytes 8912896 | tf_op jit(solution)/shard_map/dot_general | solution.py:19
  105.5 21.8 %attention_forward.2 = (bf16[2048,128]{1,0:T(8,128)(2,1)}, f32[2048,128]{1,0:T(8,128)}, bf16[2,2048,2048]{2,1,0:T(8,128)(2,1)}) custom-call(s32[1,4]{1,0:T(1,128)} %len_ref.9, bf16[2048,768]{1,0:T(8,128)(2,1)} %convolution_convert_fusion.q_ref.k_ref.v_ref, bf16[2048,768]{1,0:T(8,128)(2,1)} %convolution_convert_fusion.q_ref.k_ref.v_ref, ...), custom_call_target="tpu_custom_call" | custom-call | flops 2147483648 | bytes 83886080 | tf_op jit(solution)/shard_map/attention_forward/pallas_call | solution.py:236
  127.3 3.8 collective-permute-done
  143.2 21.7 %attention_forward.3 = (bf16[2048,128]{1,0:T(8,128)(2,1)}, f32[2048,128]{1,0:T(8,128)}, bf16[2,2048,2048]{2,1,0:T(8,128)(2,1)}) custom-call(s32[1,4]{1,0:T(1,128)} %len_ref.9, bf16[2048,768]{1,0:T(8,128)(2,1)} %convolution_convert_fusion.q_ref.k_ref.v_ref, bf16[2048,768]{1,0:T(8,128)(2,1)} %convolution_convert_fusion.q_ref.k_ref.v_ref, ...), custom_call_target="tpu_custom_call" | custom-call | flops 2147483648 | bytes 83886080 | tf_op jit(solution)/shard_map/attention_forward/pallas_call | solution.py:236
  168.5 3.2 collective-permute-start.10
  172.4 3.6 collective-permute-done.8
  177.4 4.1 collective-permute-done.9
  183.6 3.5 multiply_reduce_fusion.2
  188.4 9.0 %feed_forward.4 = (bf16[512,704]{1,0:T(8,128)(2,1)}, bf16[512,704]{1,0:T(8,128)(2,1)}, bf16[512,704]{1,0:T(8,128)(2,1)}, f32[512,1024]{1,0:T(8,128)}) custom-call(bf16[512,1024]{1,0:T(8,128)(2,1)} %copy-done.14, bf16[512,1024]{1,0:T(8,128)(2,1)} %refs_2_.5, bf16[704,1024]{1,0:T(8,128)(2,1)} %bitcast.67, bf16[704,1024]{1,0:T(8,128)(2,1)} %bitcast.65, ...), custom_call_target="tpu_custom_call" | custom-call | flops 3690987520 | bytes 10485760 | tf_op jit(solution)/shard_map/feed_forward/pallas_call | solution.py:534
  197.3 14.2 %collective-permute-done.14.x_ref.refs_1_ = bf16[512,1024]{1,0:T(8,128)(2,1)S(1)} collective-permute-done((bf16[512,1024]{1,0:T(8,128)(2,1)S(1)}, bf16[512,1024]{1,0:T(8,128)(2,1)S(1)}, u32[]{:S(2)}, u32[]{:S(2)}) %collective-permute-start.14) | collective-permute-done | bytes 1048608 | tf_op jit(solution)/shard_map/ppermute | solution.py:618
  212.5 9.1 %feed_forward.6 = (bf16[512,704]{1,0:T(8,128)(2,1)}, bf16[512,704]{1,0:T(8,128)(2,1)}, bf16[512,704]{1,0:T(8,128)(2,1)}, f32[512,1024]{1,0:T(8,128)}) custom-call(bf16[512,1024]{1,0:T(8,128)(2,1)} %copy-done.31, bf16[512,1024]{1,0:T(8,128)(2,1)} %collective-permute-done.1.g_ref.refs_3_, bf16[704,1024]{1,0:T(8,128)(2,1)} %bitcast.68, ...), custom_call_target="tpu_custom_call" | custom-call | flops 3690987520 | bytes 10485760 | tf_op jit(solution)/shard_map/feed_forward/pallas_call | solution.py:534
  221.6 9.2 %feed_forward.7 = (bf16[512,704]{1,0:T(8,128)(2,1)}, bf16[512,704]{1,0:T(8,128)(2,1)}, bf16[512,704]{1,0:T(8,128)(2,1)}, f32[512,1024]{1,0:T(8,128)}) custom-call(bf16[512,1024]{1,0:T(8,128)(2,1)} %copy-done.31, bf16[512,1024]{1,0:T(8,128)(2,1)} %collective-permute-done.1.g_ref.refs_3_, bf16[1024,2304]{1,0:T(8,128)(2,1)} %all-gather.9.cloned.1.call-done.refs_0_), custom_call_target="tpu_custom_call" | custom-call | flops 3690987520 | bytes 10485760 | tf_op jit(solution)/shard_map/feed_forward/pallas_call | solution.py:534
  233.9 9.0 %feed_forward.5 = (bf16[512,704]{1,0:T(8,128)(2,1)}, bf16[512,704]{1,0:T(8,128)(2,1)}, bf16[512,704]{1,0:T(8,128)(2,1)}, f32[512,1024]{1,0:T(8,128)}) custom-call(bf16[512,1024]{1,0:T(8,128)(2,1)} %copy-done.14, bf16[512,1024]{1,0:T(8,128)(2,1)} %refs_2_.5, bf16[1024,2304]{1,0:T(8,128)(2,1)} %all-gather.9.cloned.1.call-done.refs_0_), custom_call_target="tpu_custom_call" | custom-call | flops 3690987520 | bytes 10485760 | tf_op jit(solution)/shard_map/feed_forward/pallas_call | solution.py:534
  242.9 16.3 %weight_grads.1 = bf16[1024,4608]{1,0:T(8,128)(2,1)} custom-call(bf16[512,1024]{1,0:T(8,128)(2,1)} %copy-done.14, bf16[512,1024]{1,0:T(8,128)(2,1)} %copy-done.31, bf16[512,1024]{1,0:T(8,128)(2,1)} %refs_2_.5, bf16[512,1024]{1,0:T(8,128)(2,1)} %collective-permute-done.1.g_ref.refs_3_, bf16[512,704]{1,0:T(8,128)(2,1)} %get-tuple-element.105.refs_4_, ...), custom_call_target="tpu_custom_call" | custom-call | flops 9663676416 | bytes 27262976 | tf_op jit(solution)/shard_map/weight_grads/pallas_call | solution.py:574
  259.6 3.2 multiply_reduce_fusion.1
  263.6 3.6 fusion.82
  283.5 3.8 convolution_convert_fusion.1
  291.3 6.8 %collective-permute-start.19 = (bf16[512,1024]{1,0:T(8,128)(2,1)}, bf16[512,1024]{1,0:T(8,128)(2,1)S(1)}, u32[]{:S(2)}, u32[]{:S(2)}) collective-permute-start(bf16[512,1024]{1,0:T(8,128)(2,1)} %add_convert_fusion.1), channel_id=1, source_target_pairs={{0,1},{1,0},{2,3},{3,2},{4,5},{5,4},{6,7},{7,6},{8,9},{9,8},{10,11... | collective-permute-start | bytes 3145736 | tf_op jit(solution)/shard_map/ppermute | solution.py:618
  298.2 39.5 %attention_backward.1 = (bf16[2048,256]{1,0:T(8,128)(2,1)}, bf16[2048,256]{1,0:T(8,128)(2,1)}, bf16[2048,256]{1,0:T(8,128)(2,1)}, bf16[4,2048,2048]{2,1,0:T(8,128)(2,1)}) custom-call(s32[1,4]{1,0:T(1,128)} %len_ref.9, bf16[2048,768]{1,0:T(8,128)(2,1)} %convolution_convert_fusion.q_ref.k_ref.v_ref, ...), custom_call_target="tpu_custom_call" | custom-call | flops 8589934592 | bytes 157286400 | tf_op jit(solution)/shard_map/attention_backward/pallas_call | solution.py:365
  341.5 3.6 convolution_convert_fusion.2
  347.3 3.3 constant_dynamic-slice_fusion.13
  354.3 52.2 %table_grads.1 = (f32[256,256]{1,0:T(8,128)}, f32[128,256]{1,0:T(8,128)}) custom-call(s32[1,4]{1,0:T(1,128)} %len_ref.9, bf16[4,2048,2048]{2,1,0:T(8,128)(2,1)} %get-tuple-element.143.ds_ref, s16[2048,2048]{1,0:T(8,128)(2,1)} %get-tuple-element.144.code_ref), custom_call_target="tpu_custom_call" | custom-call | flops 8589934592 | bytes 157286400 | tf_op jit(solution)/shard_map/table_grads/pallas_call | solution.py:450
  408.2 12.7 %collective-permute-done.21 = bf16[512,768]{1,0:T(8,128)(2,1)} collective-permute-done((bf16[512,768]{1,0:T(8,128)(2,1)S(1)}, bf16[512,768]{1,0:T(8,128)(2,1)}, u32[]{:S(2)}, u32[]{:S(2)}) %collective-permute-start.21) | collective-permute-done | bytes 786464 | tf_op jit(solution)/shard_map/ppermute | solution.py:614
  426.8 7.3 %fusion.14 = (f32[512]{0:T(512)S(1)}, f32[512,1024]{1,0:T(8,128)S(1)}) fusion(bf16[512,1024]{1,0:T(8,128)(2,1)S(1)} %copy-done.3, f32[1024]{0:T(1024)S(1)} %convert_element_type.123, bf16[1024,3072]{1,0:T(8,128)(2,1)} %all-gather.11.cloned.1.call-done, bf16[512,768]{1,0:T(8,128)(2,1)} %collective-permute-done.22, ...), kind=kOutput, calls=%fused_computation.22 | convolution fusion | flops 3235905024 | bytes 12589056 | tf_op jit(solution)/shard_map/dot_general | solution.py:597
  434.2 3.6 collective-permute-done.31
  443.3 23.8 %collective-permute-done.23 = bf16[128,2304]{1,0:T(8,128)(2,1)} collective-permute-done((bf16[128,2304]{1,0:T(8,128)(2,1)}, bf16[128,2304]{1,0:T(8,128)(2,1)}, u32[]{:S(2)}, u32[]{:S(2)}) %collective-permute-start.23) | collective-permute-done | bytes 589856 | tf_op jit(solution)/shard_map/ppermute | solution.py:614
  475.4 3.8 collective-permute-start.26
  481.0 2.9 collective-permute-start.28
  (242 shorter events, 100.5 us)
Async XLA Ops:
  7.2 88.5 %all-gather.5.cloned.1.call-start = ((), (), s32[]{:S(2)}) async-start(), calls=%async_computation.2 | async-start | bytes 5242880 | tf_op jit(solution)/shard_map/all_gather | solution.py:659
  12.0 171.6 %all-gather.7.cloned.1.call-start = ((), (), s32[]{:S(2)}) async-start(), calls=%async_computation.3 | async-start | bytes 2359296 | tf_op jit(solution)/shard_map/all_gather | solution.py:674
  12.2 7.6 %collective-permute-start.13 = (bf16[128,256]{0,1:T(8,128)(2,1)S(1)}, bf16[128,256]{0,1:T(8,128)(2,1)S(1)}, u32[]{:S(2)}, u32[]{:S(2)}) collective-permute-start(bf16[128,256]{0,1:T(8,128)(2,1)S(1)} %dynamic-slice_bitcast_fusion), channel_id=1, source_target_pairs={{0,3},{1,0},{2,1},{3,2},{4,7},{5,4},{6,5},{7,6},{8,11},{9,8},{10,9... | collective-permute-start | bytes 196616 | tf_op jit(solution)/shard_map/ppermute | solution.py:614
  24.5 197.1 %all-gather.9.cloned.1.call-start = ((), (), s32[]{:S(2)}) async-start(), calls=%async_computation.4 | async-start | bytes 5308416 | tf_op jit(solution)/shard_map/all_gather | solution.py:694
  95.7 37.7 %collective-permute-start.1 = (bf16[512,1024]{1,0:T(8,128)(2,1)S(1)}, bf16[512,1024]{1,0:T(8,128)(2,1)}, u32[]{:S(2)}, u32[]{:S(2)}) collective-permute-start(bf16[512,1024]{1,0:T(8,128)(2,1)S(1)} %copy-done.17), channel_id=1, source_target_pairs={{0,1},{1,0},{2,3},{3,2},{4,5},{5,4},{6,7},{7,6},{8,9},{9,8},{10,11... | collective-permute-start | bytes 3145736 | tf_op jit(solution)/shard_map/ppermute | solution.py:618
  96.6 34.5 %collective-permute-start = (bf16[128,2304]{1,0:T(8,128)(2,1)}, bf16[128,2304]{1,0:T(8,128)(2,1)S(1)}, u32[]{:S(2)}, u32[]{:S(2)}) collective-permute-start(bf16[128,2304]{1,0:T(8,128)(2,1)} %fusion.24), channel_id=1, source_target_pairs={{0,2},{1,3},{2,0},{3,1},{4,6},{5,7},{6,4},{7,5},{8,10},{9,11},{10,... | collective-permute-start | bytes 1769480 | tf_op jit(solution)/shard_map/ppermute | solution.py:614
  133.3 158.0 %all-gather.11.cloned.1.call-start = ((), (), s32[]{:S(2)}) async-start(), calls=%async_computation.5 | async-start | bytes 7077888 | tf_op jit(solution)/shard_map/all_gather | solution.py:697
  134.6 6.5 %collective-permute-start.7 = (bf16[512,128]{1,0:T(8,128)(2,1)S(1)}, bf16[512,128]{1,0:T(8,128)(2,1)S(1)}, u32[]{:S(2)}, u32[]{:S(2)}) collective-permute-start(bf16[512,128]{1,0:T(8,128)(2,1)S(1)} %get-tuple-element.201), channel_id=1, source_target_pairs={{0,3},{1,0},{2,1},{3,2},{4,7},{5,4},{6,5},{7,6},{8,11},{9,8},{10,9... | collective-permute-start | bytes 393224 | tf_op jit(solution)/shard_map/ppermute | solution.py:614
  135.5 29.9 %collective-permute-start.4 = (bf16[128,768]{1,0:T(8,128)(2,1)S(1)}, bf16[128,768]{1,0:T(8,128)(2,1)S(1)}, u32[]{:S(2)}, u32[]{:S(2)}) collective-permute-start(bf16[128,768]{1,0:T(8,128)(2,1)S(1)} %constant_dynamic-slice_fusion.21), channel_id=1, source_target_pairs={{0,3},{1,0},{2,1},{3,2},{4,7},{5,4},{6,5},{7,6},{8,11},{9,8},{10,9... | collective-permute-start | bytes 589832 | tf_op jit(solution)/shard_map/ppermute | solution.py:614
  138.0 27.4 %collective-permute-start.3 = (bf16[128,768]{1,0:T(8,128)(2,1)S(1)}, bf16[128,768]{1,0:T(8,128)(2,1)S(1)}, u32[]{:S(2)}, u32[]{:S(2)}) collective-permute-start(bf16[128,768]{1,0:T(8,128)(2,1)S(1)} %constant_dynamic-slice_fusion.21), channel_id=1, source_target_pairs={{0,2},{1,3},{2,0},{3,1},{4,6},{5,7},{6,4},{7,5},{8,10},{9,11},{10,... | collective-permute-start | bytes 589832 | tf_op jit(solution)/shard_map/ppermute | solution.py:614
  138.1 27.3 %collective-permute-start.2 = (bf16[128,768]{1,0:T(8,128)(2,1)S(1)}, bf16[128,768]{1,0:T(8,128)(2,1)S(1)}, u32[]{:S(2)}, u32[]{:S(2)}) collective-permute-start(bf16[128,768]{1,0:T(8,128)(2,1)S(1)} %constant_dynamic-slice_fusion.21), channel_id=1, source_target_pairs={{0,1},{1,2},{2,3},{3,0},{4,5},{5,6},{6,7},{7,4},{8,9},{9,10},{10,1... | collective-permute-start | bytes 589832 | tf_op jit(solution)/shard_map/ppermute | solution.py:614
  139.8 25.6 %collective-permute-start.6 = (bf16[512,128]{1,0:T(8,128)(2,1)S(1)}, bf16[512,128]{1,0:T(8,128)(2,1)S(1)}, u32[]{:S(2)}, u32[]{:S(2)}) collective-permute-start(bf16[512,128]{1,0:T(8,128)(2,1)S(1)} %get-tuple-element.202), channel_id=1, source_target_pairs={{0,2},{1,3},{2,0},{3,1},{4,6},{5,7},{6,4},{7,5},{8,10},{9,11},{10,... | collective-permute-start | bytes 393224 | tf_op jit(solution)/shard_map/ppermute | solution.py:614
  141.1 24.3 %collective-permute-start.5 = (bf16[512,128]{1,0:T(8,128)(2,1)S(1)}, bf16[512,128]{1,0:T(8,128)(2,1)S(1)}, u32[]{:S(2)}, u32[]{:S(2)}) collective-permute-start(bf16[512,128]{1,0:T(8,128)(2,1)S(1)} %get-tuple-element.203), channel_id=1, source_target_pairs={{0,1},{1,2},{2,3},{3,0},{4,5},{5,6},{6,7},{7,4},{8,9},{9,10},{10,1... | collective-permute-start | bytes 393224 | tf_op jit(solution)/shard_map/ppermute | solution.py:614
  166.4 180.9 %reduce-scatter.3.cloned.1.call-start = ((), (), s32[]{:S(2)}) async-start(), calls=%async_computation.6 | async-start | bytes 10616832 | tf_op jit(solution)/shard_map/reduce_scatter | solution.py:720
  167.9 8.2 %collective-permute-start.8 = (bf16[512,128]{1,0:T(8,128)(2,1)S(1)}, bf16[512,128]{1,0:T(8,128)(2,1)S(1)}, u32[]{:S(2)}, u32[]{:S(2)}) collective-permute-start(bf16[512,128]{1,0:T(8,128)(2,1)S(1)} %get-tuple-element.199), channel_id=1, source_target_pairs={{0,1},{1,2},{2,3},{3,0},{4,5},{5,6},{6,7},{7,4},{8,9},{9,10},{10,1... | collective-permute-start | bytes 393224 | tf_op jit(solution)/shard_map/ppermute | solution.py:614
  168.5 14.5 %collective-permute-start.10 = (bf16[512,128]{1,0:T(8,128)(2,1)S(1)}, bf16[512,128]{1,0:T(8,128)(2,1)S(1)}, u32[]{:S(2)}, u32[]{:S(2)}) collective-permute-start(bf16[512,128]{1,0:T(8,128)(2,1)S(1)} %get-tuple-element.197), channel_id=1, source_target_pairs={{0,3},{1,0},{2,1},{3,2},{4,7},{5,4},{6,5},{7,6},{8,11},{9,8},{10,9... | collective-permute-start | bytes 393224 | tf_op jit(solution)/shard_map/ppermute | solution.py:614
  171.7 9.8 %collective-permute-start.9 = (bf16[512,128]{1,0:T(8,128)(2,1)S(1)}, bf16[512,128]{1,0:T(8,128)(2,1)S(1)}, u32[]{:S(2)}, u32[]{:S(2)}) collective-permute-start(bf16[512,128]{1,0:T(8,128)(2,1)S(1)} %get-tuple-element.198), channel_id=1, source_target_pairs={{0,2},{1,3},{2,0},{3,1},{4,6},{5,7},{6,4},{7,5},{8,10},{9,11},{10,... | collective-permute-start | bytes 393224 | tf_op jit(solution)/shard_map/ppermute | solution.py:614
  187.4 24.1 %collective-permute-start.14 = (bf16[512,1024]{1,0:T(8,128)(2,1)S(1)}, bf16[512,1024]{1,0:T(8,128)(2,1)S(1)}, u32[]{:S(2)}, u32[]{:S(2)}) collective-permute-start(bf16[512,1024]{1,0:T(8,128)(2,1)S(1)} %multiply_convert_fusion.x_ref.refs_0_), channel_id=1, source_target_pairs={{0,1},{1,0},{2,3},{3,2},{4,5},{5,4},{6,7},{7,6},{8,9},{9,8},{10,11... | collective-permute-start | bytes 3145736 | tf_op jit(solution)/shard_map/ppermute | solution.py:618
  233.6 25.6 %collective-permute-start.15 = (bf16[512,1024]{1,0:T(8,128)(2,1)}, bf16[512,1024]{1,0:T(8,128)(2,1)}, u32[]{:S(2)}, u32[]{:S(2)}) collective-permute-start(bf16[512,1024]{1,0:T(8,128)(2,1)} %add_convert_fusion.2), channel_id=1, source_target_pairs={{0,1},{1,0},{2,3},{3,2},{4,5},{5,4},{6,7},{7,6},{8,9},{9,8},{10,11... | collective-permute-start | bytes 3145736 | tf_op jit(solution)/shard_map/ppermute | solution.py:618
  259.2 211.9 %reduce-scatter.5.cloned.1.call-start = ((), (), s32[]{:S(2)}) async-start(), calls=%async_computation.7 | async-start | bytes 4128768 | tf_op jit(solution)/shard_map/reduce_scatter | solution.py:760
  270.4 20.2 %collective-permute-start.18 = (bf16[512,256]{1,0:T(8,128)(2,1)S(1)}, bf16[512,256]{1,0:T(8,128)(2,1)S(1)}, u32[]{:S(2)}, u32[]{:S(2)}) collective-permute-start(bf16[512,256]{1,0:T(8,128)(2,1)S(1)} %get-tuple-element.193), channel_id=1, source_target_pairs={{0,1},{1,2},{2,3},{3,0},{4,5},{5,6},{6,7},{7,4},{8,9},{9,10},{10,1... | collective-permute-start | bytes 786440 | tf_op jit(solution)/shard_map/ppermute | solution.py:614
  272.2 17.7 %collective-permute-start.17 = (bf16[512,256]{1,0:T(8,128)(2,1)S(1)}, bf16[512,256]{1,0:T(8,128)(2,1)S(1)}, u32[]{:S(2)}, u32[]{:S(2)}) collective-permute-start(bf16[512,256]{1,0:T(8,128)(2,1)S(1)} %get-tuple-element.194), channel_id=1, source_target_pairs={{0,2},{1,3},{2,0},{3,1},{4,6},{5,7},{6,4},{7,5},{8,10},{9,11},{10,... | collective-permute-start | bytes 786440 | tf_op jit(solution)/shard_map/ppermute | solution.py:614
  273.9 13.4 %collective-permute-start.16 = (bf16[512,256]{1,0:T(8,128)(2,1)S(1)}, bf16[512,256]{1,0:T(8,128)(2,1)S(1)}, u32[]{:S(2)}, u32[]{:S(2)}) collective-permute-start(bf16[512,256]{1,0:T(8,128)(2,1)S(1)} %get-tuple-element.195), channel_id=1, source_target_pairs={{0,3},{1,0},{2,1},{3,2},{4,7},{5,4},{6,5},{7,6},{8,11},{9,8},{10,9... | collective-permute-start | bytes 786440 | tf_op jit(solution)/shard_map/ppermute | solution.py:614
  291.3 48.5 %collective-permute-start.19 = (bf16[512,1024]{1,0:T(8,128)(2,1)}, bf16[512,1024]{1,0:T(8,128)(2,1)S(1)}, u32[]{:S(2)}, u32[]{:S(2)}) collective-permute-start(bf16[512,1024]{1,0:T(8,128)(2,1)} %add_convert_fusion.1), channel_id=1, source_target_pairs={{0,1},{1,0},{2,3},{3,2},{4,5},{5,4},{6,7},{7,6},{8,9},{9,8},{10,11... | collective-permute-start | bytes 3145736 | tf_op jit(solution)/shard_map/ppermute | solution.py:618
  350.7 57.5 %collective-permute-start.22 = (bf16[512,768]{1,0:T(8,128)(2,1)}, bf16[512,768]{1,0:T(8,128)(2,1)}, u32[]{:S(2)}, u32[]{:S(2)}) collective-permute-start(bf16[512,768]{1,0:T(8,128)(2,1)} %get-tuple-element.189), channel_id=1, source_target_pairs={{0,3},{1,0},{2,1},{3,2},{4,7},{5,4},{6,5},{7,6},{8,11},{9,8},{10,9... | collective-permute-start | bytes 2359304 | tf_op jit(solution)/shard_map/ppermute | solution.py:614
  352.0 68.9 %collective-permute-start.21 = (bf16[512,768]{1,0:T(8,128)(2,1)S(1)}, bf16[512,768]{1,0:T(8,128)(2,1)}, u32[]{:S(2)}, u32[]{:S(2)}) collective-permute-start(bf16[512,768]{1,0:T(8,128)(2,1)S(1)} %get-tuple-element.190), channel_id=1, source_target_pairs={{0,2},{1,3},{2,0},{3,1},{4,6},{5,7},{6,4},{7,5},{8,10},{9,11},{10,... | collective-permute-start | bytes 2359304 | tf_op jit(solution)/shard_map/ppermute | solution.py:614
  352.4 68.6 %collective-permute-start.20 = (bf16[512,768]{1,0:T(8,128)(2,1)S(1)}, bf16[512,768]{1,0:T(8,128)(2,1)}, u32[]{:S(2)}, u32[]{:S(2)}) collective-permute-start(bf16[512,768]{1,0:T(8,128)(2,1)S(1)} %get-tuple-element.191), channel_id=1, source_target_pairs={{0,1},{1,2},{2,3},{3,0},{4,5},{5,6},{6,7},{7,4},{8,9},{9,10},{10,1... | collective-permute-start | bytes 2359304 | tf_op jit(solution)/shard_map/ppermute | solution.py:614
  426.7 7.3 %collective-permute-start.30 = (f32[4,12,4]{1,0,2:T(4,128)S(1)}, f32[4,12,4]{1,0,2:T(4,128)S(1)}, u32[]{:S(2)}, u32[]{:S(2)}) collective-permute-start(f32[4,12,4]{1,0,2:T(4,128)S(1)} %fusion.26), channel_id=1, source_target_pairs={{0,16},{4,20},{8,24},{12,28},{16,0},{20,4},{24,8},{28,12},{1,17},{... | collective-permute-start | bytes 2312 | tf_op jit(solution)/shard_map/ppermute | solution.py:779
  438.8 28.2 %collective-permute-start.23 = (bf16[128,2304]{1,0:T(8,128)(2,1)}, bf16[128,2304]{1,0:T(8,128)(2,1)}, u32[]{:S(2)}, u32[]{:S(2)}) collective-permute-start(bf16[128,2304]{1,0:T(8,128)(2,1)} %slice.112), channel_id=1, source_target_pairs={{0,2},{1,3},{2,0},{3,1},{4,6},{5,7},{6,4},{7,5},{8,10},{9,11},{10,... | collective-permute-start | bytes 1769480 | tf_op jit(solution)/shard_map/ppermute | solution.py:614
  472.1 12.8 %collective-permute-start.27 = (bf16[128,256]{1,0:T(8,128)(2,1)S(1)}, bf16[128,256]{1,0:T(8,128)(2,1)S(1)}, u32[]{:S(2)}, u32[]{:S(2)}) collective-permute-start(bf16[128,256]{1,0:T(8,128)(2,1)S(1)} %get-tuple-element.205), channel_id=1, source_target_pairs={{0,3},{1,0},{2,1},{3,2},{4,7},{5,4},{6,5},{7,6},{8,11},{9,8},{10,9... | collective-permute-start | bytes 196616 | tf_op jit(solution)/shard_map/ppermute | solution.py:614
  472.4 12.5 %collective-permute-start.29 = (bf16[128,256]{1,0:T(8,128)(2,1)S(1)}, bf16[128,256]{1,0:T(8,128)(2,1)S(1)}, u32[]{:S(2)}, u32[]{:S(2)}) collective-permute-start(bf16[128,256]{1,0:T(8,128)(2,1)S(1)} %get-tuple-element.206), channel_id=1, source_target_pairs={{0,1},{1,2},{2,3},{3,0},{4,5},{5,6},{6,7},{7,4},{8,9},{9,10},{10,1... | collective-permute-start | bytes 196616 | tf_op jit(solution)/shard_map/ppermute | solution.py:614
  475.4 8.5 %collective-permute-start.26 = (f32[2,32]{1,0:T(2,128)S(1)}, f32[2,32]{1,0:T(2,128)S(1)}, u32[]{:S(2)}, u32[]{:S(2)}) collective-permute-start(f32[2,32]{1,0:T(2,128)S(1)} %get-tuple-element.218), channel_id=1, source_target_pairs={{0,3},{1,0},{2,1},{3,2},{4,7},{5,4},{6,5},{7,6},{8,11},{9,8},{10,9... | collective-permute-start | bytes 776 | tf_op jit(solution)/shard_map/ppermute | solution.py:614
  (44 other events, 457.8 us)
Sparse Core Ops, SparseCore 0:
  12.2 83.4 all-gather.4
  98.1 26.7 all-gather.6
  133.5 38.4 all-gather.8
  173.7 45.5 all-gather.10
  259.4 77.6 reduce-scatter.2
  347.5 46.7 reduce-scatter.4
